TPU v7x, 32 devices: a whole 2x2x4 slice. The times are simulated.
32 devices in a mesh: dp: 8 (over z, y), ulysses: 4 (over x, core).
Axes of the slice: x: 2, y: 2, z: 4, core: 2. Of those that a mesh axis runs over, the one named last changes fastest.
Arguments:
- tokens: bfloat16 [8, 1024, 2048], P('dp', 'ulysses'), may hold values from -6 to 6
- seq_lengths: int32 [8], P('dp'), may hold values from 769 to 1024, as said below
- cotangent: bfloat16 [8, 1024, 2048], P('dp', 'ulysses'), may hold values from -6 to 6
- norm1_gain: float32 [2048], replicated, may hold values from 0.1 to 1.9
- input_weight: bfloat16 [2048, 6144], P('dp'), may hold values from -0.125 to 0.125
- query_gain: float32 [128], replicated, may hold values from 0.1 to 1.9
- key_gain: float32 [128], replicated, may hold values from 0.1 to 1.9
- output_weight: bfloat16 [2048, 2048], P('dp'), may hold values from -2 to 2
- norm2_gain: float32 [2048], replicated, may hold values from 0.1 to 1.9
- perceptron_input_weight: bfloat16 [2048, 12288], P('dp'), may hold values from -0.125 to 0.125
- down_weight: bfloat16 [6144, 2048], P('dp'), may hold values from -0.078125 to 0.078125
Outputs:
- layer_out: float32 [8, 1024, 2048], P('dp', 'ulysses')
- tokens_grad: float32 [8, 1024, 2048], P('dp', 'ulysses')
- norm1_gain_grad: float32 [2048], replicated
- w_in_grad: float32 [2048, 6144], P('dp')
- query_gain_grad: float32 [128], replicated
- key_gain_grad: float32 [128], replicated
- w_out_grad: float32 [2048, 2048], P('dp')
- norm2_gain_grad: float32 [2048], replicated
- w_mlp_in_grad: float32 [2048, 12288], P('dp')
- w_down_grad: float32 [6144, 2048], P('dp')
Inputs may be any that keep to these rules, and one draw needn't show every extreme that they name: `seq_lengths`: some slot has length 1024; every slot reaches into the last 1024 / 4 positions of its bucket.
All inputs are finite; a program needn't handle non-finite values.
Results may differ from a plain program's by a relative error of at most 0.02.
Values may be sent and summed in bfloat16 or wider, within the bound.
A program may use at most 576 MiB of HBM per device.

v0:
```python
import jax
import jax.numpy as jnp
from jax import lax
from jax.sharding import PartitionSpec as P

QUERY_HEADS = 16
KEY_VALUE_HEADS = 8
HEAD_DIMENSION = 128
FF = 6144


EPSILON = 1e-06
ROPE_BASE = 1000000.0
MASKED = -1e30


def rms_scale(values):
    return lax.rsqrt(jnp.mean(values * values, axis=-1, keepdims=True) + EPSILON)


def rope_tables(positions, head_size):
    half_size = head_size // 2
    frequency = ROPE_BASE ** (-2.0 * jnp.arange(half_size).astype(jnp.float32) / head_size)
    angles = positions.astype(jnp.float32)[:, None] * frequency[None, :]
    return (jnp.cos(angles), jnp.sin(angles))


def rotate(values, cosine, sine):
    half_size = values.shape[-1] // 2
    front = values[..., :half_size]
    behind = values[..., half_size:]
    return jnp.concatenate(
        [front * cosine - behind * sine, behind * cosine + front * sine], axis=-1
    )


def unrotate(grad_values, cosine, sine):
    half_size = grad_values.shape[-1] // 2
    front = grad_values[..., :half_size]
    behind = grad_values[..., half_size:]
    return jnp.concatenate(
        [front * cosine + behind * sine, behind * cosine - front * sine], axis=-1
    )


def norm_back(source, factor, gain_vec, upstream):
    weighted = upstream * gain_vec
    inner = jnp.mean(weighted * source, axis=-1, keepdims=True)
    source_grad = factor * weighted - source * (factor * factor * factor) * inner
    return (source_grad, upstream * source * factor)


def scores_block(query_block, keys, first_row, valid_keys, score_scale):
    raw_scores = (
        jnp.einsum("sqgrd,skgd->sgrqk", query_block, keys, preferred_element_type=jnp.float32)
        * score_scale
    )
    query_index = first_row + jnp.arange(query_block.shape[1])
    key_index = jnp.arange(keys.shape[1])
    causal = key_index[None, :] <= query_index[:, None]
    allowed = causal[None, None, None] & valid_keys[:, None, None, None, :]
    return jnp.where(allowed, raw_scores, MASKED)


def attend_forward(queries, keys, values, valid_keys, score_scale, block_rows):
    sequence_count, bucket_size, head_count, head_size = queries.shape
    group_count = keys.shape[2]
    grouped = queries.reshape(
        sequence_count, bucket_size, group_count, head_count // group_count, head_size
    )
    outputs = []
    totals = []
    for block_at in range(bucket_size // block_rows):
        first_row = block_at * block_rows
        query_block = grouped[:, first_row : first_row + block_rows]
        scores = scores_block(query_block, keys, first_row, valid_keys, score_scale)
        row_top = jnp.max(scores, axis=-1, keepdims=True)
        log_total = row_top + jnp.log(jnp.sum(jnp.exp(scores - row_top), axis=-1, keepdims=True))
        soft_weights = jnp.exp(scores - log_total).astype(jnp.bfloat16)
        block_out = jnp.einsum(
            "sgrqk,skgd->sqgrd", soft_weights, values, preferred_element_type=jnp.float32
        )
        outputs.append(block_out.reshape(sequence_count, block_rows, head_count, head_size))
        totals.append(log_total)
    return (jnp.concatenate(outputs, axis=1), totals)


def attend_backward(
    queries, keys, values, grad_attended, totals, valid_keys, score_scale, block_rows
):
    sequence_count, bucket_size, head_count, head_size = queries.shape
    group_count = keys.shape[2]
    grouped = queries.reshape(
        sequence_count, bucket_size, group_count, head_count // group_count, head_size
    )
    grouped_grad = grad_attended.reshape(
        sequence_count, bucket_size, group_count, head_count // group_count, head_size
    )
    key_grad = jnp.zeros(keys.shape, jnp.float32)
    value_grad = jnp.zeros(values.shape, jnp.float32)
    query_grads = []
    for block_at in range(bucket_size // block_rows):
        first_row = block_at * block_rows
        query_block = grouped[:, first_row : first_row + block_rows]
        grad_block = grouped_grad[:, first_row : first_row + block_rows]
        scores = scores_block(query_block, keys, first_row, valid_keys, score_scale)
        soft = jnp.exp(scores - totals[block_at])
        soft_grad = jnp.einsum(
            "sqgrd,skgd->sgrqk", grad_block, values, preferred_element_type=jnp.float32
        )
        inner = jnp.sum(soft * soft_grad, axis=-1, keepdims=True)
        score_grad = (soft * (soft_grad - inner)).astype(jnp.bfloat16)
        block_grad = (
            jnp.einsum("sgrqk,skgd->sqgrd", score_grad, keys, preferred_element_type=jnp.float32)
            * score_scale
        )
        query_grads.append(block_grad.reshape(sequence_count, block_rows, head_count, head_size))
        key_grad = (
            key_grad
            + jnp.einsum(
                "sgrqk,sqgrd->skgd", score_grad, query_block, preferred_element_type=jnp.float32
            )
            * score_scale
        )
        value_grad = value_grad + jnp.einsum(
            "sgrqk,sqgrd->skgd",
            soft.astype(jnp.bfloat16),
            grad_block,
            preferred_element_type=jnp.float32,
        )
    return (jnp.concatenate(query_grads, axis=1), key_grad, value_grad)


def shards(
    tokens,
    seq_lengths,
    cotangent,
    norm1_gain,
    input_weight,
    query_gain,
    key_gain,
    output_weight,
    norm2_gain,
    perceptron_input_weight,
    down_weight,
):
    sequence_count, device_local_rows, model_width = tokens.shape
    group_size = lax.axis_size("ulysses")
    bucket_size = device_local_rows * group_size
    query_width = QUERY_HEADS * HEAD_DIMENSION
    key_value_width = KEY_VALUE_HEADS * HEAD_DIMENSION
    head_copies = QUERY_HEADS // KEY_VALUE_HEADS
    block_rows = min(512, bucket_size)
    score_scale = HEAD_DIMENSION ** (-0.5)
    positions = lax.axis_index("ulysses") * device_local_rows + jnp.arange(device_local_rows)
    cosine, sine = rope_tables(positions, HEAD_DIMENSION)
    cosine = cosine[None, :, None, :]
    sine = sine[None, :, None, :]
    valid_keys = jnp.arange(bucket_size)[None, :] < seq_lengths[:, None]
    live_rows = (positions[None, :] < seq_lengths[:, None])[..., None]
    input_weight_full, output_weight_full = (
        lax.all_gather(input_weight, "dp", axis=0, tiled=True),
        lax.all_gather(output_weight, "dp", axis=0, tiled=True),
    )
    inputs = tokens.astype(jnp.float32)
    scale_one = rms_scale(inputs)
    normalized_input = (inputs * scale_one * norm1_gain).astype(jnp.bfloat16)
    projected_output = jnp.einsum(
        "aiv,vn->ain", normalized_input, input_weight_full, preferred_element_type=jnp.float32
    )
    query_raw = projected_output[..., :query_width].reshape(
        sequence_count, device_local_rows, QUERY_HEADS, HEAD_DIMENSION
    )
    key_unrotated = projected_output[..., query_width : query_width + key_value_width].reshape(
        sequence_count, device_local_rows, KEY_VALUE_HEADS, HEAD_DIMENSION
    )
    value_unprojected = projected_output[
        ..., query_width + key_value_width : query_width + 2 * key_value_width
    ].reshape(sequence_count, device_local_rows, KEY_VALUE_HEADS, HEAD_DIMENSION)
    gate = jax.nn.sigmoid(projected_output[..., query_width + 2 * key_value_width :])
    query_scale = rms_scale(query_raw)
    key_scale = rms_scale(key_unrotated)
    queries = rotate(query_raw * query_scale * query_gain, cosine, sine).astype(jnp.bfloat16)
    keys = rotate(key_unrotated * key_scale * key_gain, cosine, sine).astype(jnp.bfloat16)
    values = value_unprojected.astype(jnp.bfloat16)
    sent_keys = jnp.repeat(keys, head_copies, axis=2)
    sent_values = jnp.repeat(values, head_copies, axis=2)
    head_q, head_k, head_v = (
        lax.all_to_all(queries, "ulysses", split_axis=2, concat_axis=1, tiled=True),
        lax.all_to_all(sent_keys, "ulysses", split_axis=2, concat_axis=1, tiled=True),
        lax.all_to_all(sent_values, "ulysses", split_axis=2, concat_axis=1, tiled=True),
    )
    head_out, log_totals = attend_forward(
        head_q, head_k, head_v, valid_keys, score_scale, block_rows
    )
    attended = lax.all_to_all(
        head_out.astype(jnp.bfloat16), "ulysses", split_axis=1, concat_axis=2, tiled=True
    )
    attended_flat = attended.reshape(sequence_count, device_local_rows, query_width).astype(
        jnp.float32
    )
    gated_product = (attended_flat * gate).astype(jnp.bfloat16)
    hidden_in = inputs + jnp.einsum(
        "hzm,mw->hzw", gated_product, output_weight_full, preferred_element_type=jnp.float32
    )
    scale_two = rms_scale(hidden_in)
    second_normalized = (hidden_in * scale_two * norm2_gain).astype(jnp.bfloat16)
    perceptron_weight_full, down_weight_full = (
        lax.all_gather(perceptron_input_weight, "dp", axis=0, tiled=True),
        lax.all_gather(down_weight, "dp", axis=0, tiled=True),
    )
    gate_up_product = jnp.einsum(
        "hmr,rz->hmz", second_normalized, perceptron_weight_full, preferred_element_type=jnp.float32
    )
    act_gate = gate_up_product[..., :FF]
    act_up = gate_up_product[..., FF:]
    sigmoid_gate = jax.nn.sigmoid(act_gate)
    silu_gate = act_gate * sigmoid_gate
    hidden_state = (silu_gate * act_up).astype(jnp.bfloat16)
    layer_out = hidden_in + jnp.einsum(
        "zbo,oh->zbh", hidden_state, down_weight_full, preferred_element_type=jnp.float32
    )
    result_gradient = jnp.where(live_rows, cotangent, jnp.zeros_like(cotangent))
    perceptron_weight_backward, down_weight_backward = (perceptron_weight_full, down_weight_full)
    token_count = sequence_count * device_local_rows
    result_flat = result_gradient.reshape(token_count, model_width)
    hidden_flat = hidden_state.reshape(token_count, FF)
    column_block = hidden_flat
    down_grad = lax.psum_scatter(
        jnp.einsum(
            "tf,td->fd", column_block, result_flat, preferred_element_type=jnp.float32
        ).astype(jnp.bfloat16),
        "dp",
        scatter_dimension=0,
        tiled=True,
    )
    grad_hidden = jnp.einsum(
        "axg,ng->axn", result_gradient, down_weight_backward, preferred_element_type=jnp.float32
    )
    grad_gate = grad_hidden * act_up * sigmoid_gate * (1.0 + act_gate * (1.0 - sigmoid_gate))
    grad_up = grad_hidden * silu_gate
    gate_up_gradient = jnp.concatenate([grad_gate, grad_up], axis=-1).astype(jnp.bfloat16)
    gate_up_flat = gate_up_gradient.reshape(token_count, 2 * FF)
    normed_two_flat = second_normalized.reshape(token_count, model_width)
    column_block = normed_two_flat
    mlp_in_grad = lax.psum_scatter(
        jnp.einsum(
            "td,tf->df", column_block, gate_up_flat, preferred_element_type=jnp.float32
        ).astype(jnp.bfloat16),
        "dp",
        scatter_dimension=0,
        tiled=True,
    )
    grad_normed_two = jnp.einsum(
        "pav,tv->pat",
        gate_up_gradient,
        perceptron_weight_backward,
        preferred_element_type=jnp.float32,
    )
    norm_two_back, gain_two_terms = norm_back(hidden_in, scale_two, norm2_gain, grad_normed_two)
    grad_hidden_in = result_gradient.astype(jnp.float32) + norm_two_back
    branch_gradient = grad_hidden_in.astype(jnp.bfloat16)
    input_weight_backward, output_weight_backward = (input_weight_full, output_weight_full)
    branch_flat = branch_gradient.reshape(token_count, model_width)
    gated_flat = gated_product.reshape(token_count, query_width)
    column_block = gated_flat
    out_grad = lax.psum_scatter(
        jnp.einsum(
            "te,td->ed", column_block, branch_flat, preferred_element_type=jnp.float32
        ).astype(jnp.bfloat16),
        "dp",
        scatter_dimension=0,
        tiled=True,
    )
    grad_gated = jnp.einsum(
        "qtk,ak->qta", branch_gradient, output_weight_backward, preferred_element_type=jnp.float32
    )
    grad_attended = (
        (grad_gated * gate)
        .astype(jnp.bfloat16)
        .reshape(sequence_count, device_local_rows, QUERY_HEADS, HEAD_DIMENSION)
    )
    grad_gate_raw = grad_gated * attended_flat * gate * (1.0 - gate)
    head_grad = lax.all_to_all(grad_attended, "ulysses", split_axis=2, concat_axis=1, tiled=True)
    query_head_grad, key_head_grad, value_head_grad = attend_backward(
        head_q, head_k, head_v, head_grad, log_totals, valid_keys, score_scale, block_rows
    )
    key_head_grad = key_head_grad.reshape(
        sequence_count,
        bucket_size,
        key_head_grad.shape[2] // head_copies,
        head_copies,
        HEAD_DIMENSION,
    ).sum(axis=3)
    value_head_grad = value_head_grad.reshape(
        sequence_count,
        bucket_size,
        value_head_grad.shape[2] // head_copies,
        head_copies,
        HEAD_DIMENSION,
    ).sum(axis=3)
    query_back, key_back, value_back = (
        lax.all_to_all(
            query_head_grad.astype(jnp.bfloat16), "ulysses", split_axis=1, concat_axis=2, tiled=True
        ),
        lax.all_to_all(
            key_head_grad.astype(jnp.bfloat16), "ulysses", split_axis=1, concat_axis=2, tiled=True
        ),
        lax.all_to_all(
            value_head_grad.astype(jnp.bfloat16), "ulysses", split_axis=1, concat_axis=2, tiled=True
        ),
    )
    query_plain = unrotate(query_back.astype(jnp.float32), cosine, sine)
    key_plain = unrotate(key_back.astype(jnp.float32), cosine, sine)
    grad_query_raw, query_terms = norm_back(query_raw, query_scale, query_gain, query_plain)
    grad_key_raw, key_terms = norm_back(key_unrotated, key_scale, key_gain, key_plain)
    projected_gradient = jnp.concatenate(
        [
            grad_query_raw.reshape(sequence_count, device_local_rows, query_width),
            grad_key_raw.reshape(sequence_count, device_local_rows, key_value_width),
            value_back.reshape(sequence_count, device_local_rows, key_value_width).astype(
                jnp.float32
            ),
            grad_gate_raw,
        ],
        axis=-1,
    ).astype(jnp.bfloat16)
    project_flat = projected_gradient.reshape(token_count, projected_gradient.shape[-1])
    normed_flat = normalized_input.reshape(token_count, model_width)
    column_block = normed_flat
    in_grad = lax.psum_scatter(
        jnp.einsum(
            "td,te->de", column_block, project_flat, preferred_element_type=jnp.float32
        ).astype(jnp.bfloat16),
        "dp",
        scatter_dimension=0,
        tiled=True,
    )
    grad_normed = jnp.einsum(
        "fvx,zx->fvz", projected_gradient, input_weight_backward, preferred_element_type=jnp.float32
    )
    norm_one_back, gain_one_terms = norm_back(inputs, scale_one, norm1_gain, grad_normed)
    tokens_grad = grad_hidden_in + norm_one_back
    gain_one, gain_query, gain_key, gain_two = lax.psum(
        (
            gain_one_terms.sum(axis=(0, 1)),
            query_terms.sum(axis=(0, 1, 2)),
            key_terms.sum(axis=(0, 1, 2)),
            gain_two_terms.sum(axis=(0, 1)),
        ),
        ("dp", "ulysses"),
    )
    in_total, out_total, mlp_total, down_total = (
        lax.psum(in_grad, "ulysses").astype(jnp.float32),
        lax.psum(out_grad, "ulysses").astype(jnp.float32),
        lax.psum(mlp_in_grad, "ulysses").astype(jnp.float32),
        lax.psum(down_grad, "ulysses").astype(jnp.float32),
    )
    return (
        layer_out,
        tokens_grad,
        gain_one,
        in_total,
        gain_query,
        gain_key,
        out_total,
        gain_two,
        mlp_total,
        down_total,
    )


def solution(mesh):
    placed = (
        P("dp", "ulysses", None),
        P("dp"),
        P("dp", "ulysses", None),
        P(),
        P("dp", None),
        P(),
        P(),
        P("dp", None),
        P(),
        P("dp", None),
        P("dp", None),
    )
    return jax.shard_map(
        shards,
        mesh=mesh,
        in_specs=placed,
        out_specs=(
            P("dp", "ulysses", None),
            P("dp", "ulysses", None),
            P(),
            P("dp", None),
            P(),
            P(),
            P("dp", None),
            P(),
            P("dp", None),
            P("dp", None),
        ),
        check_vma=False,
    )
```

profile of v0, /device:TPU:0, one launch (start us, length us, event | category | flops | bytes accessed | tf_op | source)
XLA Modules:
  0.0 4128.6 jit_solution(13353313125181815715)
XLA Ops:
  12.0 480.7 %all-gather.5.cloned.1.call-done = bf16[2048,6144]{1,0:T(8,128)(2,1)} async-done(((bf16[256,6144]{1,0:T(8,128)(2,1)}), bf16[2048,6144]{1,0:T(8,128)(2,1)}) %all-gather.5.cloned.1.call-update) | async-done | bytes 25165840 | tf_op jit(solution)/shard_map/all_gather | solution.py:162
  492.7 11.7 convolution_bitcast_fusion.2
  535.1 11.4 all-to-all-done.1
  557.1 8.7 all-to-all-done.2
  584.5 14.2 all-to-all-done.3
  604.8 14.9 all-gather.7.cloned.1.call-done
  626.0 945.9 %all-gather.9.cloned.1.call-done = bf16[2048,12288]{1,0:T(8,128)(2,1)} async-done(((bf16[256,12288]{1,0:T(8,128)(2,1)}), bf16[2048,12288]{1,0:T(8,128)(2,1)}) %all-gather.9.cloned.1.call-update) | async-done | bytes 50331664 | tf_op jit(solution)/shard_map/all_gather | solution.py:209
  1571.9 25.6 convolution_bitcast_fusion
  1597.5 456.2 %all-gather.11.cloned.1.call-done = bf16[6144,2048]{1,0:T(8,128)(2,1)} async-done(((bf16[768,2048]{1,0:T(8,128)(2,1)}), bf16[6144,2048]{1,0:T(8,128)(2,1)}) %all-gather.11.cloned.1.call-update) | async-done | bytes 25165840 | tf_op jit(solution)/shard_map/all_gather | solution.py:210
  2053.7 19.5 fusion.18
  2073.1 23.9 fusion.41
  2105.9 14.4 convolution_convert_fusion.1
  2123.4 8.4 fusion.57
  2159.8 6.9 bitcast_reduce_fusion
  2173.1 6.3 fusion.3
  2247.2 12.1 convolution_convert_fusion.2
  2259.6 23.2 convolution_convert_fusion
  2282.9 379.0 %reduce-scatter.11.cloned.1.call-done = bf16[768,2048]{1,0:T(8,128)(2,1)} async-done(((bf16[6144,2048]{1,0:T(8,128)(2,1)}), bf16[768,2048]{1,0:T(8,128)(2,1)}) %reduce-scatter.11.cloned.1.call-update) | async-done | bytes 3145744 | tf_op jit(solution)/shard_map/reduce_scatter | solution.py:229
  2661.9 407.0 %reduce-scatter.7.cloned.1.call-done = bf16[256,6144]{1,0:T(8,128)(2,1)} async-done(((bf16[2048,6144]{1,0:T(8,128)(2,1)}), bf16[256,6144]{1,0:T(8,128)(2,1)}) %reduce-scatter.7.cloned.1.call-update) | async-done | bytes 3145744 | tf_op jit(solution)/shard_map/reduce_scatter | solution.py:331
  3069.0 793.7 %reduce-scatter.13.cloned.1.call-done = bf16[256,12288]{1,0:T(8,128)(2,1)} async-done(((bf16[2048,12288]{1,0:T(8,128)(2,1)}), bf16[256,12288]{1,0:T(8,128)(2,1)}) %reduce-scatter.13.cloned.1.call-update) | async-done | bytes 6291472
  3862.7 15.7 fusion.19
  3878.5 13.4 fusion.28
  3891.9 40.9 all-reduce.1
  3936.2 168.5 %all-reduce.5.cloned.1.call-done = (bf16[256,6144]{1,0:T(8,128)(2,1)}, bf16[256,2048]{1,0:T(8,128)(2,1)}, bf16[256,12288]{1,0:T(8,128)(2,1)}, bf16[768,2048]{1,0:T(8,128)(2,1)}) async-done(((bf16[256,6144]{1,0:T(8,128)(2,1)}, bf16[256,2048]{1,0:T(8,128)(2,1)}, bf16[256,12288]{1,0:T(8,128)(2,1)}, bf16[768,2048]{1,0:T(8,128)(2,1)}), (bf16[256,6144]{1,0:T(8,128)(2,1)}, bf16[256,2048]{1,0:T(8,128)(2,1)}, ...) | async-done | bytes 13631504 | tf_op jit(solution)/shard_map/psum | solution.py:354
  (261 shorter events, 210.4 us)
Async XLA Ops:
  7.2 485.5 %all-gather.5.cloned.1.call-start = ((), (), s32[]{:S(2)}) async-start(), calls=%async_computation.12 | async-start | bytes 28311552 | tf_op jit(solution)/shard_map/all_gather | solution.py:162
  7.9 611.9 %all-gather.7.cloned.1.call-start = ((), (), s32[]{:S(2)}) async-start(), calls=%async_computation.13 | async-start | bytes 9437184 | tf_op jit(solution)/shard_map/all_gather | solution.py:163
  8.7 1563.2 %all-gather.9.cloned.1.call-start = ((), (), s32[]{:S(2)}) async-start(), calls=%async_computation.14 | async-start | bytes 56623104 | tf_op jit(solution)/shard_map/all_gather | solution.py:209
  9.4 483.3 %copy-start.44 = (f32[2048]{0:T(1024)S(1)}, f32[2048]{0:T(1024)}, u32[]{:S(2)}) copy-start(f32[2048]{0:T(1024)} %param.14) | copy-start | bytes 24580
  9.4 2044.3 %all-gather.11.cloned.1.call-start = ((), (), s32[]{:S(2)}) async-start(), calls=%async_computation.15 | async-start | bytes 28311552 | tf_op jit(solution)/shard_map/all_gather | solution.py:210
  11.5 493.0 %copy-start.47 = (f32[256]{0:T(256)}, f32[256]{0:T(256)S(1)}, u32[]{:S(2)}) copy-start(f32[256]{0:T(256)S(1)} %get-tuple-element.54) | copy-start | bytes 3076
  12.0 520.7 %copy-start.33 = (f32[256,64]{1,0:T(8,128)}, f32[256,64]{1,0:T(8,128)S(1)}, u32[]{:S(2)}) copy-start(f32[256,64]{1,0:T(8,128)S(1)} %get-tuple-element.51) | copy-start | bytes 196612
  12.0 520.7 %copy-start.35 = (f32[256,64]{1,0:T(8,128)}, f32[256,64]{1,0:T(8,128)S(1)}, u32[]{:S(2)}) copy-start(f32[256,64]{1,0:T(8,128)S(1)} %get-tuple-element.52) | copy-start | bytes 196612
  508.6 18.8 all-to-all-start
  528.5 18.0 all-to-all-start.1
  546.5 19.3 all-to-all-start.2
  580.8 18.0 all-to-all-start.3
  584.3 1698.6 %reduce-scatter.9.cloned.1.call-start = ((), (), s32[]{:S(2)}) async-start(), calls=%async_computation.17 | async-start | bytes 9437184 | tf_op jit(solution)/shard_map/reduce_scatter | solution.py:267
  604.8 967.0 %copy-start.46 = (f32[2048]{0:T(1024)S(1)}, f32[2048]{0:T(1024)}, u32[]{:S(2)}) copy-start(f32[2048]{0:T(1024)} %param.19) | copy-start | bytes 24580
  626.0 1447.2 %copy-start.23 = (f32[1,256,2048]{2,1,0:T(8,128)}, f32[1,256,2048]{2,1,0:T(8,128)S(1)}, u32[]{:S(2)}) copy-start(f32[1,256,2048]{2,1,0:T(8,128)S(1)} %get-tuple-element.64) | copy-start | bytes 6291460
  1571.8 481.8 %copy-start.30 = (bf16[1,256,2048]{2,1,0:T(8,128)(2,1)S(1)}, bf16[1,256,2048]{2,1,0:T(8,128)(2,1)}, u32[]{:S(2)}) copy-start(bf16[1,256,2048]{2,1,0:T(8,128)(2,1)} %param.13) | copy-start | bytes 3145732
  2105.8 556.1 %reduce-scatter.11.cloned.1.call-start = ((), (), s32[]{:S(2)}) async-start(), calls=%async_computation.18 | async-start | bytes 28311552 | tf_op jit(solution)/shard_map/reduce_scatter | solution.py:229
  2133.0 19.2 all-to-all-start.4
  2168.8 32.4 all-to-all-start.7
  2201.2 13.1 all-to-all-start.6
  2214.2 18.0 all-to-all-start.5
  2217.8 851.2 %reduce-scatter.7.cloned.1.call-start = ((), (), s32[]{:S(2)}) async-start(), calls=%async_computation.16 | async-start | bytes 28311552 | tf_op jit(solution)/shard_map/reduce_scatter | solution.py:331
  2259.3 1603.3 %reduce-scatter.13.cloned.1.call-start = ((), (), s32[]{:S(2)}) async-start(), calls=%async_computation.19 | async-start | bytes 56623104
  2282.8 1821.8 %all-reduce.5.cloned.1.call-start = ((), (), s32[]{:S(2)}) async-start(), calls=%async_computation.20 | async-start | bytes 27262976 | tf_op jit(solution)/shard_map/psum | solution.py:354
  (52 other events, 431.2 us)
Sparse Core Ops, SparseCore 0:
  9.5 483.1 all-gather.4
  494.8 124.8 all-gather.6
  621.3 950.4 all-gather.8
  1573.2 480.3 all-gather.10
  2106.0 148.9 reduce-scatter.8
  2259.2 402.6 reduce-scatter.10
  2666.3 402.6 reduce-scatter.6
  3073.3 789.2 reduce-scatter.12
  3865.4 239.2 all-reduce.4
where the time goes:
time: 4140 us; the launch traced here: 4130 us
  waiting for transfers between devices  3690 us (89%)
  matrix products  221 us (5%)
  other arithmetic  62.2 us (2%)
  local copies, waits for them, and re-layouts  61.5 us (1%)
    all_gather x1, waiting for transfers between devices, shards(): lax.all_gather(perceptron_input_weight, 'dp', axis=0, tiled=True)  946 us
    unnamed x10, waiting for transfers between devices  796 us
    all_gather x1, waiting for transfers between devices, shards(): lax.all_gather(input_weight, 'dp', axis=0, tiled=True)  481 us
    all_gather x1, waiting for transfers between devices, shards(): lax.all_gather(down_weight, 'dp', axis=0, tiled=True)  456 us
    reduce_scatter x1, waiting for transfers between devices, shards(): lax.psum_scatter(jnp.einsum('td,te->de', column_block, project_flat, pref...  407 us
    reduce_scatter x1, waiting for transfers between devices, shards(): lax.psum_scatter(jnp.einsum('tf,td->fd', column_block, result_flat, prefe...  379 us
    psum x1, waiting for transfers between devices, shards(): lax.psum(in_grad, 'ulysses').astype(jnp.float32)  168 us
  transfers between devices with their start and end apart: 17, of which 15 were waited for; matrix products, arithmetic and copies ran while one was open for 7% of the time, Pallas kernels for 0%

commit v1 on v0

v1 whole, which is shorter than its diff:
```python
import functools

import jax
import jax.numpy as jnp
import numpy as np
from jax import lax
from jax.experimental import pallas as pl
from jax.experimental.pallas import tpu as pltpu
from jax.sharding import PartitionSpec as P

QUERY_HEADS = 16
KEY_VALUE_HEADS = 8
HEAD_DIMENSION = 128
FF = 6144


EPSILON = 1e-06
ROPE_BASE = 1000000.0
MASKED = -1e30


def rms_scale(values):
    return lax.rsqrt(jnp.mean(values * values, axis=-1, keepdims=True) + EPSILON)


VMEM_LIMIT = 56 * 1024 * 1024
NT = (((1,), (1,)), ((), ()))
TN = (((0,), (0,)), ((), ()))


def params():
    return pltpu.CompilerParams(vmem_limit_bytes=VMEM_LIMIT)


def cost(*_):
    return pl.CostEstimate(flops=1, bytes_accessed=1, transcendentals=0)


def steady(shape):
    return pl.BlockSpec(shape, lambda *_: (0,) * len(shape), pipeline_mode=pl.Buffered(1))


def tile_of(size):
    return 256 if size % 256 == 0 else 128


def head_scale(raw):
    return lax.rsqrt(jnp.mean(raw * raw, axis=-1, keepdims=True) + EPSILON)


def turn_pairs(value, cosine, sine):
    return value * cosine + pltpu.roll(value, HEAD_DIMENSION // 2, 1) * sine


def masked_scores(q, k, first_row, length):
    scores = lax.dot_general(q, k, NT, preferred_element_type=jnp.float32)
    scores = scores * HEAD_DIMENSION ** (-0.5)
    row = first_row + lax.broadcasted_iota(jnp.int32, scores.shape, 0)
    column = lax.broadcasted_iota(jnp.int32, scores.shape, 1)
    return jnp.where((column <= row) & (column < length), scores, MASKED)


def in_order(ref, me):
    return jnp.concatenate([ref[me ^ t] for t in range(ref.shape[0])], axis=0)


def attend_back_kernel(
    block, copies, heads, kv_heads, place_ref, q_raw, k_raw, q_ref, k_ref, v_ref, gate_ref, attended_ref, up_ref,
    total_ref, q_gain, k_gain, cosine, sine, qk_out, vg_out, q_gain_out, k_gain_out, grad_ref, dq_ref, dk_ref, dv_ref,
):
    group = pl.program_id(0)
    bucket, size = k_ref.shape
    n_u, rows_own, _ = q_raw.shape
    scale = size ** (-0.5)
    length, me = place_ref[0], place_ref[1]

    @pl.when(group == 0)
    def _():
        q_gain_out[...] = jnp.zeros_like(q_gain_out)
        k_gain_out[...] = jnp.zeros_like(k_gain_out)

    def store(out, at, width, value):
        for t in range(n_u):
            out[me ^ t, :, pl.ds(pl.multiple_of(at, size), width)] = value[t * rows_own : (t + 1) * rows_own]

    up, gate = in_order(up_ref, me), gate_ref[...]
    grad_ref[...] = (up * gate).astype(jnp.bfloat16)
    grad_gate = (up * attended_ref[...].astype(jnp.float32) * gate * (1.0 - gate)).astype(jnp.bfloat16)
    store(vg_out, (kv_heads + group * copies) * size, copies * size, grad_gate)
    dk_ref[...] = jnp.zeros_like(dk_ref)
    dv_ref[...] = jnp.zeros_like(dv_ref)

    def norm_grad(raw, gain, upstream, gain_out):
        factor = head_scale(raw)
        weighted = upstream * gain
        inner = jnp.mean(weighted * raw, axis=-1, keepdims=True)
        gain_out[...] += jnp.sum(upstream * raw * factor, axis=0, keepdims=True)
        return (factor * weighted - raw * (factor * factor * factor) * inner).astype(jnp.bfloat16)

    raw_q = in_order(q_raw, me)
    for copy in range(copies):
        columns = slice(copy * size, (copy + 1) * size)
        for first in range(0, bucket, block):
            rows = slice(first, first + block)
            reach = slice(0, first + block)
            q, g = q_ref[rows, columns], grad_ref[rows, columns]
            soft = jnp.exp(masked_scores(q, k_ref[reach], first, length) - total_ref[copy, rows])
            soft_grad = lax.dot_general(g, v_ref[reach], NT, preferred_element_type=jnp.float32)
            inner = jnp.sum(soft * soft_grad, axis=-1, keepdims=True)
            score_grad = (soft * (soft_grad - inner)).astype(jnp.bfloat16)
            dq_ref[rows] = jnp.dot(score_grad, k_ref[reach], preferred_element_type=jnp.float32) * scale
            dk_ref[reach] += lax.dot_general(score_grad, q, TN, preferred_element_type=jnp.float32)
            dv_ref[reach] += lax.dot_general(soft.astype(jnp.bfloat16), g, TN, preferred_element_type=jnp.float32)
        plain = turn_pairs(dq_ref[...].astype(jnp.bfloat16).astype(jnp.float32), cosine[...], -sine[...])
        store(qk_out, (group * copies + copy) * size, size, norm_grad(raw_q[:, columns], q_gain[...], plain, q_gain_out))
    plain = turn_pairs((dk_ref[...] * scale).astype(jnp.bfloat16).astype(jnp.float32), cosine[...], -sine[...])
    store(qk_out, (heads + group) * size, size, norm_grad(in_order(k_raw, me), k_gain[...], plain, k_gain_out))
    store(vg_out, group * size, size, dv_ref[...].astype(jnp.bfloat16))


def attend_back(place, raw_qk, q, k, v, gate, attended, upstream, totals, q_gain, k_gain, cosine, sine):
    size = HEAD_DIMENSION
    n_u, rows_own, _ = raw_qk.shape
    bucket = n_u * rows_own
    heads, kv_heads = q.shape[1] // size, k.shape[1] // size
    copies = heads // kv_heads

    def blocks(width, start):
        return pl.BlockSpec((n_u, rows_own, width), lambda g: (0, 0, start + g))

    wide = pl.BlockSpec((bucket, copies * size), lambda g: (0, g))
    slim = pl.BlockSpec((bucket, size), lambda g: (0, g))
    total = (heads + kv_heads) * size
    whole = pl.BlockSpec((n_u, rows_own, total), lambda g: (0, 0, 0))
    gain = pl.BlockSpec((1, size), lambda g: (0, 0))
    return pl.pallas_call(
        functools.partial(attend_back_kernel, min(256, bucket), copies, heads, kv_heads),
        grid=(kv_heads,),
        in_specs=[
            pl.BlockSpec(memory_space=pltpu.SMEM),
            blocks(copies * size, 0),
            blocks(size, heads),
            wide,
            slim,
            slim,
            wide,
            wide,
            blocks(copies * size, 0),
            pl.BlockSpec((copies, bucket, 1), lambda g: (g, 0, 0)),
            steady((1, size)),
            steady((1, size)),
            steady((bucket, size)),
            steady((bucket, size)),
        ],
        out_specs=[whole, whole, gain, gain],
        out_shape=[
            jax.ShapeDtypeStruct((n_u, rows_own, total), jnp.bfloat16),
            jax.ShapeDtypeStruct((n_u, rows_own, total), jnp.bfloat16),
            jax.ShapeDtypeStruct((1, size), jnp.float32),
            jax.ShapeDtypeStruct((1, size), jnp.float32),
        ],
        scratch_shapes=[
            pltpu.VMEM((bucket, copies * size), jnp.bfloat16),
            pltpu.VMEM((bucket, size), jnp.float32),
            pltpu.VMEM((bucket, size), jnp.float32),
            pltpu.VMEM((bucket, size), jnp.float32),
        ],
        compiler_params=params(),
        cost_estimate=cost(5 * heads * bucket * bucket * size, 24 * bucket * heads * size, heads * bucket * bucket // 2),
        name="attention_back",
    )(place, raw_qk, raw_qk, q, k, v, gate, attended, upstream, totals, q_gain, k_gain, cosine, sine)


def gate_up(x, first, second):
    m, width = x.shape
    n = first.shape[1]
    tile = tile_of(n)
    step_rows = min(256, m)

    def kernel(x_ref, first_ref, second_ref, a_out, b_out, hidden_out):
        for at in range(0, m, step_rows):
            rows = slice(at, at + step_rows)
            a = jnp.dot(x_ref[rows], first_ref[...], preferred_element_type=jnp.float32)
            b = jnp.dot(x_ref[rows], second_ref[...], preferred_element_type=jnp.float32)
            a_out[rows] = a
            b_out[rows] = b
            hidden_out[rows] = (a * jax.nn.sigmoid(a) * b).astype(jnp.bfloat16)

    weight = pl.BlockSpec((width, tile), lambda j: (0, j))
    out = pl.BlockSpec((m, tile), lambda j: (0, j))
    return pl.pallas_call(
        kernel,
        grid=(n // tile,),
        in_specs=[steady((m, width)), weight, weight],
        out_specs=[out] * 3,
        out_shape=[jax.ShapeDtypeStruct((m, n), d) for d in (jnp.float32, jnp.float32, jnp.bfloat16)],
        compiler_params=params(),
        cost_estimate=cost(),
        name="gate_up",
    )(x, first, second)


def back_matmul(a, b, first, second, rows):
    m, n = a.shape
    width = first.shape[0]
    part = 256

    def kernel(a_ref, b_ref, first_ref, second_ref, keep_ref, send_ref):
        for at in range(0, width, part):
            where = slice(at, at + part)
            out = lax.dot_general(a_ref[...], first_ref[where], NT, preferred_element_type=jnp.float32)
            out += lax.dot_general(b_ref[...], second_ref[where], NT, preferred_element_type=jnp.float32)
            out = out.astype(jnp.bfloat16)
            keep_ref[0, :, where] = out[:rows]
            send_ref[0, :, where] = out[rows:]

    step = pl.BlockSpec((2 * rows, n), lambda i: (i, 0))
    out = pl.BlockSpec((1, rows, width), lambda i: (i, 0, 0))
    shape = jax.ShapeDtypeStruct((m // rows // 2, rows, width), jnp.bfloat16)
    return pl.pallas_call(
        kernel,
        grid=(m // rows // 2,),
        in_specs=[step, step, steady(first.shape), steady(second.shape)],
        out_specs=[out, out],
        out_shape=[shape, shape],
        compiler_params=params(),
        cost_estimate=cost(),
        name="back_matmul",
    )(a, b, first, second)


def outer_terms(x, y, count):
    m, width = x.shape
    n = y.shape[1]
    depth = width // count

    def kernel(x_ref, y_ref, out_ref):
        out_ref[...] = lax.dot_general(x_ref[...], y_ref[...], TN, preferred_element_type=jnp.float32).astype(jnp.bfloat16)

    return pl.pallas_call(
        kernel,
        grid=(count,),
        in_specs=[pl.BlockSpec((m, depth), lambda k: (0, k)), steady((m, n))],
        out_specs=pl.BlockSpec((depth, n), lambda k: (k, 0)),
        out_shape=jax.ShapeDtypeStruct((width, n), jnp.bfloat16),
        compiler_params=params(),
        cost_estimate=cost(2 * m * n * width, 2 * m * width + 2 * m * n + 2 * n * width),
        name="outer_terms",
    )(x, y)


def down_back(upstream, a, b, weight):
    m, width = upstream.shape
    n = a.shape[1]
    rows = min(256, m)

    def kernel(up_ref, a_ref, b_ref, weight_ref, gate_out, up_out):
        grad = lax.dot_general(up_ref[...], weight_ref[...], NT, preferred_element_type=jnp.float32)
        a, b = a_ref[...], b_ref[...]
        sig = jax.nn.sigmoid(a)
        gate_out[...] = (grad * b * sig * (1.0 + a * (1.0 - sig))).astype(jnp.bfloat16)
        up_out[...] = (grad * a * sig).astype(jnp.bfloat16)

    step = pl.BlockSpec((rows, n), lambda i: (i, 0))
    shape = jax.ShapeDtypeStruct((m, n), jnp.bfloat16)
    return pl.pallas_call(
        kernel,
        grid=(m // rows,),
        in_specs=[pl.BlockSpec((rows, width), lambda i: (i, 0)), step, step, steady((n, width))],
        out_specs=[step, step],
        out_shape=[shape, shape],
        compiler_params=params(),
        cost_estimate=cost(2 * m * n * width, 2 * m * width + 12 * m * n + 2 * n * width),
        name="down_back",
    )(upstream, a, b, weight)


def strips_kernel(n_dp, n_u, strip, place_ref, w_ref, gate_ref, up_ref):
    for t in range(n_u):

        @pl.when(place_ref[1] == t)
        def _():
            for half, out in enumerate((gate_ref, up_ref)):
                starts = [((half * n_dp + b) * n_u + t) * strip for b in range(n_dp)]
                out[...] = jnp.concatenate([w_ref[:, s : s + strip] for s in starts], axis=1)


def take_strips(place, w, n_dp, n_u, strip):
    depth, total = w.shape
    rows = 64
    out = pl.BlockSpec((rows, n_dp * strip), lambda i: (i, 0))
    shape = jax.ShapeDtypeStruct((depth, n_dp * strip), w.dtype)
    return pl.pallas_call(
        functools.partial(strips_kernel, n_dp, n_u, strip),
        grid=(depth // rows,),
        in_specs=[pl.BlockSpec(memory_space=pltpu.SMEM), pl.BlockSpec((rows, total), lambda i: (i, 0))],
        out_specs=[out, out],
        out_shape=[shape, shape],
        compiler_params=params(),
        cost_estimate=cost(0, 2 * depth * total + 4 * depth * n_dp * strip),
        name="take_strips",
    )(place, w)


def fill(scratch, keys, refs):
    for key_list, ref in zip(keys, refs):
        for at, key in enumerate(key_list):
            scratch[key] = ref[at]


def put_call(kernel, place, helds, grid, blocks, at, out_block, out_at, out_shape, name):
    n_u = sum(len(k) for k in helds[0][0])
    count = sum(len(b) for _, b in helds)

    def body(place_ref, *refs):
        refs = list(refs)
        scratches = refs[count + 1 :]
        for (keys, _), scratch in zip(helds, scratches):
            fill(scratch, keys, [refs.pop(0) for _ in keys])
        kernel(place_ref[1], scratches, refs[0])

    return pl.pallas_call(
        body,
        grid=(grid,),
        in_specs=[pl.BlockSpec(memory_space=pltpu.SMEM)]
        + [pl.BlockSpec((len(k),) + block, at) for (keys, _), block in zip(helds, blocks) for k in keys],
        out_specs=pl.BlockSpec(out_block, out_at),
        out_shape=jax.ShapeDtypeStruct(out_shape, jnp.float32),
        scratch_shapes=[pltpu.VMEM((n_u,) + block, jnp.bfloat16) for block in blocks],
        compiler_params=params(),
        cost_estimate=cost(0, 6 * out_shape[0] * out_shape[1]),
        name=name,
    )(place, *[v for _, held in helds for v in held])


def put_strips(place, helds, n_dp, strip):
    n_u = sum(len(k) for k in helds[0][0])
    depth, width = helds[0][1][0].shape[1:]
    rows = min(32, depth)

    def kernel(me, scratches, out_ref):
        size = n_u * strip
        for h, scratch in enumerate(scratches):
            parts = [scratch[me ^ t].astype(jnp.float32) for t in range(n_u)]
            for b in range(n_dp):
                at = (h * n_dp + b) * size
                out_ref[:, at : at + size] = jnp.concatenate(
                    [p[:, b * strip : (b + 1) * strip] for p in parts], axis=1
                )

    total = len(helds) * n_u * width
    return put_call(
        kernel, place, helds, depth // rows, [(rows, width)] * len(helds), lambda i: (0, i, 0),
        (rows, total), lambda i: (i, 0), (depth, total), "put_strips",
    )


def put_columns(place, helds, sections):
    n_u = sum(len(k) for k in helds[0][0])
    depth = helds[0][1][0].shape[1]
    rows = min(64, depth)

    def kernel(me, scratches, out_ref):
        at = 0
        for scratch, parts in zip(scratches, sections):
            for start, size in parts:
                for t in range(n_u):
                    out_ref[:, at : at + size] = scratch[me ^ t, :, start : start + size].astype(jnp.float32)
                    at += size

    total = n_u * sum(size for parts in sections for _, size in parts)
    return put_call(
        kernel, place, helds, depth // rows, [(rows, held[0].shape[2]) for _, held in helds], lambda i: (0, i, 0),
        (rows, total), lambda i: (i, 0), (depth, total), "put_columns",
    )


def put_rows(place, held):
    n_u = sum(len(k) for k in held[0])
    depth, width = held[1][0].shape[1:]
    tile = 512

    def kernel(me, scratches, out_ref):
        for t in range(n_u):
            out_ref[t * depth : (t + 1) * depth] = scratches[0][me ^ t].astype(jnp.float32)

    return put_call(
        kernel, place, [held], width // tile, [(depth, tile)], lambda i: (0, 0, i),
        (n_u * depth, tile), lambda i: (0, i), (n_u * depth, width), "put_rows",
    )


def norm_call(kernel, inputs, gain, outs, gain_sum, name):
    r, width = inputs[0].shape
    tile = min(64, r)
    step = pl.BlockSpec((tile, width), lambda i: (i, 0))
    one = pl.BlockSpec((1, width), lambda i: (0, 0))
    shapes = [jax.ShapeDtypeStruct((r, width), o) for o in outs]
    if gain_sum:
        shapes.append(jax.ShapeDtypeStruct((1, width), jnp.float32))
    return pl.pallas_call(
        kernel,
        grid=(r // tile,),
        in_specs=[step] * len(inputs) + [one],
        out_specs=[step] * len(outs) + [one] * gain_sum,
        out_shape=shapes,
        compiler_params=params(),
        cost_estimate=cost(0, sum(4 * v.size for v in inputs)),
        name=name,
    )(*inputs, gain)


def norm_back(source, keep, got, residual, gain, rounded):
    def kernel(source_ref, keep_ref, got_ref, residual_ref, gain_ref, *outs):
        @pl.when(pl.program_id(0) == 0)
        def _():
            outs[-1][...] = jnp.zeros_like(outs[-1])

        up = keep_ref[...] + got_ref[...].astype(jnp.float32)
        source = source_ref[...].astype(jnp.float32)
        factor = head_scale(source)
        weighted = up * gain_ref[...]
        inner = jnp.mean(weighted * source, axis=-1, keepdims=True)
        total = residual_ref[...].astype(jnp.float32) + factor * weighted
        total = total - source * (factor * factor * factor) * inner
        outs[0][...] = total
        if rounded:
            outs[1][...] = total.astype(jnp.bfloat16)
        outs[-1][...] += jnp.sum(up * source * factor, axis=0, keepdims=True)

    outs = [jnp.float32] + [jnp.bfloat16] * rounded
    return norm_call(kernel, (source, keep, got, residual), gain, outs, 1, "norm_back")


def halve(keep, got):
    pairs, (r, c) = keep.shape[0] // 2, keep.shape[1:]
    tile = min(64, r)

    def kernel(keep_ref, got_ref, even_ref, odd_ref):
        even_ref[0] = keep_ref[0].astype(jnp.float32) + got_ref[0].astype(jnp.float32)
        odd_ref[0] = (keep_ref[1].astype(jnp.float32) + got_ref[1].astype(jnp.float32)).astype(jnp.bfloat16)

    two = pl.BlockSpec((2, tile, c), lambda p, i: (p, i, 0))
    one = pl.BlockSpec((1, tile, c), lambda p, i: (p, i, 0))
    return pl.pallas_call(
        kernel,
        grid=(pairs, r // tile),
        in_specs=[two, two],
        out_specs=[one, one],
        out_shape=[jax.ShapeDtypeStruct((pairs, r, c), jnp.float32), jax.ShapeDtypeStruct((pairs, r, c), jnp.bfloat16)],
        compiler_params=params(),
        cost_estimate=cost(0, 16 * pairs * r * c),
        name="halve",
    )(keep, got)


def out_terms(place, gated, upstream, n_u):
    m, q = gated.shape
    c = upstream.shape[1] // n_u

    def kernel(place_ref, x_ref, y_ref, out_ref):
        out_ref[0] = lax.dot_general(x_ref[...], y_ref[...], TN, preferred_element_type=jnp.float32).astype(jnp.bfloat16)

    return pl.pallas_call(
        kernel,
        grid_spec=pltpu.PrefetchScalarGridSpec(
            num_scalar_prefetch=1,
            grid=(n_u,),
            in_specs=[
                pl.BlockSpec((m, q), lambda k, p: (0, 0)),
                pl.BlockSpec((m, c), lambda k, p: (0, p[1] ^ k)),
            ],
            out_specs=pl.BlockSpec((1, q, c), lambda k, p: (k, 0, 0)),
        ),
        out_shape=jax.ShapeDtypeStruct((n_u, q, c), jnp.bfloat16),
        compiler_params=params(),
        cost_estimate=cost(2 * m * q * c * n_u, 2 * m * q + 4 * m * c * n_u),
        name="out_terms",
    )(place, gated, upstream)


MESH = pl.DeviceIdType.MESH


class Group:
    def __init__(self, n_dp, n_u):
        self.n_dp, self.n_u = n_dp, n_u
        index = lax.axis_index("dp")
        self.me = lax.axis_index("ulysses")
        odd = index % 2
        self.position = (1 - odd) * (index // 2) + odd * (n_dp - 1 - index // 2)
        self.next = (self.owner(1), self.owner(-1))
        self.bits = [1 << k for k in range(n_u.bit_length() - 1)]

    def owner(self, offset):
        place = (self.position + offset + self.n_dp) % self.n_dp
        late = place // (self.n_dp // 2)
        return (1 - late) * (2 * place) + late * (2 * (self.n_dp - 1 - place) + 1)

    def greet(self):
        barrier = pltpu.get_barrier_semaphore()
        for way in (0, 1):
            pl.semaphore_signal(barrier, inc=1, device_id={"dp": self.next[way]}, device_id_type=MESH)
        for other in range(1, self.n_u):
            pl.semaphore_signal(barrier, inc=1, device_id={"ulysses": self.me ^ other}, device_id_type=MESH)
        pl.semaphore_wait(barrier, 1 + self.n_u)

    def to_ring(self, way, source, target, send, recv):
        copy = pltpu.make_async_remote_copy(
            src_ref=source, dst_ref=target, send_sem=send, recv_sem=recv,
            device_id={"dp": self.next[way]}, device_id_type=MESH,
        )
        copy.start()
        return copy

    def to_cube(self, bit, source, target, send, recv):
        copy = pltpu.make_async_remote_copy(
            src_ref=source, dst_ref=target, send_sem=send, recv_sem=recv,
            device_id={"ulysses": self.me ^ bit}, device_id_type=MESH,
        )
        copy.start()
        return copy

    def reach(self, more_ahead):
        longer = self.n_dp // 2
        shorter = self.n_dp - 1 - longer
        return (longer, shorter) if more_ahead else (shorter, longer)


class Spread:
    def __init__(self, group, own, out, send, recv):
        self.group, self.own, self.out, self.send, self.recv = group, own, out, send, recv
        self.keys, self.levels, self.copies, self.used, self.waited = [0], group.bits[::-1], [], 0, 0

    def level(self):
        for copy in self.copies[self.waited :]:
            copy.wait_recv()
        self.waited = len(self.copies)
        if not self.levels:
            return False
        bit = self.levels.pop(0)
        for key in sorted(self.keys):
            source = self.own if key == 0 else self.out.at[key]
            at = self.used
            self.copies.append(
                self.group.to_cube(bit, source, self.out.at[key ^ bit], self.send.at[at], self.recv.at[at])
            )
            self.used += 1
        self.keys += [key ^ bit for key in self.keys]
        return True

    def finish(self):
        while self.level():
            pass
        for copy in self.copies:
            copy.wait_send()


class RingGather:
    def __init__(self, group, chains, send, recv):
        self.group, self.chains, self.send_sems, self.recv_sems = group, chains, send, recv
        self.copies = {}

    def place(self, c, owner):
        _, out, block, low, rows, _ = self.chains[c]
        return out.at[pl.ds(pl.multiple_of(owner * block + low, 16), rows)]

    def item(self, c):
        item, _, _, low, rows, _ = self.chains[c]
        return item.at[low : low + rows]

    def reach(self, c, way):
        return self.group.reach(self.chains[c][5])[way]

    def send(self, c, way, step):
        owner = self.group.owner(1 - step if way == 0 else step - 1)
        source = self.item(c) if step == 1 else self.place(c, owner)
        sems = (c, way, step - 1)
        self.copies[sems] = self.group.to_ring(
            way, source, self.place(c, owner), self.send_sems.at[sems], self.recv_sems.at[sems]
        )

    def start(self, c):
        for way in (0, 1):
            self.send(c, way, 1)

    def event(self, c, way, step):
        if step <= self.reach(c, way):
            self.copies[c, way, step - 1].wait_recv()
            if step < self.reach(c, way):
                self.send(c, way, step + 1)

    def finish(self):
        for copy in self.copies.values():
            copy.wait_send()


def by_rows(count, tile, function):
    def body(i, carry):
        function(pl.ds(pl.multiple_of(i * tile, tile), tile))
        return carry

    lax.fori_loop(0, count // tile, body, 0)


def forward_kernel(
    n_dp, n_u, heads, kv_heads, length_ref, tokens_ref, gain_one, gain_two, q_gain, k_gain, cosine, sine, grad_ref,
    out_item, qk_item, vg_item, gate_item, up_item, down_item,
    w_qk, w_vg, w_gate, w_up, w_down, normed_out, grad_out, second_out,
    raw_qk, raw_vg, q_out, k_out, v_out, gate_out, attended_out, gated_out, total_out, w_out, hidden_out,
    normed, own, qk_local, vg_local, columns, turned, parts, core_got, total, second_own,
    ring_send, ring_recv, cube_send, cube_recv, turn_send, turn_recv, sum_send, sum_recv, local,
):
    rows_own, width = tokens_ref.shape
    bucket = rows_own * n_u
    size = HEAD_DIMENSION
    copies = heads // kv_heads
    depth = width // n_dp
    group = Group(n_dp, n_u)
    me, mine = group.me, group.owner(0)
    group.greet()
    strip = down_item.shape[0]
    halves = 2 if strip % 32 == 0 else 1
    chains = [
        (out_item, columns, depth, 0, depth, True),
        (qk_item, w_qk, depth, 0, depth, False),
        (vg_item, w_vg, depth, 0, depth, True),
        (gate_item, w_gate, depth, 0, depth, True),
        (up_item, w_up, depth, 0, depth, False),
    ]
    for p in range(halves):
        chains.append((down_item, w_down, strip, p * strip // halves, strip // halves, p == 0))
    ring = RingGather(group, chains, ring_send, ring_recv)
    kept = []

    def keep(source, target):
        copy = pltpu.make_async_copy(source, target, local.at[len(kept)])
        copy.start()
        kept.append(copy)
        return copy

    for c in (0, 1, 2):
        ring.start(c)
    own_rows = lambda out, block: out.at[pl.ds(pl.multiple_of(mine * block, 16), block)]
    for item, out, block in (
        (out_item, columns, depth), (qk_item, w_qk, depth), (vg_item, w_vg, depth),
        (gate_item, w_gate, depth), (up_item, w_up, depth), (down_item, w_down, strip),
    ):
        keep(item, own_rows(out, block))

    def first(rows):
        x = tokens_ref[rows].astype(jnp.float32)
        own[rows] = (x * head_scale(x) * gain_one[...]).astype(jnp.bfloat16)

    by_rows(rows_own, 64, first)
    keep(own, normed.at[0]).wait()
    keep(grad_ref, grad_out.at[0])
    spreads = [
        Spread(group, own, normed, cube_send.at[0], cube_recv.at[0]),
        Spread(group, grad_ref, grad_out, cube_send.at[1], cube_recv.at[1]),
    ]
    spreads[0].level()
    longest = n_dp // 2
    for step in range(1, longest + 1):
        for c in (0, 1, 2):
            for way in (0, 1):
                ring.event(c, way, step)
        if step == 1:
            spreads[1].level()
        if step < longest:
            spreads[0 if step % 2 == 1 else 1].level()
        if step == longest - 1:
            for c in (3, 4):
                ring.start(c)
    spreads[0].finish()
    events = []
    for step in range(1, longest + 1):
        events += [[(3, 0, step), (4, 1, step)], [(4, 0, step), (3, 1, step)]]
        if step == longest - 1:
            events.append([("start",)])
    for step in range(1, longest + 1):
        if halves == 2:
            events += [[(5, 0, step), (6, 1, step)], [(6, 0, step), (5, 1, step)]]
        else:
            events += [[(5, 0, step), (5, 1, step)]]

    def pump(count=1):
        while count and events:
            pair = events.pop(0)
            if pair[0][0] == "start":
                for c in range(5, len(chains)):
                    ring.start(c)
                continue
            for event in pair:
                ring.event(*event)
            count -= 1

    for copy in kept[:3]:
        copy.wait()
    share = depth * n_dp // n_u
    turns = []
    for k in range(1, n_u):
        source = columns.at[pl.ds(pl.multiple_of((me ^ k) * share, 16), share)]
        turns.append(group.to_cube(k, source, turned.at[k], turn_send.at[k - 1], turn_recv.at[k - 1]))
    keep(columns.at[pl.ds(pl.multiple_of(me * share, 16), share)], turned.at[0]).wait()
    one, two = keep(w_qk, qk_local), keep(w_vg, vg_local)
    keep(normed, normed_out)
    one.wait()
    two.wait()

    def project(b, carry):
        x = normed[b]
        raw_qk[b] = jnp.dot(x, qk_local[...], preferred_element_type=jnp.float32)
        raw_vg[b] = jnp.dot(x, vg_local[...], preferred_element_type=jnp.float32)
        return carry

    lax.fori_loop(0, n_u, project, 0)
    pump()

    length = length_ref[0]
    block = min(256, bucket)

    def attention(h, carry):
        def column(ref, at):
            at = pl.multiple_of(at * size, size)
            return jnp.concatenate([ref[me ^ t, :, pl.ds(at, size)] for t in range(n_u)], axis=0)

        at = pl.ds(pl.multiple_of(h * size, size), size)
        kv = pl.ds(pl.multiple_of(h // copies * size, size), size)
        q = column(raw_qk, h)
        q = turn_pairs(q * head_scale(q) * q_gain[...], cosine[...], sine[...]).astype(jnp.bfloat16)
        q_out[:, at] = q
        k = column(raw_qk, heads + h // copies)
        k = turn_pairs(k * head_scale(k) * k_gain[...], cosine[...], sine[...]).astype(jnp.bfloat16)
        k_out[:, kv] = k
        v = column(raw_vg, h // copies).astype(jnp.bfloat16)
        v_out[:, kv] = v
        gate = jax.nn.sigmoid(column(raw_vg, kv_heads + h))
        gate_out[:, at] = gate
        for start in range(0, bucket, block):
            rows = slice(start, start + block)
            scores = masked_scores(q[rows], k[: start + block], start, length)
            top = jnp.max(scores, axis=-1, keepdims=True)
            soft = jnp.exp(scores - top)
            sums = jnp.sum(soft, axis=-1, keepdims=True)
            out = jnp.dot(soft.astype(jnp.bfloat16), v[: start + block], preferred_element_type=jnp.float32) / sums
            out = out.astype(jnp.bfloat16)
            attended_out[rows, at] = out
            total_out[h, rows] = top + jnp.log(sums)
            gated = (out.astype(jnp.float32) * gate[rows]).astype(jnp.bfloat16)
            for t in range(start // rows_own, (start + block) // rows_own):
                inside = slice(t * rows_own - start, (t + 1) * rows_own - start)
                gated_out[me ^ t, :, at] = gated[inside]
        return carry

    lax.fori_loop(0, heads, attention, 0)
    pump()
    for copy in turns:
        copy.wait_recv()
    c_width = columns.shape[1]
    for k in range(n_u):
        w_out[:, pl.ds(pl.multiple_of((me ^ k) * c_width, c_width), c_width)] = turned[k]

    def branch(b, carry):
        parts[b] = jnp.dot(gated_out[b], w_out[...], preferred_element_type=jnp.float32).astype(jnp.bfloat16)
        return carry

    lax.fori_loop(0, n_u, branch, 0)
    held = list(range(n_u))
    used = 0
    sums = []
    for bit in group.bits:
        keys = [key for key in held if not key & bit]
        level = []
        for key in keys:
            level.append(
                group.to_cube(bit, parts.at[key | bit], core_got.at[used], sum_send.at[used], sum_recv.at[used])
            )
            used += 1
        sums += level
        pump()
        for at, (key, copy) in enumerate(zip(keys, level)):
            copy.wait_recv()
            slot = used - len(keys) + at

            def add(rows, key=key, slot=slot):
                got = core_got[slot, rows].astype(jnp.float32)
                if key:
                    parts[key, rows] = (parts[key, rows].astype(jnp.float32) + got).astype(jnp.bfloat16)
                elif bit == 1:
                    total[rows] = tokens_ref[rows].astype(jnp.float32) + parts[0, rows].astype(jnp.float32) + got
                else:
                    total[rows] = total[rows] + got

            by_rows(rows_own, 64, add)
        held = keys

    def second(rows):
        hidden = total[rows]
        hidden_out[rows] = hidden
        second_own[rows] = (hidden * head_scale(hidden) * gain_two[...]).astype(jnp.bfloat16)

    by_rows(rows_own, 64, second)
    spread = Spread(group, second_own, second_out, cube_send.at[2], cube_recv.at[2])
    keep(second_own, second_out.at[0])
    while spread.level():
        pump(2)
    spreads[1].finish()
    spread.finish()
    pump(1000)
    ring.finish()
    for copy in turns + sums:
        copy.wait_send()
    for copy in kept[3:6] + kept[7:8] + kept[11:]:
        copy.wait()


def forward(length, tokens_own, gains, tables, grad_own, items, n_dp, n_u, heads, kv_heads):
    anywhere = pl.BlockSpec(memory_space=pl.ANY)
    local = pl.BlockSpec(memory_space=pltpu.VMEM)
    rows, width = tokens_own.shape
    bucket, size = rows * n_u, HEAD_DIMENSION
    total = (heads + kv_heads) * size
    depth = width // n_dp
    columns = items[0].shape[1]
    share = width // n_u
    longest = n_dp // 2

    def shape(*dims, dtype=jnp.bfloat16):
        return jax.ShapeDtypeStruct(dims, dtype)

    out_shape = [shape(n_dp * i.shape[0], i.shape[1]) for i in items[1:]]
    out_shape += [shape(n_u, rows, width)] * 3
    out_shape += [shape(n_u, rows, total, dtype=jnp.float32)] * 2
    out_shape += [
        shape(bucket, heads * size), shape(bucket, kv_heads * size), shape(bucket, kv_heads * size),
        shape(bucket, heads * size, dtype=jnp.float32), shape(bucket, heads * size),
        shape(n_u, rows, heads * size), shape(heads, bucket, 1, dtype=jnp.float32),
        shape(share, width), shape(rows, width, dtype=jnp.float32),
    ]
    dma = pltpu.SemaphoreType.DMA
    return pl.pallas_call(
        functools.partial(forward_kernel, n_dp, n_u, heads, kv_heads),
        in_specs=[pl.BlockSpec(memory_space=pltpu.SMEM)] + [local] * 7 + [anywhere] * 7,
        out_specs=[anywhere] * 8 + [local] * 11,
        out_shape=out_shape,
        scratch_shapes=[
            pltpu.VMEM((n_u, rows, width), jnp.bfloat16),
            pltpu.VMEM((rows, width), jnp.bfloat16),
            pltpu.VMEM((width, total), jnp.bfloat16),
            pltpu.VMEM((width, total), jnp.bfloat16),
            pltpu.VMEM((width, columns), jnp.bfloat16),
            pltpu.VMEM((n_u, share, columns), jnp.bfloat16),
            pltpu.VMEM((n_u, rows, width), jnp.bfloat16),
            pltpu.VMEM((n_u - 1, rows, width), jnp.bfloat16),
            pltpu.VMEM((rows, width), jnp.float32),
            pltpu.VMEM((rows, width), jnp.bfloat16),
            dma((7, 2, longest)), dma((7, 2, longest)), dma((3, n_u - 1)), dma((3, n_u - 1)),
            dma((n_u - 1,)), dma((n_u - 1,)), dma((n_u - 1,)), dma((n_u - 1,)), dma((13,)),
        ],
        compiler_params=pltpu.CompilerParams(vmem_limit_bytes=60 * 1024 * 1024, collective_id=0, has_side_effects=True),
        cost_estimate=cost(),
        name="forward",
    )(length, tokens_own, *gains, *tables, grad_own, *items)


def reduce_kernel(n_dp, n_u, count, blocks_ref, *refs):
    terms, outs = list(refs[: count - 1]), refs[count - 1 : 2 * count - 1]
    refs = refs[2 * count - 1 :]
    slots, sums = refs[:count], refs[count : 2 * count]
    out_terms_ref, ring_send, ring_recv, cube_send, cube_recv, turn_send, turn_recv, local = refs[2 * count :]
    terms.append(out_terms_ref)
    group = Group(n_dp, n_u)
    group.greet()
    copies = {}
    reaches = [group.reach(c % 2 == 0) for c in range(count)]
    longest = n_dp // 2
    share = blocks_ref.shape[1]
    here = out_terms_ref.at[pl.ds(pl.multiple_of(group.me * share, share), share)]

    def add(c, target, offset, others):
        r = target.shape[0]
        tile = 16
        first = group.owner(offset) * r

        def body(i, carry):
            rows = pl.ds(pl.multiple_of(i * tile, tile), tile)
            total = terms[c][pl.ds(pl.multiple_of(first + i * tile, tile), tile)].astype(jnp.float32)
            for other in others:
                total = total + other[rows].astype(jnp.float32)
            target[rows] = total.astype(jnp.bfloat16)
            return carry

        lax.fori_loop(0, r // tile, body, 0)

    def slot(c, way, step):
        return slots[c].at[way, step]

    def send(c, way, step):
        reach = reaches[c][way]
        offset = (reach - step) if way == 0 else (step - reach)
        if step == 0:
            r = sums[c].shape[0]
            source = terms[c].at[pl.ds(pl.multiple_of(group.owner(offset) * r, r), r)]
        else:
            source = slot(c, way, step - 1)
            add(c, source, offset, [source])
        sems = (c, way, step)
        copies[sems] = group.to_ring(way, source, slot(c, way, step), ring_send.at[sems], ring_recv.at[sems])

    def start(chains):
        for c in chains:
            for way in (0, 1):
                send(c, way, 0)

    phases = [(0, 1), (2, 3)]
    start(phases[0])
    turns = []
    for k in range(1, n_u):
        turns.append(group.to_cube(k, blocks_ref.at[k], here, turn_send.at[k - 1], turn_recv.at[k - 1]))
    own = pltpu.make_async_copy(blocks_ref.at[0], here, local.at[count])
    own.start()
    own.wait()
    spreads, kept = [], []
    for phase, chains in enumerate(phases):
        for step in range(longest):
            for c in chains:
                for way in (0, 1):
                    if step < reaches[c][way]:
                        copies[c, way, step].wait_recv()
                        if step + 1 < reaches[c][way]:
                            send(c, way, step + 1)
            if step == longest - 2 and phase == 0:
                for copy in turns:
                    copy.wait_recv()
                start(phases[1])
            if phase == 1 and step % 2 == 1 and step < longest - 1:
                for spread in spreads:
                    spread.level()
            if step == longest - 1:
                for c in chains:
                    add(c, sums[c], 0, [slot(c, way, reaches[c][way] - 1) for way in (0, 1)])
                    spread = Spread(group, sums[c], outs[c], cube_send.at[c], cube_recv.at[c])
                    copy = pltpu.make_async_copy(sums[c], outs[c].at[0], local.at[c])
                    copy.start()
                    kept.append(copy)
                    spread.level()
                    spreads.append(spread)
    for spread in spreads:
        spread.level()
    for spread in spreads:
        spread.finish()
    for copy in list(copies.values()) + turns:
        copy.wait_send()
    for copy in kept:
        copy.wait()


def reduce_all(blocks, terms, n_dp, n_u):
    count = len(terms) + 1
    anywhere = pl.BlockSpec(memory_space=pl.ANY)
    local = pl.BlockSpec(memory_space=pltpu.VMEM)
    longest = n_dp // 2
    whole = (blocks.shape[0] * blocks.shape[1], blocks.shape[2])
    sizes = [(r // n_dp, c) for r, c in [t.shape for t in terms] + [whole]]
    dma = pltpu.SemaphoreType.DMA
    return pl.pallas_call(
        functools.partial(reduce_kernel, n_dp, n_u, count),
        in_specs=[local] * count,
        out_specs=[anywhere] * count,
        out_shape=[jax.ShapeDtypeStruct((n_u,) + b, jnp.bfloat16) for b in sizes],
        scratch_shapes=[pltpu.VMEM((2, longest) + b, jnp.bfloat16) for b in sizes]
        + [pltpu.VMEM(b, jnp.bfloat16) for b in sizes]
        + [
            pltpu.VMEM(whole, jnp.bfloat16),
            dma((count, 2, longest)), dma((count, 2, longest)), dma((count, n_u - 1)), dma((count, n_u - 1)),
            dma((n_u - 1,)), dma((n_u - 1,)), dma((count + 1,)),
        ],
        compiler_params=pltpu.CompilerParams(vmem_limit_bytes=VMEM_LIMIT, collective_id=1, has_side_effects=True),
        cost_estimate=cost(),
        name="reduce_all",
    )(blocks, *terms)


START = 0.9
LATENCY = 2.0
RATES = {"ring": 50.0, "x": 50.0, "core": 250.0}


class Flight:
    def __init__(self, value, arrival):
        self.value, self.arrival = value, arrival


class Sequence:
    def __init__(self):
        self.last = ()
        self.now = 0.0
        self.free = {}
        self.sources = []
        self.fillers = []

    def tie(self, *values):
        tied, _ = lax.optimization_barrier((values, self.last))
        self.last = tied
        return tied

    def run(self, cost, function, *values):
        self.poll()
        out = function(*self.tie(*values))
        self.now += cost
        if isinstance(out, (tuple, list)):
            return self.tie(*out)
        return self.tie(out)[0]

    def fly(self, value, axis, pairs, link, kind):
        (value,) = self.tie(value)
        got = lax.ppermute(value, axis, pairs)
        start = max(self.now + START, self.free.get(link, 0.0))
        end = start + value.size * value.dtype.itemsize / 1000.0 / RATES[kind]
        self.free[link] = end
        self.now += START
        return Flight(got, end + LATENCY)

    def land(self, *flights):
        self.idle(max(f.arrival for f in flights))
        return self.tie(*[f.value for f in flights])

    def poll(self):
        moved = True
        while moved:
            moved = any([source.poll(self.now) for source in self.sources])

    def later(self, cost, ready, function):
        self.fillers.append((cost, ready, function))

    def fill(self):
        for at, (cost, ready, function) in enumerate(self.fillers):
            if ready():
                self.fillers.pop(at)
                function()
                return True
        return False

    def idle(self, until):
        while True:
            self.poll()
            if self.now >= until:
                return
            if until - self.now > 2.0 and self.fill():
                continue
            events = [e for source in self.sources for e in [source.next()] if e is not None]
            self.now = max(self.now, min(events + [until]))

    def drain(self, done):
        while not done():
            self.poll()
            if done():
                return
            if self.fill():
                continue
            events = [e for source in self.sources for e in [source.next()] if e is not None]
            assert events
            self.now = max(self.now, min(events))


def pick(value, index):
    return lax.dynamic_index_in_dim(value, index, 0, keepdims=False, allow_negative_indices=False)


class Cube:
    def __init__(self, axis, seq):
        self.axis = axis
        self.seq = seq
        self.count = lax.axis_size(axis)
        self.me = lax.axis_index(axis)
        bits = []
        bit = 1
        while bit < self.count:
            bits.append(bit)
            bit *= 2
        self.bits = bits

    def swap(self, value, bit):
        kind = "core" if bit == 1 else "x"
        return self.seq.fly(value, self.axis, [(i, i ^ bit) for i in range(self.count)], kind, kind)

    def gather(self, item):
        keys, blocks = [[0]], [item[None]]
        for bit in self.bits[::-1]:
            order = sorted((key, at, sub) for at, ks in enumerate(keys) for sub, key in enumerate(ks))
            if len(order) > 1:
                sent = self.seq.run(
                    2.0, lambda *b: jnp.concatenate([b[at][sub : sub + 1] for _, at, sub in order]), *blocks
                )
            else:
                sent = blocks[0]
            (got,) = yield [self.swap(sent, bit)]
            keys = keys + [[key ^ bit for key, _, _ in order]]
            blocks = blocks + [got]
        return (keys, blocks)

    def joined(self, held):
        keys, blocks = held
        order = sorted((key, at, sub) for at, ks in enumerate(keys) for sub, key in enumerate(ks))
        return self.seq.run(3.0, lambda *b: jnp.concatenate([b[at][sub : sub + 1] for _, at, sub in order]), *blocks)

    def reduce(self, keep, send):
        for bit in self.bits:
            (got,) = yield [self.swap(send, bit)]
            if bit != self.bits[-1]:
                keep, send = self.seq.run(4.4, halve, keep, got)
        return (keep[0], got[0])

    def turn(self, blocks):
        got = yield [self.swap(blocks[bit], bit) for bit in range(1, self.count)]
        return [blocks[0]] + list(got)

    def total(self, value, axes):
        for axis in axes:
            count = lax.axis_size(axis)
            bit = 1
            while bit < count:
                pairs = [(i, i ^ bit) for i in range(count)]
                (got,) = yield [self.seq.fly(value, axis, pairs, "sum", "ring")]
                value = self.seq.run(1.0, lambda a, b: a + b, value, got)
                bit *= 2
        return value


class Task:
    def __init__(self, seq, generator, urgent=True):
        self.seq, self.generator = seq, generator
        self.value, self.flights, self.over, self.busy = None, None, False, False
        seq.sources.append(self)
        self.go(None)

    def go(self, values):
        self.busy = True
        try:
            self.flights = self.generator.send(values)
        except StopIteration as stop:
            self.value, self.over = stop.value, True
            self.seq.sources.remove(self)
        self.busy = False

    def next(self):
        return None if self.busy or self.over else max(f.arrival for f in self.flights)

    def poll(self, now):
        if self.busy or self.over or self.next() > now + 0.5:
            return False
        self.go(self.seq.tie(*[f.value for f in self.flights]))
        return True

    def finish(self):
        while not self.over:
            if self.busy:
                raise RuntimeError
            self.seq.idle(self.next())
        return self.value


def dot(a, b):
    return jnp.einsum("mk,kn->mn", a, b, preferred_element_type=jnp.float32)


def dot_nt(a, b):
    return jnp.einsum("mk,nk->mn", a, b, preferred_element_type=jnp.float32)


def dot_tn(a, b):
    return jnp.einsum("km,kn->mn", a, b, preferred_element_type=jnp.float32)


def low(value):
    return value.astype(jnp.bfloat16)


def high(value):
    return value.astype(jnp.float32)


def shards(
    tokens,
    seq_lengths,
    cotangent,
    norm1_gain,
    input_weight,
    query_gain,
    key_gain,
    output_weight,
    norm2_gain,
    perceptron_input_weight,
    down_weight,
):
    _, rows, width = tokens.shape
    seq = Sequence()
    cube = Cube("ulysses", seq)
    n_dp = lax.axis_size("dp")
    n_u, me = cube.count, cube.me
    bucket = rows * n_u
    depth = width // n_dp
    heads = QUERY_HEADS // n_u
    kv_heads = KEY_VALUE_HEADS // n_u
    copies = QUERY_HEADS // KEY_VALUE_HEADS
    head_width = HEAD_DIMENSION
    q_w, kv_w = heads * head_width, kv_heads * head_width
    query_width = QUERY_HEADS * head_width
    kv_all = KEY_VALUE_HEADS * head_width
    ff_strip = FF // n_dp // n_u
    ff_local = FF // n_u
    half = width // 2
    out_cols = width // n_u
    place = jnp.stack([seq_lengths[0], me])
    length = seq_lengths[0]
    q_gain, k_gain = query_gain[None], key_gain[None]
    gain_one, gain_two = norm1_gain[None], norm2_gain[None]
    positions = me * rows + jnp.arange(rows)
    def cut(value, start, size):
        return lax.dynamic_slice_in_dim(value, start, size, 1)

    def task(generator):
        return Task(seq, generator)

    frequency = np.float32(ROPE_BASE) ** (np.float32(-2.0) * np.arange(head_width // 2, dtype=np.float32) / head_width)
    angles = np.arange(bucket, dtype=np.float32)[:, None] * frequency.astype(np.float32)[None, :]
    cosine, sine = np.cos(angles), np.sin(angles)
    tables = (
        jnp.asarray(np.concatenate([cosine, cosine], axis=1), jnp.float32),
        jnp.asarray(np.concatenate([-sine, sine], axis=1), jnp.float32),
    )

    gate_item, up_item = seq.run(
        4.9, lambda p, w: take_strips(p, w, n_dp, n_u, ff_strip), place, perceptron_input_weight
    )
    out_item, qk_item, vg_item, grad_own, down_item = seq.run(
        3.0,
        lambda o, w, c, d: (
            cut(o, me * out_cols, out_cols),
            jnp.concatenate([cut(w, me * q_w, q_w), cut(w, query_width + me * kv_w, kv_w)], axis=1),
            jnp.concatenate(
                [
                    cut(w, query_width + kv_all + me * kv_w, kv_w),
                    cut(w, query_width + 2 * kv_all + me * q_w, q_w),
                ],
                axis=1,
            ),
            jnp.where((positions < length)[:, None], c, jnp.zeros_like(c)),
            lax.dynamic_slice_in_dim(d, me * ff_strip, ff_strip, 0),
        ),
        output_weight,
        input_weight,
        cotangent[0],
        down_weight,
    )
    (
        w_qk, w_vg, w_gate, w_up, w_down, normed, grad_result, second,
        raw_qk, raw_vg, queries, keys, values, gate, attended, gated, log_totals, w_out, hidden_in,
    ) = seq.run(
        250.0,
        lambda t, g, *items: forward(
            seq_lengths, t, (gain_one, gain_two, q_gain, k_gain), tables, g, items, n_dp, n_u, heads, kv_heads
        ),
        tokens[0], grad_own, out_item, qk_item, vg_item, gate_item, up_item, down_item,
    )
    normed, grad_result = normed.reshape(bucket, width), grad_result.reshape(bucket, width)
    second, gated = second.reshape(bucket, width), gated.reshape(bucket, q_w)

    def even_odd(value):
        value = low(value).reshape(n_u, rows, width)
        return (value[0::2], value[1::2])

    act_gate, act_up, hidden = seq.run(20.0, gate_up, second, w_gate, w_up)
    down_own = lax.psum_scatter(
        seq.run(10.7, lambda h, g: low(dot_tn(h, g)), hidden, grad_result), "dp", scatter_dimension=0, tiled=True
    )

    grad_gate, grad_up = seq.run(15.5, down_back, grad_result, act_gate, act_up, w_down)
    up_own = lax.psum_scatter(
        seq.run(12.5, lambda a, b: outer_terms(a, b, n_dp), second, grad_up), "dp", scatter_dimension=0, tiled=True
    )

    def input_grads(a, b, first, second):
        return back_matmul(a, b, first, second, rows)

    two_keep, two_send = seq.run(20.5, input_grads, grad_gate, grad_up, w_gate, w_up)
    t_two = task(cube.reduce(two_keep, two_send))
    gate_terms = seq.run(12.5, lambda a, b: outer_terms(a, b, n_dp), second, grad_gate)
    down_keep, down_send = seq.run(11.5, lambda h, w: even_odd(dot(h, w)), hidden, w_down)
    grad_hidden_in, branch_own, gain_two_own = seq.run(
        5.8, lambda *a: norm_back(*a, True), hidden_in, *t_two.finish(), grad_own, gain_two
    )
    t_branch_grad = task(cube.gather(branch_own))
    branch_grad = cube.joined(t_branch_grad.finish()).reshape(bucket, width)

    grad_gated = seq.run(3.8, dot_nt, branch_grad, w_out)
    t_down = task(cube.reduce(down_keep, down_send))
    t_down_all = task(cube.gather(seq.tie(down_own)[0]))
    grad_qk, grad_vg, gain_query_own, gain_key_own = seq.run(
        20.0,
        attend_back,
        place, raw_qk, queries, keys, values, gate, attended, grad_gated.reshape(n_u, rows, q_w), log_totals,
        q_gain, k_gain, *tables,
    )
    grad_qk, grad_vg = grad_qk.reshape(bucket, -1), grad_vg.reshape(bucket, -1)
    one_keep, one_send = seq.run(12.0, input_grads, grad_qk, grad_vg, w_qk, w_vg)
    t_one = task(cube.reduce(one_keep, one_send))
    out_parts = seq.run(7.0, lambda p, a, b: out_terms(p, a, b, n_u), place, gated, branch_grad)
    qk_terms = seq.run(9.3, lambda a, b: outer_terms(a, b, n_dp), normed, grad_qk)
    vg_terms = seq.run(9.3, lambda a, b: outer_terms(a, b, n_dp), normed, grad_vg)

    gate_all, qk_all, vg_all, out_all = seq.run(
        150.0, lambda b, *t: reduce_all(b, t, n_dp, n_u), out_parts, gate_terms, qk_terms, vg_terms
    )
    t_up_all = task(cube.gather(seq.tie(up_own)[0]))
    tokens_grad, gain_one_own = seq.run(
        5.6, lambda *a: norm_back(*a, False), tokens[0], *t_one.finish(), grad_hidden_in, gain_one
    )
    gains = seq.run(
        1.0, lambda *g: jnp.concatenate(g, axis=1)[0], gain_one_own, gain_query_own, gain_key_own, gain_two_own
    )
    t_gains = task(cube.total(gains, ("ulysses", "dp")))
    keys_all = [list(range(n_u))]
    in_all = seq.run(
        5.5,
        lambda p, a, b: put_columns(
            p, [(keys_all, [a]), (keys_all, [b])], [[(0, q_w), (q_w, kv_w)], [(0, kv_w), (kv_w, q_w)]]
        ),
        place, qk_all, vg_all,
    )
    out_all = seq.run(4.0, lambda p, a: put_columns(p, [(keys_all, [a])], [[(0, out_cols)]]), place, out_all)
    down_held = t_down_all.finish()
    down_all = seq.run(5.3, lambda p, *b: put_rows(p, (down_held[0], b)), place, *down_held[1])
    up_held = t_up_all.finish()
    mlp_all = seq.run(
        10.0, lambda p, a, *b: put_strips(p, [(keys_all, [a]), (up_held[0], b)], n_dp, ff_strip), place, gate_all, *up_held[1]
    )
    layer_out = seq.run(2.2, lambda a, b, c: a + high(b) + high(c), hidden_in, *t_down.finish())
    gains = t_gains.finish()

    gain_one_sum = gains[:width]
    gain_query_sum = gains[width : width + head_width]
    gain_key_sum = gains[width + head_width : width + 2 * head_width]
    gain_two_sum = gains[width + 2 * head_width :]
    return (
        layer_out[None],
        tokens_grad[None],
        gain_one_sum,
        in_all,
        gain_query_sum,
        gain_key_sum,
        out_all,
        gain_two_sum,
        mlp_all,
        down_all,
    )


def solution(mesh):
    placed = (
        P("dp", "ulysses", None),
        P("dp"),
        P("dp", "ulysses", None),
        P(),
        P("dp", None),
        P(),
        P(),
        P("dp", None),
        P(),
        P("dp", None),
        P("dp", None),
    )
    return jax.shard_map(
        shards,
        mesh=mesh,
        in_specs=placed,
        out_specs=(
            P("dp", "ulysses", None),
            P("dp", "ulysses", None),
            P(),
            P("dp", None),
            P(),
            P(),
            P("dp", None),
            P(),
            P("dp", None),
            P("dp", None),
        ),
        check_vma=False,
    )
```

time: 4140 us -> 789 us (0.19)
  waiting for transfers between devices: 3690 us -> 55.1 us
  Pallas kernels: 0 us -> 647 us
  matrix products: 221 us -> 22.5 us
  other arithmetic: 62.2 us -> 9.86 us
  local copies, waits for them, and re-layouts: 61.5 us -> 13 us
    all_gather x4 -> x0, waiting for transfers between devices: 1900 us -> none  [the longest x1 946 us: shards(): lax.all_gather(perceptron_input_weight, 'dp', axis=0, tiled=True)]
    unnamed x10 -> x2, waiting for transfers between devices: 796 us -> 0.03 us
    reduce_scatter x3 -> x2, waiting for transfers between devices: 786 us -> 0.02 us  [the longest x1 0.02 us: shards(): lax.psum_scatter(seq.run(12.5, lambda a, b: outer_terms(a, b, n_dp), seco...]
    pallas_call x0 -> x22, Pallas kernels: none -> 647 us  [the longest x1 274 us: forward(): pl.pallas_call(functools.partial(forward_kernel, n_dp, n_u, heads, kv_hea...]
    dot_general x24 -> x3, matrix products: 221 us -> 22.5 us  [the longest x1 10.5 us: dot_tn(): return jnp.einsum('km,kn->mn', a, b, preferred_element_type=jnp.float32)]
    psum x1 -> x0, waiting for transfers between devices: 168 us -> none  [shards(): lax.psum(in_grad, 'ulysses').astype(jnp.float32)]
    ppermute x0 -> x17, waiting for transfers between devices: none -> 55.1 us  [fly(): got = lax.ppermute(value, axis, pairs)]
    all_to_all x8 -> x0, waiting for transfers between devices: 44.2 us -> none  [the longest x1 14.2 us: shards(): lax.all_to_all(head_out.astype(jnp.bfloat16), 'ulysses', split_axis=1, co...]
  transfers between devices with their start and end apart: 17 -> 19, of which waited for: 15 -> 8; matrix products, arithmetic and copies ran while one was open for 7% -> 2% of each run, Pallas kernels for 0% -> 45%
where the time goes in v1:
time: 789 us; the launch traced here: 778 us
  Pallas kernels  647 us (82%)
  waiting for transfers between devices  55.1 us (7%)
  matrix products  22.5 us (3%)
  starting transfers between devices  15.6 us (2%)
  between operations  15.6 us (2%)
  local copies, waits for them, and re-layouts  13 us (2%)
  other arithmetic  9.86 us (1%)
    pallas_call x1, Pallas kernels, forward(): pl.pallas_call(functools.partial(forward_kernel, n_dp, n_u, heads, kv_hea...  274 us
    pallas_call x1, Pallas kernels, reduce_all(): pl.pallas_call(functools.partial(reduce_kernel, n_dp, n_u, count), in_spe...  184 us
    ppermute x17, waiting for transfers between devices, fly(): got = lax.ppermute(value, axis, pairs)  55.1 us
    pallas_call x4, Pallas kernels, outer_terms(): pl.pallas_call(kernel, grid=(count,), in_specs=[pl.BlockSpec((m, depth),...  43 us
    pallas_call x2, Pallas kernels, back_matmul(): pl.pallas_call(kernel, grid=(m // rows // 2,), in_specs=[step, step, stea...  32.2 us
    pallas_call x4, Pallas kernels, put_call(): pl.pallas_call(body, grid=(grid,), in_specs=[pl.BlockSpec(memory_space=pl...  23.5 us
    pallas_call x1, Pallas kernels, attend_back(): pl.pallas_call(functools.partial(attend_back_kernel, min(256, bucket), co...  19.7 us
    pallas_call x1, Pallas kernels, gate_up(): pl.pallas_call(kernel, grid=(n // tile,), in_specs=[steady((m, width)), w...  19 us
  transfers between devices with their start and end apart: 19, of which 8 were waited for; matrix products, arithmetic and copies ran while one was open for 2% of the time, Pallas kernels for 45%

profile of v1, /device:TPU:0, one launch (start us, length us, event | category | flops | bytes accessed | tf_op | source)
XLA Modules:
  0.0 778.2 jit_solution(17134870050973469948)
XLA Ops:
  8.7 4.8 take_strips.1
  20.0 273.7 %forward.1 = (bf16[2048,768]{1,0:T(8,128)(2,1)}, bf16[2048,768]{1,0:T(8,128)(2,1)}, bf16[2048,1536]{1,0:T(8,128)(2,1)}, bf16[2048,1536]{1,0:T(8,128)(2,1)}, bf16...) custom-call(s32[1]{0:T(128)} %copy.23.length_ref, ...), custom_call_target="tpu_custom_call" | custom-call | flops 1 | bytes 1 | tf_op jit(solution)/shard_map/forward/pallas_call | solution.py:842
  293.7 19.0 %gate_up.1 = (f32[1024,1536]{1,0:T(8,128)}, f32[1024,1536]{1,0:T(8,128)}, bf16[1024,1536]{1,0:T(8,128)(2,1)}) custom-call(bf16[1024,2048]{1,0:T(8,128)(2,1)} %bitcast.35, bf16[2048,1536]{1,0:T(8,128)(2,1)} %get-tuple-element.371.first_ref, bf16[2048,1536]{1,0:T(8,128)(2,1)} %get-tuple-element.372.second_ref), custom_call_target="tpu_custom_call" | custom-call | flops 1 | bytes 1 | tf_op jit(solution)/shard_map/gate_up/pallas_call | solution.py:191
  312.7 10.5 %convolution_convert_fusion = bf16[1536,2048]{1,0:T(8,128)(2,1)} fusion(bf16[1024,1536]{1,0:T(8,128)(2,1)} %get-tuple-element.389, bf16[1024,2048]{1,0:T(8,128)(2,1)S(1)} %bitcast.50), kind=kOutput, calls=%fused_computation | convolution fusion | flops 6445596672 | bytes 13631488 | tf_op jit(solution)/shard_map/km,kn->mn/dot_general | solution.py:1173
  323.4 15.3 %down_back.1 = (bf16[1024,1536]{1,0:T(8,128)(2,1)}, bf16[1024,1536]{1,0:T(8,128)(2,1)}) custom-call(bf16[1024,2048]{1,0:T(8,128)(2,1)} %bitcast.49, f32[1024,1536]{1,0:T(8,128)} %get-tuple-element.359.a_ref, f32[1024,1536]{1,0:T(8,128)} %get-tuple-element.360.b_ref, bf16[1536,2048]{1,0:T(8,128)(2,1)} %get-tuple-element.390.weight_ref), custom_call_target="tpu_custom_call" | custom-call | flops 1 | bytes 1 | tf_op jit(solution)/shard_map/down_back/pallas_call | solution.py:266
  338.8 12.1 %outer_terms.4 = bf16[2048,1536]{1,0:T(8,128)(2,1)} custom-call(bf16[1024,2048]{1,0:T(8,128)(2,1)} %bitcast.36, bf16[1024,1536]{1,0:T(8,128)(2,1)} %get-tuple-element.370.y_ref.b_ref), custom_call_target="tpu_custom_call" | custom-call | flops 1 | bytes 1 | tf_op jit(solution)/shard_map/outer_terms/pallas_call | solution.py:240
  350.9 20.5 %back_matmul.2 = (bf16[2,256,2048]{2,1,0:T(8,128)(2,1)}, bf16[2,256,2048]{2,1,0:T(8,128)(2,1)}) custom-call(bf16[1024,1536]{1,0:T(8,128)(2,1)} %get-tuple-element.379.a_ref.y_ref, bf16[1024,1536]{1,0:T(8,128)(2,1)} %get-tuple-element.370.y_ref.b_ref, bf16[2048,1536]{1,0:T(8,128)(2,1)} %get-tuple-element.371.first_ref, ...), custom_call_target="tpu_custom_call" | custom-call | flops 1 | bytes 1 | tf_op jit(solution)/shard_map/back_matmul/pallas_call | solution.py:220
  371.5 12.4 %outer_terms.5.refs_0_ = bf16[2048,1536]{1,0:T(8,128)(2,1)} custom-call(bf16[1024,2048]{1,0:T(8,128)(2,1)} %bitcast.37, bf16[1024,1536]{1,0:T(8,128)(2,1)} %get-tuple-element.379.a_ref.y_ref), custom_call_target="tpu_custom_call" | custom-call | flops 1 | bytes 1 | tf_op jit(solution)/shard_map/outer_terms/pallas_call | solution.py:240
  389.2 8.3 %convolution_convert_fusion.1 = bf16[1024,2048]{1,0:T(8,128)(2,1)S(1)} fusion(bf16[1024,1536]{1,0:T(8,128)(2,1)} %get-tuple-element.389, bf16[1536,2048]{1,0:T(8,128)(2,1)S(1)} %bitcast.43), kind=kOutput, calls=%fused_computation.2 | convolution fusion | flops 6444548096 | bytes 13631488 | tf_op jit(solution)/shard_map/mk,kn->mn/dot_general | solution.py:1165
  400.0 14.0 %collective-permute-done.1 = bf16[1,256,2048]{2,1,0:T(8,128)(2,1)S(1)} collective-permute-done((bf16[1,256,2048]{2,1,0:T(8,128)(2,1)}, bf16[1,256,2048]{2,1,0:T(8,128)(2,1)S(1)}, u32[]{:S(2)}, u32[]{:S(2)}) %collective-permute-start.1) | collective-permute-done | bytes 1048608 | tf_op jit(solution)/shard_map/ppermute | solution.py:1018
  415.0 5.7 norm_back.2
  421.5 24.1 %collective-permute-done.2 = bf16[1,256,2048]{2,1,0:T(8,128)(2,1)S(1)} collective-permute-done((bf16[1,256,2048]{2,1,0:T(8,128)(2,1)}, bf16[1,256,2048]{2,1,0:T(8,128)(2,1)S(1)}, u32[]{:S(2)}, u32[]{:S(2)}) %collective-permute-start.2) | collective-permute-done | bytes 1048608 | tf_op jit(solution)/shard_map/ppermute | solution.py:1018
  458.5 19.7 %attention_back.1 = (bf16[4,256,768]{2,1,0:T(8,128)(2,1)}, bf16[4,256,768]{2,1,0:T(8,128)(2,1)}, f32[1,128]{1,0:T(1,128)}, f32[1,128]{1,0:T(1,128)}) custom-call(s32[2]{0:T(128)} %pad_add_fusion.place_ref, f32[4,256,768]{2,1,0:T(8,128)} %get-tuple-element.422.q_raw.k_raw, f32[4,256,768]{2,1,0:T(8,128)} %get-tuple-element.422.q_raw.k_raw, ...), custom_call_target="tpu_custom_call" | custom-call | flops 1 | bytes 1 | tf_op jit(solution)/shard_map/attention_back/pallas_call | solution.py:136
  483.1 11.6 %back_matmul.3 = (bf16[2,256,2048]{2,1,0:T(8,128)(2,1)}, bf16[2,256,2048]{2,1,0:T(8,128)(2,1)}) custom-call(bf16[1024,768]{1,0:T(8,128)(2,1)} %bitcast.46, bf16[1024,768]{1,0:T(8,128)(2,1)} %bitcast.44, bf16[2048,768]{1,0:T(8,128)(2,1)} %get-tuple-element.456.first_ref, bf16[2048,768]{1,0:T(8,128)(2,1)} %get-tuple-element.457.second_ref), custom_call_target="tpu_custom_call" | custom-call | flops 1 | bytes 1 | tf_op jit(solution)/shard_map/back_matmul/pallas_call | solution.py:220
  495.5 5.5 collective-permute-done.7.refs_2_
  501.0 7.2 out_terms.1.blocks_ref
  508.2 9.2 %outer_terms.6.refs_1_ = bf16[2048,768]{1,0:T(8,128)(2,1)} custom-call(bf16[1024,2048]{1,0:T(8,128)(2,1)} %bitcast.38, bf16[1024,768]{1,0:T(8,128)(2,1)} %bitcast.47), custom_call_target="tpu_custom_call" | custom-call | flops 1 | bytes 1 | tf_op jit(solution)/shard_map/outer_terms/pallas_call | solution.py:240
  526.6 9.2 %outer_terms.7.refs_2_ = bf16[2048,768]{1,0:T(8,128)(2,1)} custom-call(bf16[1024,2048]{1,0:T(8,128)(2,1)} %bitcast.39, bf16[1024,768]{1,0:T(8,128)(2,1)} %bitcast.45), custom_call_target="tpu_custom_call" | custom-call | flops 1 | bytes 1 | tf_op jit(solution)/shard_map/outer_terms/pallas_call | solution.py:240
  535.8 184.0 %reduce_all.1 = (bf16[4,256,1536]{2,1,0:T(8,128)(2,1)}, bf16[4,256,768]{2,1,0:T(8,128)(2,1)}, bf16[4,256,768]{2,1,0:T(8,128)(2,1)}, bf16[4,256,512]{2,1,0:T(8,128)(2,1)}) custom-call(bf16[4,512,512]{2,1,0:T(8,128)(2,1)} %out_terms.1.blocks_ref, bf16[2048,1536]{1,0:T(8,128)(2,1)} %outer_terms.5.refs_0_, bf16[2048,768]{1,0:T(8,128)(2,1)} %outer_terms.6.refs_1_, ...), custom_call_target="tpu_custom_call" | custom-call | flops 1 | bytes 1 | tf_op jit(solution)/shard_map/reduce_all/pallas_call | solution.py:967
  722.4 5.2 norm_back.3
  728.6 5.1 put_columns.2
  740.6 4.8 collective-permute-start.13
  748.7 5.3 put_rows.1
  757.0 9.5 %put_strips.1 = f32[256,12288]{1,0:T(8,128)} custom-call(s32[2]{0:T(128)} %pad_add_fusion.place_ref, bf16[4,256,1536]{2,1,0:T(8,128)(2,1)} %get-tuple-element.551.refs_0_, bf16[1,256,1536]{2,1,0:T(8,128)(2,1)} %bitcast.57, bf16[1,256,1536]{2,1,0:T(8,128)(2,1)} %copy-done.7, bf16[2,256,1536]{2,1,0:T(8,128)(2,1)} %copy-done.13), custom_call_target="tpu_custom_call" | custom-call | flops 1 | bytes 1 | tf_op jit(solution)/shard_map/put_strips/pallas_call | solution.py:322
  (113 shorter events, 66.0 us)
Async XLA Ops:
  7.2 449.7 %reduce-scatter.3.cloned.1.call-start = ((), (), s32[]{:S(2)}) async-start(), calls=%async_computation.2 | async-start | bytes 7077888 | tf_op jit(solution)/shard_map/reduce_scatter | solution.py:1275
  293.6 19.0 %copy-start.4 = (bf16[4,256,2048]{2,1,0:T(8,128)(2,1)S(1)}, bf16[4,256,2048]{2,1,0:T(8,128)(2,1)}, u32[]{:S(2)}) copy-start(bf16[4,256,2048]{2,1,0:T(8,128)(2,1)} %get-tuple-element.336) | copy-start | bytes 12582916
  323.2 396.6 %reduce-scatter.5.cloned.1.call-start = ((), (), s32[]{:S(2)}) async-start(), calls=%async_computation.3 | async-start | bytes 7077888 | tf_op jit(solution)/shard_map/reduce_scatter | solution.py:1280
  371.4 12.5 %collective-permute-start = (bf16[2,256,2048]{2,1,0:T(8,128)(2,1)}, bf16[2,256,2048]{2,1,0:T(8,128)(2,1)}, u32[]{:S(2)}, u32[]{:S(2)}) collective-permute-start(bf16[2,256,2048]{2,1,0:T(8,128)(2,1)} %get-tuple-element.377), channel_id=1, source_target_pairs={{0,1},{1,0},{2,3},{3,2},{4,5},{5,4},{6,7},{7,6},{8,9},{9,8},{10,11... | collective-permute-start | bytes 6291464 | tf_op jit(solution)/shard_map/ppermute | solution.py:1018
  371.4 17.7 %slice-start = ((s8[6291456]{0:T(1024)(128)(4,1)}), s8[2097152]{0:T(1024)(128)(4,1)S(1)}, s32[]{:S(2)}) async-start(s8[6291456]{0:T(1024)(128)(4,1)} %bitcast.42), calls=%async_computation.4 | async-start | bytes 4194304
  371.5 17.7 %slice-start.1 = ((s8[6291456]{0:T(1024)(128)(4,1)}), s8[4194304]{0:T(1024)(128)(4,1)S(1)}, s32[]{:S(2)}) async-start(s8[6291456]{0:T(1024)(128)(4,1)} %bitcast.42), calls=%async_computation.5 | async-start | bytes 8388608
  388.3 25.7 %collective-permute-start.1 = (bf16[1,256,2048]{2,1,0:T(8,128)(2,1)}, bf16[1,256,2048]{2,1,0:T(8,128)(2,1)S(1)}, u32[]{:S(2)}, u32[]{:S(2)}) collective-permute-start(bf16[1,256,2048]{2,1,0:T(8,128)(2,1)} %get-tuple-element.388), channel_id=1, source_target_pairs={{0,2},{1,3},{2,0},{3,1},{4,6},{5,7},{6,4},{7,5},{8,10},{9,11},{10,... | collective-permute-start | bytes 3145736 | tf_op jit(solution)/shard_map/ppermute | solution.py:1018
  420.6 24.9 %collective-permute-start.2 = (bf16[1,256,2048]{2,1,0:T(8,128)(2,1)}, bf16[1,256,2048]{2,1,0:T(8,128)(2,1)S(1)}, u32[]{:S(2)}, u32[]{:S(2)}) collective-permute-start(bf16[1,256,2048]{2,1,0:T(8,128)(2,1)} %bitcast.53), channel_id=1, source_target_pairs={{0,2},{1,3},{2,0},{3,1},{4,6},{5,7},{6,4},{7,5},{8,10},{9,11},{10,... | collective-permute-start | bytes 3145736 | tf_op jit(solution)/shard_map/ppermute | solution.py:1018
  447.0 4.2 collective-permute-start.3
  456.7 21.4 %collective-permute-start.4 = (bf16[2,256,2048]{2,1,0:T(8,128)(2,1)}, bf16[2,256,2048]{2,1,0:T(8,128)(2,1)}, u32[]{:S(2)}, u32[]{:S(2)}) collective-permute-start(bf16[2,256,2048]{2,1,0:T(8,128)(2,1)} %get-tuple-element.418), channel_id=1, source_target_pairs={{0,1},{1,0},{2,3},{3,2},{4,5},{5,4},{6,7},{7,6},{8,9},{9,8},{10,11... | collective-permute-start | bytes 6291464 | tf_op jit(solution)/shard_map/ppermute | solution.py:1018
  456.9 21.3 %collective-permute-start.5 = (bf16[1,192,2048]{2,1,0:T(8,128)(2,1)}, bf16[1,192,2048]{2,1,0:T(8,128)(2,1)S(1)}, u32[]{:S(2)}, u32[]{:S(2)}) collective-permute-start(bf16[1,192,2048]{2,1,0:T(8,128)(2,1)} %bitcast.59), channel_id=1, source_target_pairs={{0,2},{1,3},{2,0},{3,1},{4,6},{5,7},{6,4},{7,5},{8,10},{9,11},{10,... | collective-permute-start | bytes 2359304 | tf_op jit(solution)/shard_map/ppermute | solution.py:1018
  458.4 19.7 %copy-start.8 = (bf16[192,2048]{1,0:T(8,128)(2,1)S(1)}, bf16[192,2048]{1,0:T(8,128)(2,1)}, u32[]{:S(2)}) copy-start(bf16[192,2048]{1,0:T(8,128)(2,1)} %reduce-scatter.3.cloned.1.call-done) | copy-start | bytes 2359300
  494.7 25.7 %collective-permute-start.8 = (bf16[2,256,2048]{2,1,0:T(8,128)(2,1)}, bf16[2,256,2048]{2,1,0:T(8,128)(2,1)S(1)}, u32[]{:S(2)}, u32[]{:S(2)}) collective-permute-start(bf16[2,256,2048]{2,1,0:T(8,128)(2,1)} %get-tuple-element.462), channel_id=1, source_target_pairs={{0,1},{1,0},{2,3},{3,2},{4,5},{5,4},{6,7},{7,6},{8,9},{9,8},{10,11... | collective-permute-start | bytes 6291464 | tf_op jit(solution)/shard_map/ppermute | solution.py:1018
  494.7 6.3 collective-permute-start.7
  495.2 25.2 %collective-permute-start.6 = (bf16[1,256,2048]{2,1,0:T(8,128)(2,1)S(1)}, bf16[1,256,2048]{2,1,0:T(8,128)(2,1)}, u32[]{:S(2)}, u32[]{:S(2)}) collective-permute-start(bf16[1,256,2048]{2,1,0:T(8,128)(2,1)S(1)} %copy-done.21), channel_id=1, source_target_pairs={{0,2},{1,3},{2,0},{3,1},{4,6},{5,7},{6,4},{7,5},{8,10},{9,11},{10,... | collective-permute-start | bytes 3145736 | tf_op jit(solution)/shard_map/ppermute | solution.py:1018
  526.2 195.2 %collective-permute-start.9 = (bf16[1,256,2048]{2,1,0:T(8,128)(2,1)}, bf16[1,256,2048]{2,1,0:T(8,128)(2,1)S(1)}, u32[]{:S(2)}, u32[]{:S(2)}) collective-permute-start(bf16[1,256,2048]{2,1,0:T(8,128)(2,1)} %get-tuple-element.479), channel_id=1, source_target_pairs={{0,2},{1,3},{2,0},{3,1},{4,6},{5,7},{6,4},{7,5},{8,10},{9,11},{10,... | collective-permute-start | bytes 3145736 | tf_op jit(solution)/shard_map/ppermute | solution.py:1018
  719.9 20.3 %collective-permute-start.12 = (bf16[1,256,1536]{2,1,0:T(8,128)(2,1)}, bf16[1,256,1536]{2,1,0:T(8,128)(2,1)S(1)}, u32[]{:S(2)}, u32[]{:S(2)}) collective-permute-start(bf16[1,256,1536]{2,1,0:T(8,128)(2,1)} %bitcast.56), channel_id=1, source_target_pairs={{0,2},{1,3},{2,0},{3,1},{4,6},{5,7},{6,4},{7,5},{8,10},{9,11},{10,... | collective-permute-start | bytes 2359304 | tf_op jit(solution)/shard_map/ppermute | solution.py:1018
  728.4 5.3 collective-permute-start.10
  733.7 6.7 collective-permute-start.11
  740.2 13.8 %copy-start.7 = (bf16[1,256,1536]{2,1,0:T(8,128)(2,1)}, bf16[1,256,1536]{2,1,0:T(8,128)(2,1)S(1)}, u32[]{:S(2)}) copy-start(bf16[1,256,1536]{2,1,0:T(8,128)(2,1)S(1)} %collective-permute-done.12.refs_2_) | copy-start | bytes 2359300
  740.6 15.3 %collective-permute-start.16 = (bf16[2,256,1536]{2,1,0:T(8,128)(2,1)S(1)}, bf16[2,256,1536]{2,1,0:T(8,128)(2,1)S(1)}, u32[]{:S(2)}, u32[]{:S(2)}) collective-permute-start(bf16[2,256,1536]{2,1,0:T(8,128)(2,1)S(1)} %pad_maximum_fusion.3), channel_id=1, source_target_pairs={{0,1},{1,0},{2,3},{3,2},{4,5},{5,4},{6,7},{7,6},{8,9},{9,8},{10,11... | collective-permute-start | bytes 4718600 | tf_op jit(solution)/shard_map/ppermute | solution.py:1018
  740.6 6.6 collective-permute-start.13
  747.3 6.7 collective-permute-start.14
  754.0 12.5 %collective-permute-start.15 = (f32[4352]{0:T(1024)S(1)}, f32[4352]{0:T(1024)S(1)}, u32[]{:S(2)}, u32[]{:S(2)}) collective-permute-start(f32[4352]{0:T(1024)S(1)} %add.74), channel_id=1, source_target_pairs={{0,16},{4,20},{8,24},{12,28},{16,0},{20,4},{24,8},{28,12},{1,17},{... | collective-permute-start | bytes 52232 | tf_op jit(solution)/shard_map/ppermute | solution.py:1018
  (19 other events, 108.4 us)
Sparse Core Ops, SparseCore 0:
  323.3 117.6 reduce-scatter.2
  445.2 128.8 reduce-scatter.4

commit v2 on v1

--- a/solution.py
+++ b/solution.py
@@ -390,6 +390,58 @@
     )
 
 
+def ring_sums(chains):
+    steps = 2 if all(parts[0][0].shape[1] % 32 == 0 for parts, _, _ in chains) else 1
+    scalars, operands, specs, out_shape, out_specs = [], [], [], [], []
+    for parts, offset, arrived in chains:
+        width = 0
+        for terms, at in parts:
+            r, c = terms.shape[1:]
+            slot = [k for k, have in enumerate(scalars) if have is at]
+            if not slot:
+                slot = [len(scalars)]
+                scalars.append(at)
+            specs.append(
+                pl.BlockSpec((1, r // steps, c), lambda i, *sc, slot=slot[0], offset=offset: (sc[slot][offset], i, 0))
+            )
+            operands.append(terms)
+            width += c
+        for value in arrived:
+            specs.append(pl.BlockSpec((r // steps, width), lambda i, *sc: (i, 0)))
+            operands.append(value)
+        out_shape.append(jax.ShapeDtypeStruct((r, width), jnp.bfloat16))
+        out_specs.append(pl.BlockSpec((r // steps, width), lambda i, *sc: (i, 0)))
+
+    def kernel(*refs):
+        refs = refs[len(scalars) :]
+        ins, outs = list(refs[: len(operands)]), refs[len(operands) :]
+        for (parts, _, arrived), out in zip(chains, outs):
+            terms = [ins.pop(0) for _ in parts]
+            got = [ins.pop(0) for _ in arrived]
+            start = 0
+            for term in terms:
+                columns = slice(start, start + term.shape[2])
+                total = term[0]
+                if got:
+                    total = total.astype(jnp.float32)
+                    for value in got:
+                        total = total + value[:, columns].astype(jnp.float32)
+                    total = total.astype(jnp.bfloat16)
+                out[:, columns] = total
+                start += term.shape[2]
+
+    return pl.pallas_call(
+        kernel,
+        grid_spec=pltpu.PrefetchScalarGridSpec(
+            num_scalar_prefetch=len(scalars), grid=(steps,), in_specs=specs, out_specs=out_specs
+        ),
+        out_shape=out_shape,
+        compiler_params=params(),
+        cost_estimate=cost(0, sum(2 * o.size for o in out_shape) * 3),
+        name="ring_sums",
+    )(*scalars, *operands)
+
+
 def norm_call(kernel, inputs, gain, outs, gain_sum, name):
     r, width = inputs[0].shape
     tile = min(64, r)
@@ -913,8 +965,7 @@
             for way in (0, 1):
                 send(c, way, 0)
 
-    phases = [(0, 1), (2, 3)]
-    start(phases[0])
+    start(range(count - 1))
     turns = []
     for k in range(1, n_u):
         turns.append(group.to_cube(k, blocks_ref.at[k], here, turn_send.at[k - 1], turn_recv.at[k - 1]))
@@ -922,30 +973,24 @@
     own.start()
     own.wait()
     spreads, kept = [], []
-    for phase, chains in enumerate(phases):
-        for step in range(longest):
-            for c in chains:
-                for way in (0, 1):
-                    if step < reaches[c][way]:
-                        copies[c, way, step].wait_recv()
-                        if step + 1 < reaches[c][way]:
-                            send(c, way, step + 1)
-            if step == longest - 2 and phase == 0:
-                for copy in turns:
-                    copy.wait_recv()
-                start(phases[1])
-            if phase == 1 and step % 2 == 1 and step < longest - 1:
-                for spread in spreads:
-                    spread.level()
+    for copy in turns:
+        copy.wait_recv()
+    start([count - 1])
+    for step in range(longest):
+        for c in range(count):
+            for way in (0, 1):
+                if step < reaches[c][way]:
+                    copies[c, way, step].wait_recv()
+                    if step + 1 < reaches[c][way]:
+                        send(c, way, step + 1)
             if step == longest - 1:
-                for c in chains:
-                    add(c, sums[c], 0, [slot(c, way, reaches[c][way] - 1) for way in (0, 1)])
-                    spread = Spread(group, sums[c], outs[c], cube_send.at[c], cube_recv.at[c])
-                    copy = pltpu.make_async_copy(sums[c], outs[c].at[0], local.at[c])
-                    copy.start()
-                    kept.append(copy)
-                    spread.level()
-                    spreads.append(spread)
+                add(c, sums[c], 0, [slot(c, way, reaches[c][way] - 1) for way in (0, 1)])
+                spread = Spread(group, sums[c], outs[c], cube_send.at[c], cube_recv.at[c])
+                copy = pltpu.make_async_copy(sums[c], outs[c].at[0], local.at[c])
+                copy.start()
+                kept.append(copy)
+                spread.level()
+                spreads.append(spread)
     for spread in spreads:
         spread.level()
     for spread in spreads:
@@ -984,7 +1029,7 @@
 
 START = 0.9
 LATENCY = 2.0
-RATES = {"ring": 50.0, "x": 50.0, "core": 250.0}
+RATES = {"ring": 36.0, "x": 50.0, "core": 250.0}
 
 
 class Flight:
@@ -1066,6 +1111,143 @@
 
 def pick(value, index):
     return lax.dynamic_index_in_dim(value, index, 0, keepdims=False, allow_negative_indices=False)
+
+
+def ring_order(count):
+    evens = list(range(0, count, 2))
+    odds = list(range(1, count, 2))
+    return evens + odds[::-1]
+
+
+class Ring:
+    def __init__(self, axis):
+        self.axis = axis
+        self.count = lax.axis_size(axis)
+        order = ring_order(self.count)
+        place = [0] * self.count
+        for position, index in enumerate(order):
+            place[index] = position
+        me = lax.axis_index(axis)
+        owners = [[order[(place[i] + o) % self.count] for o in range(self.count)] for i in range(self.count)]
+        self.owners = pick(jnp.array(owners, jnp.int32), me)
+        following = [(order[k], order[(k + 1) % self.count]) for k in range(self.count)]
+        self.pairs = (following, [(b, a) for a, b in following])
+
+    def reach(self, more_ahead):
+        longer = self.count // 2
+        shorter = self.count - 1 - longer
+        return (longer, shorter) if more_ahead else (shorter, longer)
+
+    def owner(self, offset):
+        return self.owners[offset % self.count]
+
+
+class ReduceChain:
+    def __init__(self, ring, more_ahead):
+        self.ring = ring
+        self.reach = ring.reach(more_ahead)
+        self.terms = None
+        self.moving = [None, None]
+        self.seen = [None, None]
+
+    def have(self, *parts):
+        self.terms = parts
+
+    def ready(self, way, step):
+        return self.terms is not None and (step == self.reach[way] or self.seen[way] == step + 1)
+
+    def entries(self, way):
+        return [(self, step) for step in range(self.reach[way], 0, -1)]
+
+    def operand(self, way, step):
+        offset = (step if way == 0 else -step) % self.ring.count
+        arrived = [self.moving[way]] if step < self.reach[way] else []
+        return (self.terms, offset, arrived)
+
+    def deliver(self, way, step, value):
+        self.moving[way] = value
+        self.seen[way] = step
+
+
+def totals(seq, *chains):
+    return apply_sums(seq, [(c.terms, 0, list(c.moving)) for c in chains])
+
+
+def apply_sums(seq, chains):
+    flat = []
+    for parts, _, arrived in chains:
+        flat.extend([terms for terms, _ in parts] + arrived)
+
+    def call(*values):
+        values = list(values)
+        rebuilt = []
+        for parts, offset, arrived in chains:
+            new = [(values.pop(0), at) for _, at in parts]
+            rebuilt.append((new, offset, [values.pop(0) for _ in arrived]))
+        return tuple(ring_sums(rebuilt))
+
+    return seq.run(1.6 * len(chains) + 0.8, call, *flat)
+
+
+def alternate(*lists):
+    out = []
+    for at in range(max(len(x) for x in lists)):
+        out.extend(x[at] for x in lists if at < len(x))
+    return out
+
+
+class Pump:
+    def __init__(self, seq, ring, queues, window):
+        self.seq, self.ring, self.queues = seq, ring, queues
+        self.window = window
+        self.flying = ([], [])
+        self.busy = False
+        seq.sources.append(self)
+
+    def send(self):
+        sends = []
+        for way in (0, 1):
+            room = self.window - len(self.flying[way])
+            while self.queues[way] and room > 0 and self.queues[way][0][0].ready(way, self.queues[way][0][1]):
+                chain, step = self.queues[way].pop(0)
+                sends.append((way, chain, step, chain.operand(way, step)))
+                room -= 1
+        if not sends:
+            return False
+        self.busy = True
+        sums = [k for k, s in enumerate(sends) if isinstance(s[1], ReduceChain)]
+        values = [s[3] for s in sends]
+        if sums:
+            for k, value in zip(sums, apply_sums(self.seq, [values[k] for k in sums])):
+                values[k] = value
+        for (way, chain, step, _), value in zip(sends, values):
+            flight = self.seq.fly(value, self.ring.axis, self.ring.pairs[way], ("ring", way), "ring")
+            self.flying[way].append((chain, step, flight))
+        self.busy = False
+        return True
+
+    def poll(self, now):
+        if self.busy:
+            return False
+        waits = []
+        for way in (0, 1):
+            if self.flying[way] and self.flying[way][0][2].arrival <= now + 0.5:
+                waits.append((way,) + self.flying[way].pop(0))
+        if waits:
+            values = self.seq.tie(*[w[3].value for w in waits])
+            for (way, chain, step, _), value in zip(waits, values):
+                chain.deliver(way, step, value)
+        return self.send() or bool(waits)
+
+    def next(self):
+        arrivals = [f[0][2].arrival for f in self.flying if f]
+        return min(arrivals) if arrivals else None
+
+    def left(self, *chains):
+        return any(e[0] in chains for way in (0, 1) for e in self.queues[way] + self.flying[way])
+
+    def until(self, *chains):
+        self.seq.drain(lambda: not self.left(*chains))
 
 
 class Cube:
@@ -1197,7 +1379,8 @@
     _, rows, width = tokens.shape
     seq = Sequence()
     cube = Cube("ulysses", seq)
-    n_dp = lax.axis_size("dp")
+    ring = Ring("dp")
+    n_dp = ring.count
     n_u, me = cube.count, cube.me
     bucket = rows * n_u
     depth = width // n_dp
@@ -1223,6 +1406,9 @@
     def task(generator):
         return Task(seq, generator)
 
+    r_gate = ReduceChain(ring, True)
+    pump = Pump(seq, ring, [r_gate.entries(way) for way in (0, 1)], 1)
+
     frequency = np.float32(ROPE_BASE) ** (np.float32(-2.0) * np.arange(head_width // 2, dtype=np.float32) / head_width)
     angles = np.arange(bucket, dtype=np.float32)[:, None] * frequency.astype(np.float32)[None, :]
     cosine, sine = np.cos(angles), np.sin(angles)
@@ -1277,16 +1463,18 @@
     )
 
     grad_gate, grad_up = seq.run(15.5, down_back, grad_result, act_gate, act_up, w_down)
+    gate_terms = seq.run(12.5, lambda a, b: outer_terms(a, b, n_dp), second, grad_gate)
+    r_gate.have((gate_terms.reshape(n_dp, depth, ff_local), ring.owners))
+    pump.send()
+
+    def input_grads(a, b, first, second):
+        return back_matmul(a, b, first, second, rows)
+
+    two_keep, two_send = seq.run(20.5, input_grads, grad_gate, grad_up, w_gate, w_up)
+    t_two = task(cube.reduce(two_keep, two_send))
     up_own = lax.psum_scatter(
         seq.run(12.5, lambda a, b: outer_terms(a, b, n_dp), second, grad_up), "dp", scatter_dimension=0, tiled=True
     )
-
-    def input_grads(a, b, first, second):
-        return back_matmul(a, b, first, second, rows)
-
-    two_keep, two_send = seq.run(20.5, input_grads, grad_gate, grad_up, w_gate, w_up)
-    t_two = task(cube.reduce(two_keep, two_send))
-    gate_terms = seq.run(12.5, lambda a, b: outer_terms(a, b, n_dp), second, grad_gate)
     down_keep, down_send = seq.run(11.5, lambda h, w: even_odd(dot(h, w)), hidden, w_down)
     grad_hidden_in, branch_own, gain_two_own = seq.run(
         5.8, lambda *a: norm_back(*a, True), hidden_in, *t_two.finish(), grad_own, gain_two
@@ -1295,6 +1483,8 @@
     branch_grad = cube.joined(t_branch_grad.finish()).reshape(bucket, width)
 
     grad_gated = seq.run(3.8, dot_nt, branch_grad, w_out)
+    pump.until(r_gate)
+    t_gate_all = task(cube.gather(totals(seq, r_gate)[0]))
     t_down = task(cube.reduce(down_keep, down_send))
     t_down_all = task(cube.gather(seq.tie(down_own)[0]))
     grad_qk, grad_vg, gain_query_own, gain_key_own = seq.run(
@@ -1310,8 +1500,8 @@
     qk_terms = seq.run(9.3, lambda a, b: outer_terms(a, b, n_dp), normed, grad_qk)
     vg_terms = seq.run(9.3, lambda a, b: outer_terms(a, b, n_dp), normed, grad_vg)
 
-    gate_all, qk_all, vg_all, out_all = seq.run(
-        150.0, lambda b, *t: reduce_all(b, t, n_dp, n_u), out_parts, gate_terms, qk_terms, vg_terms
+    qk_all, vg_all, out_all = seq.run(
+        100.0, lambda b, *t: reduce_all(b, t, n_dp, n_u), out_parts, qk_terms, vg_terms
     )
     t_up_all = task(cube.gather(seq.tie(up_own)[0]))
     tokens_grad, gain_one_own = seq.run(
@@ -1333,9 +1523,14 @@
     down_held = t_down_all.finish()
     down_all = seq.run(5.3, lambda p, *b: put_rows(p, (down_held[0], b)), place, *down_held[1])
     up_held = t_up_all.finish()
-    mlp_all = seq.run(
-        10.0, lambda p, a, *b: put_strips(p, [(keys_all, [a]), (up_held[0], b)], n_dp, ff_strip), place, gate_all, *up_held[1]
-    )
+    gate_held = t_gate_all.finish()
+
+    def whole_mlp(p, *blocks):
+        count = len(blocks) // 2
+        both = [(up_held[0], blocks[:count]), (up_held[0], blocks[count:])]
+        return put_strips(p, both, n_dp, ff_strip)
+
+    mlp_all = seq.run(10.0, whole_mlp, place, *gate_held[1], *up_held[1])
     layer_out = seq.run(2.2, lambda a, b, c: a + high(b) + high(c), hidden_in, *t_down.finish())
     gains = t_gains.finish()
 

time: 789 us -> 832 us (1.054)
  waiting for transfers between devices: 55.1 us -> 118 us
  Pallas kernels: 647 us -> 597 us
  starting transfers between devices: 15.6 us -> 31.2 us
    pallas_call x1, Pallas kernels: 184 us -> 117 us  [reduce_all(): pl.pallas_call(functools.partial(reduce_kernel, n_dp, n_u, count), in_spe...]
    ppermute x17 -> x26, waiting for transfers between devices: 55.1 us -> 118 us  [fly(): got = lax.ppermute(value, axis, pairs)]
    pallas_call x0 -> x5, Pallas kernels: none -> 16.9 us  [ring_sums(): pl.pallas_call(kernel, grid_spec=pltpu.PrefetchScalarGridSpec(num_scalar_...]
    ppermute x17 -> x26, starting transfers between devices: 15.3 us -> 30.8 us  [fly(): got = lax.ppermute(value, axis, pairs)]
    concatenate x1, other arithmetic: 0.79 us -> 9.27 us  [joined(): jnp.concatenate([b[at][sub:sub + 1] for _, at, sub in order])]
  transfers between devices with their start and end apart: 19 -> 28, of which waited for: 8 -> 11; matrix products, arithmetic and copies ran while one was open for 2% -> 3% of each run, Pallas kernels for 45% -> 37%
where the time goes in v2:
time: 832 us; the launch traced here: 821 us
  Pallas kernels  597 us (72%)
  waiting for transfers between devices  118 us (14%)
  starting transfers between devices  31.2 us (4%)
  matrix products  22.5 us (3%)
  local copies, waits for them, and re-layouts  19.2 us (2%)
  other arithmetic  17.3 us (2%)
  between operations  15.5 us (2%)
    pallas_call x1, Pallas kernels, forward(): pl.pallas_call(functools.partial(forward_kernel, n_dp, n_u, heads, kv_hea...  274 us
    ppermute x26, waiting for transfers between devices, fly(): got = lax.ppermute(value, axis, pairs)  118 us
    pallas_call x1, Pallas kernels, reduce_all(): pl.pallas_call(functools.partial(reduce_kernel, n_dp, n_u, count), in_spe...  117 us
    pallas_call x4, Pallas kernels, outer_terms(): pl.pallas_call(kernel, grid=(count,), in_specs=[pl.BlockSpec((m, depth),...  43.6 us
    pallas_call x2, Pallas kernels, back_matmul(): pl.pallas_call(kernel, grid=(m // rows // 2,), in_specs=[step, step, stea...  32.4 us
    ppermute x26, starting transfers between devices, fly(): got = lax.ppermute(value, axis, pairs)  30.8 us
    pallas_call x4, Pallas kernels, put_call(): pl.pallas_call(body, grid=(grid,), in_specs=[pl.BlockSpec(memory_space=pl...  24 us
    pallas_call x1, Pallas kernels, attend_back(): pl.pallas_call(functools.partial(attend_back_kernel, min(256, bucket), co...  19.6 us
  transfers between devices with their start and end apart: 28, of which 11 were waited for; matrix products, arithmetic and copies ran while one was open for 3% of the time, Pallas kernels for 37%

profile of v2, /device:TPU:0, one launch (start us, length us, event | category | flops | bytes accessed | tf_op | source)
XLA Modules:
  0.0 821.2 jit_solution(13766581233220935533)
XLA Ops:
  20.0 273.6 %forward.1 = (bf16[2048,768]{1,0:T(8,128)(2,1)}, bf16[2048,768]{1,0:T(8,128)(2,1)}, bf16[2048,1536]{1,0:T(8,128)(2,1)}, bf16[2048,1536]{1,0:T(8,128)(2,1)}, bf16...) custom-call(s32[1]{0:T(128)} %copy.24.length_ref, ...), custom_call_target="tpu_custom_call" | custom-call | flops 1 | bytes 1 | tf_op jit(solution)/shard_map/forward/pallas_call | solution.py:894
  293.7 19.0 %gate_up.1 = (f32[1024,1536]{1,0:T(8,128)}, f32[1024,1536]{1,0:T(8,128)}, bf16[1024,1536]{1,0:T(8,128)(2,1)}) custom-call(bf16[1024,2048]{1,0:T(8,128)(2,1)} %bitcast.47, bf16[2048,1536]{1,0:T(8,128)(2,1)} %get-tuple-element.426.first_ref, bf16[2048,1536]{1,0:T(8,128)(2,1)} %get-tuple-element.427.second_ref), custom_call_target="tpu_custom_call" | custom-call | flops 1 | bytes 1 | tf_op jit(solution)/shard_map/gate_up/pallas_call | solution.py:191
  312.6 10.5 %convolution_convert_fusion = bf16[1536,2048]{1,0:T(8,128)(2,1)} fusion(bf16[1024,1536]{1,0:T(8,128)(2,1)} %get-tuple-element.456, bf16[1024,2048]{1,0:T(8,128)(2,1)S(1)} %bitcast.65), kind=kOutput, calls=%fused_computation | convolution fusion | flops 6445596672 | bytes 13631488 | tf_op jit(solution)/shard_map/km,kn->mn/dot_general | solution.py:1355
  323.5 15.3 %down_back.1 = (bf16[1024,1536]{1,0:T(8,128)(2,1)}, bf16[1024,1536]{1,0:T(8,128)(2,1)}) custom-call(bf16[1024,2048]{1,0:T(8,128)(2,1)} %bitcast.64, f32[1024,1536]{1,0:T(8,128)} %get-tuple-element.406.a_ref, f32[1024,1536]{1,0:T(8,128)} %get-tuple-element.407.b_ref, bf16[1536,2048]{1,0:T(8,128)(2,1)} %get-tuple-element.457.weight_ref), custom_call_target="tpu_custom_call" | custom-call | flops 1 | bytes 1 | tf_op jit(solution)/shard_map/down_back/pallas_call | solution.py:266
  338.7 12.2 %outer_terms.4 = bf16[2048,1536]{1,0:T(8,128)(2,1)} custom-call(bf16[1024,2048]{1,0:T(8,128)(2,1)} %bitcast.48, bf16[1024,1536]{1,0:T(8,128)(2,1)} %get-tuple-element.424.y_ref.a_ref), custom_call_target="tpu_custom_call" | custom-call | flops 1 | bytes 1 | tf_op jit(solution)/shard_map/outer_terms/pallas_call | solution.py:240
  355.2 20.7 %back_matmul.2 = (bf16[2,256,2048]{2,1,0:T(8,128)(2,1)}, bf16[2,256,2048]{2,1,0:T(8,128)(2,1)}) custom-call(bf16[1024,1536]{1,0:T(8,128)(2,1)} %get-tuple-element.424.y_ref.a_ref, bf16[1024,1536]{1,0:T(8,128)(2,1)} %get-tuple-element.434.b_ref.y_ref, bf16[2048,1536]{1,0:T(8,128)(2,1)} %get-tuple-element.426.first_ref, ...), custom_call_target="tpu_custom_call" | custom-call | flops 1 | bytes 1 | tf_op jit(solution)/shard_map/back_matmul/pallas_call | solution.py:220
  377.9 12.2 %outer_terms.5 = bf16[2048,1536]{1,0:T(8,128)(2,1)} custom-call(bf16[1024,2048]{1,0:T(8,128)(2,1)} %bitcast.49, bf16[1024,1536]{1,0:T(8,128)(2,1)} %get-tuple-element.434.b_ref.y_ref), custom_call_target="tpu_custom_call" | custom-call | flops 1 | bytes 1 | tf_op jit(solution)/shard_map/outer_terms/pallas_call | solution.py:240
  390.2 16.7 %collective-permute-done.1.refs_4_ = bf16[256,1536]{1,0:T(8,128)(2,1)S(1)} collective-permute-done((bf16[256,1536]{1,0:T(8,128)(2,1)}, bf16[256,1536]{1,0:T(8,128)(2,1)S(1)}, u32[]{:S(2)}, u32[]{:S(2)}) %collective-permute-start.1) | collective-permute-done | bytes 786464 | tf_op jit(solution)/shard_map/ppermute | solution.py:1063
  420.5 8.3 %convolution_convert_fusion.1 = bf16[1024,2048]{1,0:T(8,128)(2,1)S(1)} fusion(bf16[1024,1536]{1,0:T(8,128)(2,1)} %get-tuple-element.456, bf16[1536,2048]{1,0:T(8,128)(2,1)S(1)} %bitcast.58), kind=kOutput, calls=%fused_computation.2 | convolution fusion | flops 6444548096 | bytes 13631488 | tf_op jit(solution)/shard_map/mk,kn->mn/dot_general | solution.py:1347
  431.3 7.8 collective-permute-done.5
  449.2 18.0 %collective-permute-done.4.refs_4_ = bf16[256,1536]{1,0:T(8,128)(2,1)S(1)} collective-permute-done((bf16[256,1536]{1,0:T(8,128)(2,1)S(1)}, bf16[256,1536]{1,0:T(8,128)(2,1)S(1)}, u32[]{:S(2)}, u32[]{:S(2)}) %collective-permute-start.4) | collective-permute-done | bytes 786464 | tf_op jit(solution)/shard_map/ppermute | solution.py:1063
  475.6 33.9 %collective-permute-done.6.refs_2_ = bf16[256,1536]{1,0:T(8,128)(2,1)S(1)} collective-permute-done((bf16[256,1536]{1,0:T(8,128)(2,1)S(1)}, bf16[256,1536]{1,0:T(8,128)(2,1)S(1)}, u32[]{:S(2)}, u32[]{:S(2)}) %collective-permute-start.6) | collective-permute-done | bytes 786464 | tf_op jit(solution)/shard_map/ppermute | solution.py:1063
  513.3 11.5 %collective-permute-start.8 = (bf16[256,1536]{1,0:T(8,128)(2,1)}, bf16[256,1536]{1,0:T(8,128)(2,1)S(1)}, u32[]{:S(2)}, u32[]{:S(2)}) collective-permute-start(bf16[256,1536]{1,0:T(8,128)(2,1)} %ring_sums.8), channel_id=1, source_target_pairs={{0,8},{8,16},{16,24},{24,28},{28,20},{20,12},{12,4},{4,0},{1,9},{9... | collective-permute-start | bytes 2359304 | tf_op jit(solution)/shard_map/ppermute | solution.py:1063
  524.9 9.3 %pad_maximum_fusion = bf16[4,256,2048]{2,1,0:T(8,128)(2,1)S(1)} fusion(bf16[1,256,2048]{2,1,0:T(8,128)(2,1)S(1)} %get-tuple-element.665, bf16[1,256,2048]{2,1,0:T(8,128)(2,1)S(1)} %collective-permute-done.7, bf16[1,256,2048]{2,1,0:T(8,128)(2,1)S(1)} %get-tuple-element.664, bf16[1,256,2048]{2,1,0:T(8,128)(2,1)S(1)} %bitcast.70), kind=kLoop, calls=%fused_computation.1 | loop fusion | flops 6291456 | bytes 8388608 | tf_op jit(solution)/shard_map/concatenate | solution.py:1288
  538.0 14.9 %collective-permute-done.8.refs_2_ = bf16[256,1536]{1,0:T(8,128)(2,1)S(1)} collective-permute-done((bf16[256,1536]{1,0:T(8,128)(2,1)}, bf16[256,1536]{1,0:T(8,128)(2,1)S(1)}, u32[]{:S(2)}, u32[]{:S(2)}) %collective-permute-start.8) | collective-permute-done | bytes 786464 | tf_op jit(solution)/shard_map/ppermute | solution.py:1063
  558.5 19.6 %attention_back.1 = (bf16[4,256,768]{2,1,0:T(8,128)(2,1)}, bf16[4,256,768]{2,1,0:T(8,128)(2,1)}, f32[1,128]{1,0:T(1,128)}, f32[1,128]{1,0:T(1,128)}) custom-call(s32[2]{0:T(128)} %pad_add_fusion.place_ref, f32[4,256,768]{2,1,0:T(8,128)} %get-tuple-element.512.q_raw.k_raw, f32[4,256,768]{2,1,0:T(8,128)} %get-tuple-element.512.q_raw.k_raw, ...), custom_call_target="tpu_custom_call" | custom-call | flops 1 | bytes 1 | tf_op jit(solution)/shard_map/attention_back/pallas_call | solution.py:136
  583.8 11.7 %back_matmul.3 = (bf16[2,256,2048]{2,1,0:T(8,128)(2,1)}, bf16[2,256,2048]{2,1,0:T(8,128)(2,1)}) custom-call(bf16[1024,768]{1,0:T(8,128)(2,1)} %bitcast.61, bf16[1024,768]{1,0:T(8,128)(2,1)} %bitcast.59, bf16[2048,768]{1,0:T(8,128)(2,1)} %get-tuple-element.546.first_ref, bf16[2048,768]{1,0:T(8,128)(2,1)} %get-tuple-element.547.second_ref), custom_call_target="tpu_custom_call" | custom-call | flops 1 | bytes 1 | tf_op jit(solution)/shard_map/back_matmul/pallas_call | solution.py:220
  595.7 7.6 collective-permute-done.15.refs_1_
  603.9 6.8 out_terms.1.blocks_ref
  618.0 11.7 %collective-permute-done.13 = bf16[1,256,2048]{2,1,0:T(8,128)(2,1)S(1)} collective-permute-done((bf16[1,256,2048]{2,1,0:T(8,128)(2,1)}, bf16[1,256,2048]{2,1,0:T(8,128)(2,1)S(1)}, u32[]{:S(2)}, u32[]{:S(2)}) %collective-permute-start.13) | collective-permute-done | bytes 1048608 | tf_op jit(solution)/shard_map/ppermute | solution.py:1063
  629.7 9.5 %outer_terms.6.refs_0_ = bf16[2048,768]{1,0:T(8,128)(2,1)} custom-call(bf16[1024,2048]{1,0:T(8,128)(2,1)} %bitcast.50, bf16[1024,768]{1,0:T(8,128)(2,1)} %bitcast.62), custom_call_target="tpu_custom_call" | custom-call | flops 1 | bytes 1 | tf_op jit(solution)/shard_map/outer_terms/pallas_call | solution.py:240
  639.2 9.7 %outer_terms.7.refs_1_ = bf16[2048,768]{1,0:T(8,128)(2,1)} custom-call(bf16[1024,2048]{1,0:T(8,128)(2,1)} %bitcast.51, bf16[1024,768]{1,0:T(8,128)(2,1)} %bitcast.60), custom_call_target="tpu_custom_call" | custom-call | flops 1 | bytes 1 | tf_op jit(solution)/shard_map/outer_terms/pallas_call | solution.py:240
  649.0 116.8 %reduce_all.1 = (bf16[4,256,768]{2,1,0:T(8,128)(2,1)}, bf16[4,256,768]{2,1,0:T(8,128)(2,1)}, bf16[4,256,512]{2,1,0:T(8,128)(2,1)}) custom-call(bf16[4,512,512]{2,1,0:T(8,128)(2,1)} %out_terms.1.blocks_ref, bf16[2048,768]{1,0:T(8,128)(2,1)} %outer_terms.6.refs_0_, bf16[2048,768]{1,0:T(8,128)(2,1)} %outer_terms.7.refs_1_), custom_call_target="tpu_custom_call" | custom-call | flops 1 | bytes 1 | tf_op jit(solution)/shard_map/reduce_all/pallas_call | solution.py:1012
  799.6 10.0 %put_strips.1 = f32[256,12288]{1,0:T(8,128)} custom-call(s32[2]{0:T(128)} %pad_add_fusion.place_ref, bf16[1,256,1536]{2,1,0:T(8,128)(2,1)} %bitcast.55, bf16[1,256,1536]{2,1,0:T(8,128)(2,1)} %copy-done.8, bf16[2,256,1536]{2,1,0:T(8,128)(2,1)} %collective-permute-done.16.refs_2_, bf16[1,256,1536]{2,1,0:T(8,128)(2,1)} %bitcast.72, ...), custom_call_target="tpu_custom_call" | custom-call | flops 1 | bytes 1 | tf_op jit(solution)/shard_map/put_strips/pallas_call | solution.py:322
  (162 shorter events, 118.6 us)
Async XLA Ops:
  7.2 551.3 %reduce-scatter.3.cloned.1.call-start = ((), (), s32[]{:S(2)}) async-start(), calls=%async_computation.2 | async-start | bytes 7077888 | tf_op jit(solution)/shard_map/reduce_scatter | solution.py:1461
  323.2 442.7 %reduce-scatter.5.cloned.1.call-start = ((), (), s32[]{:S(2)}) async-start(), calls=%async_computation.3 | async-start | bytes 7077888 | tf_op jit(solution)/shard_map/reduce_scatter | solution.py:1475
  375.8 34.4 %collective-permute-start.2 = (bf16[2,256,2048]{2,1,0:T(8,128)(2,1)}, bf16[2,256,2048]{2,1,0:T(8,128)(2,1)S(1)}, u32[]{:S(2)}, u32[]{:S(2)}) collective-permute-start(bf16[2,256,2048]{2,1,0:T(8,128)(2,1)} %get-tuple-element.432), channel_id=1, source_target_pairs={{0,1},{1,0},{2,3},{3,2},{4,5},{5,4},{6,7},{7,6},{8,9},{9,8},{10,11... | collective-permute-start | bytes 6291464 | tf_op jit(solution)/shard_map/ppermute | solution.py:1063
  375.9 31.0 %collective-permute-start.1 = (bf16[256,1536]{1,0:T(8,128)(2,1)}, bf16[256,1536]{1,0:T(8,128)(2,1)S(1)}, u32[]{:S(2)}, u32[]{:S(2)}) collective-permute-start(bf16[256,1536]{1,0:T(8,128)(2,1)} %get-tuple-element.423), channel_id=1, source_target_pairs={{8,0},{16,8},{24,16},{28,24},{20,28},{12,20},{4,12},{0,4},{9,1},{1... | collective-permute-start | bytes 2359304 | tf_op jit(solution)/shard_map/ppermute | solution.py:1063
  377.5 32.8 %collective-permute-start = (bf16[256,1536]{1,0:T(8,128)(2,1)}, bf16[256,1536]{1,0:T(8,128)(2,1)}, u32[]{:S(2)}, u32[]{:S(2)}) collective-permute-start(bf16[256,1536]{1,0:T(8,128)(2,1)} %get-tuple-element.422), channel_id=1, source_target_pairs={{0,8},{8,16},{16,24},{24,28},{28,20},{20,12},{12,4},{4,0},{1,9},{9... | collective-permute-start | bytes 2359304 | tf_op jit(solution)/shard_map/ppermute | solution.py:1063
  415.9 23.2 %collective-permute-start.5 = (bf16[1,256,2048]{2,1,0:T(8,128)(2,1)}, bf16[1,256,2048]{2,1,0:T(8,128)(2,1)S(1)}, u32[]{:S(2)}, u32[]{:S(2)}) collective-permute-start(bf16[1,256,2048]{2,1,0:T(8,128)(2,1)} %get-tuple-element.445), channel_id=1, source_target_pairs={{0,2},{1,3},{2,0},{3,1},{4,6},{5,7},{6,4},{7,5},{8,10},{9,11},{10,... | collective-permute-start | bytes 3145736 | tf_op jit(solution)/shard_map/ppermute | solution.py:1063
  445.8 26.6 %collective-permute-start.7 = (bf16[1,256,2048]{2,1,0:T(8,128)(2,1)}, bf16[1,256,2048]{2,1,0:T(8,128)(2,1)S(1)}, u32[]{:S(2)}, u32[]{:S(2)}) collective-permute-start(bf16[1,256,2048]{2,1,0:T(8,128)(2,1)} %bitcast.68), channel_id=1, source_target_pairs={{0,2},{1,3},{2,0},{3,1},{4,6},{5,7},{6,4},{7,5},{8,10},{9,11},{10,... | collective-permute-start | bytes 3145736 | tf_op jit(solution)/shard_map/ppermute | solution.py:1063
  447.1 20.0 %collective-permute-start.4 = (bf16[256,1536]{1,0:T(8,128)(2,1)S(1)}, bf16[256,1536]{1,0:T(8,128)(2,1)S(1)}, u32[]{:S(2)}, u32[]{:S(2)}) collective-permute-start(bf16[256,1536]{1,0:T(8,128)(2,1)S(1)} %copy-done.32), channel_id=1, source_target_pairs={{8,0},{16,8},{24,16},{28,24},{20,28},{12,20},{4,12},{0,4},{9,1},{1... | collective-permute-start | bytes 2359304 | tf_op jit(solution)/shard_map/ppermute | solution.py:1063
  448.1 19.1 %collective-permute-start.3 = (bf16[256,1536]{1,0:T(8,128)(2,1)S(1)}, bf16[256,1536]{1,0:T(8,128)(2,1)S(1)}, u32[]{:S(2)}, u32[]{:S(2)}) collective-permute-start(bf16[256,1536]{1,0:T(8,128)(2,1)S(1)} %copy-done.31), channel_id=1, source_target_pairs={{0,8},{8,16},{16,24},{24,28},{28,20},{20,12},{12,4},{4,0},{1,9},{9... | collective-permute-start | bytes 2359304 | tf_op jit(solution)/shard_map/ppermute | solution.py:1063
  472.6 52.1 %collective-permute-start.9 = (bf16[2,256,2048]{2,1,0:T(8,128)(2,1)S(1)}, bf16[2,256,2048]{2,1,0:T(8,128)(2,1)S(1)}, u32[]{:S(2)}, u32[]{:S(2)}) collective-permute-start(bf16[2,256,2048]{2,1,0:T(8,128)(2,1)S(1)} %pad_maximum_fusion.1), channel_id=1, source_target_pairs={{0,1},{1,0},{2,3},{3,2},{4,5},{5,4},{6,7},{7,6},{8,9},{9,8},{10,11... | collective-permute-start | bytes 6291464 | tf_op jit(solution)/shard_map/ppermute | solution.py:1063
  473.6 35.9 %collective-permute-start.6 = (bf16[256,1536]{1,0:T(8,128)(2,1)S(1)}, bf16[256,1536]{1,0:T(8,128)(2,1)S(1)}, u32[]{:S(2)}, u32[]{:S(2)}) collective-permute-start(bf16[256,1536]{1,0:T(8,128)(2,1)S(1)} %copy-done.33), channel_id=1, source_target_pairs={{0,8},{8,16},{16,24},{24,28},{28,20},{20,12},{12,4},{4,0},{1,9},{9... | collective-permute-start | bytes 2359304 | tf_op jit(solution)/shard_map/ppermute | solution.py:1063
  475.1 49.7 %collective-permute-start.10 = (bf16[256,1536]{1,0:T(8,128)(2,1)}, bf16[256,1536]{1,0:T(8,128)(2,1)S(1)}, u32[]{:S(2)}, u32[]{:S(2)}) collective-permute-start(bf16[256,1536]{1,0:T(8,128)(2,1)} %get-tuple-element.484), channel_id=1, source_target_pairs={{8,0},{16,8},{24,16},{28,24},{20,28},{12,20},{4,12},{0,4},{9,1},{1... | collective-permute-start | bytes 2359304 | tf_op jit(solution)/shard_map/ppermute | solution.py:1063
  513.3 39.6 %collective-permute-start.8 = (bf16[256,1536]{1,0:T(8,128)(2,1)}, bf16[256,1536]{1,0:T(8,128)(2,1)S(1)}, u32[]{:S(2)}, u32[]{:S(2)}) collective-permute-start(bf16[256,1536]{1,0:T(8,128)(2,1)} %ring_sums.8), channel_id=1, source_target_pairs={{0,8},{8,16},{16,24},{24,28},{28,20},{20,12},{12,4},{4,0},{1,9},{9... | collective-permute-start | bytes 2359304 | tf_op jit(solution)/shard_map/ppermute | solution.py:1063
  557.0 21.1 %collective-permute-start.11 = (bf16[2,256,2048]{2,1,0:T(8,128)(2,1)}, bf16[2,256,2048]{2,1,0:T(8,128)(2,1)}, u32[]{:S(2)}, u32[]{:S(2)}) collective-permute-start(bf16[2,256,2048]{2,1,0:T(8,128)(2,1)} %get-tuple-element.508), channel_id=1, source_target_pairs={{0,1},{1,0},{2,3},{3,2},{4,5},{5,4},{6,7},{7,6},{8,9},{9,8},{10,11... | collective-permute-start | bytes 6291464 | tf_op jit(solution)/shard_map/ppermute | solution.py:1063
  557.0 21.1 %collective-permute-start.12 = (bf16[1,256,1536]{2,1,0:T(8,128)(2,1)}, bf16[1,256,1536]{2,1,0:T(8,128)(2,1)S(1)}, u32[]{:S(2)}, u32[]{:S(2)}) collective-permute-start(bf16[1,256,1536]{2,1,0:T(8,128)(2,1)} %bitcast.54), channel_id=1, source_target_pairs={{0,2},{1,3},{2,0},{3,1},{4,6},{5,7},{6,4},{7,5},{8,10},{9,11},{10,... | collective-permute-start | bytes 2359304 | tf_op jit(solution)/shard_map/ppermute | solution.py:1063
  583.2 12.4 %collective-permute-start.16 = (bf16[2,256,1536]{2,1,0:T(8,128)(2,1)S(1)}, bf16[2,256,1536]{2,1,0:T(8,128)(2,1)}, u32[]{:S(2)}, u32[]{:S(2)}) collective-permute-start(bf16[2,256,1536]{2,1,0:T(8,128)(2,1)S(1)} %pad_maximum_fusion.2), channel_id=1, source_target_pairs={{0,1},{1,0},{2,3},{3,2},{4,5},{5,4},{6,7},{7,6},{8,9},{9,8},{10,11... | collective-permute-start | bytes 4718600 | tf_op jit(solution)/shard_map/ppermute | solution.py:1063
  583.5 19.8 %collective-permute-start.15 = (bf16[1,192,2048]{2,1,0:T(8,128)(2,1)S(1)}, bf16[1,192,2048]{2,1,0:T(8,128)(2,1)S(1)}, u32[]{:S(2)}, u32[]{:S(2)}) collective-permute-start(bf16[1,192,2048]{2,1,0:T(8,128)(2,1)S(1)} %bitcast.75), channel_id=1, source_target_pairs={{0,2},{1,3},{2,0},{3,1},{4,6},{5,7},{6,4},{7,5},{8,10},{9,11},{10,... | collective-permute-start | bytes 2359304 | tf_op jit(solution)/shard_map/ppermute | solution.py:1063
  595.6 15.1 %collective-permute-start.14 = (bf16[2,256,2048]{2,1,0:T(8,128)(2,1)}, bf16[2,256,2048]{2,1,0:T(8,128)(2,1)S(1)}, u32[]{:S(2)}, u32[]{:S(2)}) collective-permute-start(bf16[2,256,2048]{2,1,0:T(8,128)(2,1)} %get-tuple-element.552), channel_id=1, source_target_pairs={{0,1},{1,0},{2,3},{3,2},{4,5},{5,4},{6,7},{7,6},{8,9},{9,8},{10,11... | collective-permute-start | bytes 6291464 | tf_op jit(solution)/shard_map/ppermute | solution.py:1063
  603.4 35.9 %collective-permute-start.18 = (bf16[2,192,2048]{2,1,0:T(8,128)(2,1)S(1)}, bf16[2,192,2048]{2,1,0:T(8,128)(2,1)S(1)}, u32[]{:S(2)}, u32[]{:S(2)}) collective-permute-start(bf16[2,192,2048]{2,1,0:T(8,128)(2,1)S(1)} %pad_maximum_fusion.3), channel_id=1, source_target_pairs={{0,1},{1,0},{2,3},{3,2},{4,5},{5,4},{6,7},{7,6},{8,9},{9,8},{10,11... | collective-permute-start | bytes 4718600 | tf_op jit(solution)/shard_map/ppermute | solution.py:1063
  603.5 26.2 %collective-permute-start.13 = (bf16[1,256,2048]{2,1,0:T(8,128)(2,1)}, bf16[1,256,2048]{2,1,0:T(8,128)(2,1)S(1)}, u32[]{:S(2)}, u32[]{:S(2)}) collective-permute-start(bf16[1,256,2048]{2,1,0:T(8,128)(2,1)} %get-tuple-element.540), channel_id=1, source_target_pairs={{0,2},{1,3},{2,0},{3,1},{4,6},{5,7},{6,4},{7,5},{8,10},{9,11},{10,... | collective-permute-start | bytes 3145736 | tf_op jit(solution)/shard_map/ppermute | solution.py:1063
  616.3 151.9 %collective-permute-start.17 = (bf16[1,256,2048]{2,1,0:T(8,128)(2,1)}, bf16[1,256,2048]{2,1,0:T(8,128)(2,1)S(1)}, u32[]{:S(2)}, u32[]{:S(2)}) collective-permute-start(bf16[1,256,2048]{2,1,0:T(8,128)(2,1)} %get-tuple-element.569), channel_id=1, source_target_pairs={{0,2},{1,3},{2,0},{3,1},{4,6},{5,7},{6,4},{7,5},{8,10},{9,11},{10,... | collective-permute-start | bytes 3145736 | tf_op jit(solution)/shard_map/ppermute | solution.py:1063
  765.8 20.9 %collective-permute-start.21 = (bf16[1,256,1536]{2,1,0:T(8,128)(2,1)}, bf16[1,256,1536]{2,1,0:T(8,128)(2,1)S(1)}, u32[]{:S(2)}, u32[]{:S(2)}) collective-permute-start(bf16[1,256,1536]{2,1,0:T(8,128)(2,1)} %bitcast.71), channel_id=1, source_target_pairs={{0,2},{1,3},{2,0},{3,1},{4,6},{5,7},{6,4},{7,5},{8,10},{9,11},{10,... | collective-permute-start | bytes 2359304 | tf_op jit(solution)/shard_map/ppermute | solution.py:1063
  787.1 11.4 %collective-permute-start.25 = (bf16[2,256,1536]{2,1,0:T(8,128)(2,1)S(1)}, bf16[2,256,1536]{2,1,0:T(8,128)(2,1)S(1)}, u32[]{:S(2)}, u32[]{:S(2)}) collective-permute-start(bf16[2,256,1536]{2,1,0:T(8,128)(2,1)S(1)} %pad_maximum_fusion.4), channel_id=1, source_target_pairs={{0,1},{1,0},{2,3},{3,2},{4,5},{5,4},{6,7},{7,6},{8,9},{9,8},{10,11... | collective-permute-start | bytes 4718600 | tf_op jit(solution)/shard_map/ppermute | solution.py:1063
  798.1 11.5 %collective-permute-start.24 = (f32[4352]{0:T(1024)S(1)}, f32[4352]{0:T(1024)S(1)}, u32[]{:S(2)}, u32[]{:S(2)}) collective-permute-start(f32[4352]{0:T(1024)S(1)} %add.74), channel_id=1, source_target_pairs={{0,16},{4,20},{8,24},{12,28},{16,0},{20,4},{24,8},{28,12},{1,17},{... | collective-permute-start | bytes 52232 | tf_op jit(solution)/shard_map/ppermute | solution.py:1063
  (40 other events, 382.1 us)
Sparse Core Ops, SparseCore 0:
  323.3 133.1 reduce-scatter.2
  460.7 147.6 reduce-scatter.4

commit v3 on v1

--- a/solution.py
+++ b/solution.py
@@ -171,35 +171,6 @@
     )(place, raw_qk, raw_qk, q, k, v, gate, attended, upstream, totals, q_gain, k_gain, cosine, sine)
 
 
-def gate_up(x, first, second):
-    m, width = x.shape
-    n = first.shape[1]
-    tile = tile_of(n)
-    step_rows = min(256, m)
-
-    def kernel(x_ref, first_ref, second_ref, a_out, b_out, hidden_out):
-        for at in range(0, m, step_rows):
-            rows = slice(at, at + step_rows)
-            a = jnp.dot(x_ref[rows], first_ref[...], preferred_element_type=jnp.float32)
-            b = jnp.dot(x_ref[rows], second_ref[...], preferred_element_type=jnp.float32)
-            a_out[rows] = a
-            b_out[rows] = b
-            hidden_out[rows] = (a * jax.nn.sigmoid(a) * b).astype(jnp.bfloat16)
-
-    weight = pl.BlockSpec((width, tile), lambda j: (0, j))
-    out = pl.BlockSpec((m, tile), lambda j: (0, j))
-    return pl.pallas_call(
-        kernel,
-        grid=(n // tile,),
-        in_specs=[steady((m, width)), weight, weight],
-        out_specs=[out] * 3,
-        out_shape=[jax.ShapeDtypeStruct((m, n), d) for d in (jnp.float32, jnp.float32, jnp.bfloat16)],
-        compiler_params=params(),
-        cost_estimate=cost(),
-        name="gate_up",
-    )(x, first, second)
-
-
 def back_matmul(a, b, first, second, rows):
     m, n = a.shape
     width = first.shape[0]
@@ -606,9 +577,9 @@
 def forward_kernel(
     n_dp, n_u, heads, kv_heads, length_ref, tokens_ref, gain_one, gain_two, q_gain, k_gain, cosine, sine, grad_ref,
     out_item, qk_item, vg_item, gate_item, up_item, down_item,
-    w_qk, w_vg, w_gate, w_up, w_down, normed_out, grad_out, second_out,
+    w_qk, w_vg, w_gate, w_up, w_down, normed_out, grad_out, second_out, act_gate, act_up, act_hidden,
     raw_qk, raw_vg, q_out, k_out, v_out, gate_out, attended_out, gated_out, total_out, w_out, hidden_out,
-    normed, own, qk_local, vg_local, columns, turned, parts, core_got, total, second_own,
+    normed, own, qk_local, vg_local, columns, turned, parts, core_got, total, second_own, gate_stage, up_stage, hidden_stage,
     ring_send, ring_recv, cube_send, cube_recv, turn_send, turn_recv, sum_send, sum_recv, local,
 ):
     rows_own, width = tokens_ref.shape
@@ -704,7 +675,7 @@
         turns.append(group.to_cube(k, source, turned.at[k], turn_send.at[k - 1], turn_recv.at[k - 1]))
     keep(columns.at[pl.ds(pl.multiple_of(me * share, 16), share)], turned.at[0]).wait()
     one, two = keep(w_qk, qk_local), keep(w_vg, vg_local)
-    keep(normed, normed_out)
+    normed_copy = keep(normed, normed_out)
     one.wait()
     two.wait()
 
@@ -715,6 +686,7 @@
         return carry
 
     lax.fori_loop(0, n_u, project, 0)
+    normed_copy.wait()
     pump()
 
     length = length_ref[0]
@@ -801,17 +773,55 @@
         second_own[rows] = (hidden * head_scale(hidden) * gain_two[...]).astype(jnp.bfloat16)
 
     by_rows(rows_own, 64, second)
-    spread = Spread(group, second_own, second_out, cube_send.at[2], cube_recv.at[2])
-    keep(second_own, second_out.at[0])
+    spread = Spread(group, second_own, normed, cube_send.at[2], cube_recv.at[2])
+    keep(second_own, normed.at[0])
     while spread.level():
         pump(2)
+    kept[12].wait()
+    second_copy = keep(normed, second_out)
+    while events and events[0][0][0] in ("start", 3, 4):
+        pump(1)
+    for copy in kept[3:5]:
+        copy.wait()
+    n = qk_local.shape[1]
+    for part in range(w_gate.shape[1] // n):
+        where = slice(part * n, (part + 1) * n)
+        at = 14 + 5 * part
+        loads = [
+            pltpu.make_async_copy(w_gate.at[:, where], qk_local, local.at[at]),
+            pltpu.make_async_copy(w_up.at[:, where], vg_local, local.at[at + 1]),
+        ]
+        for copy in loads:
+            copy.start()
+        for copy in loads:
+            copy.wait()
+
+        def expand(b, carry):
+            x = normed[b]
+            one = jnp.dot(x, qk_local[...], preferred_element_type=jnp.float32)
+            two = jnp.dot(x, vg_local[...], preferred_element_type=jnp.float32)
+            gate_stage[b] = one
+            up_stage[b] = two
+            hidden_stage[b] = (one * jax.nn.sigmoid(one) * two).astype(jnp.bfloat16)
+            return carry
+
+        lax.fori_loop(0, n_u, expand, 0)
+        stores = []
+        for k, (stage, out) in enumerate(((gate_stage, act_gate), (up_stage, act_up), (hidden_stage, act_hidden))):
+            copy = pltpu.make_async_copy(stage, out.at[:, :, where], local.at[at + 2 + k])
+            copy.start()
+            stores.append(copy)
+        pump(2)
+        for copy in stores:
+            copy.wait()
+    second_copy.wait()
     spreads[1].finish()
     spread.finish()
     pump(1000)
     ring.finish()
     for copy in turns + sums:
         copy.wait_send()
-    for copy in kept[3:6] + kept[7:8] + kept[11:]:
+    for copy in kept[5:6] + kept[7:8]:
         copy.wait()
 
 
@@ -831,6 +841,8 @@
 
     out_shape = [shape(n_dp * i.shape[0], i.shape[1]) for i in items[1:]]
     out_shape += [shape(n_u, rows, width)] * 3
+    hidden = items[4].shape[1]
+    out_shape += [shape(n_u, rows, hidden, dtype=jnp.float32)] * 2 + [shape(n_u, rows, hidden)]
     out_shape += [shape(n_u, rows, total, dtype=jnp.float32)] * 2
     out_shape += [
         shape(bucket, heads * size), shape(bucket, kv_heads * size), shape(bucket, kv_heads * size),
@@ -842,7 +854,7 @@
     return pl.pallas_call(
         functools.partial(forward_kernel, n_dp, n_u, heads, kv_heads),
         in_specs=[pl.BlockSpec(memory_space=pltpu.SMEM)] + [local] * 7 + [anywhere] * 7,
-        out_specs=[anywhere] * 8 + [local] * 11,
+        out_specs=[anywhere] * 11 + [local] * 11,
         out_shape=out_shape,
         scratch_shapes=[
             pltpu.VMEM((n_u, rows, width), jnp.bfloat16),
@@ -855,8 +867,11 @@
             pltpu.VMEM((n_u - 1, rows, width), jnp.bfloat16),
             pltpu.VMEM((rows, width), jnp.float32),
             pltpu.VMEM((rows, width), jnp.bfloat16),
+            pltpu.VMEM((n_u, rows, total), jnp.float32),
+            pltpu.VMEM((n_u, rows, total), jnp.float32),
+            pltpu.VMEM((n_u, rows, total), jnp.bfloat16),
             dma((7, 2, longest)), dma((7, 2, longest)), dma((3, n_u - 1)), dma((3, n_u - 1)),
-            dma((n_u - 1,)), dma((n_u - 1,)), dma((n_u - 1,)), dma((n_u - 1,)), dma((13,)),
+            dma((n_u - 1,)), dma((n_u - 1,)), dma((n_u - 1,)), dma((n_u - 1,)), dma((14 + 5 * (hidden // total),)),
         ],
         compiler_params=pltpu.CompilerParams(vmem_limit_bytes=60 * 1024 * 1024, collective_id=0, has_side_effects=True),
         cost_estimate=cost(),
@@ -1005,8 +1020,9 @@
         self.last = tied
         return tied
 
-    def run(self, cost, function, *values):
-        self.poll()
+    def run(self, cost, function, *values, take=True):
+        if take:
+            self.poll()
         out = function(*self.tie(*values))
         self.now += cost
         if isinstance(out, (tuple, list)):
@@ -1255,7 +1271,7 @@
         down_weight,
     )
     (
-        w_qk, w_vg, w_gate, w_up, w_down, normed, grad_result, second,
+        w_qk, w_vg, w_gate, w_up, w_down, normed, grad_result, second, act_gate, act_up, hidden,
         raw_qk, raw_vg, queries, keys, values, gate, attended, gated, log_totals, w_out, hidden_in,
     ) = seq.run(
         250.0,
@@ -1271,27 +1287,28 @@
         value = low(value).reshape(n_u, rows, width)
         return (value[0::2], value[1::2])
 
-    act_gate, act_up, hidden = seq.run(20.0, gate_up, second, w_gate, w_up)
+    act_gate, act_up, hidden = (v.reshape(bucket, ff_local) for v in (act_gate, act_up, hidden))
     down_own = lax.psum_scatter(
         seq.run(10.7, lambda h, g: low(dot_tn(h, g)), hidden, grad_result), "dp", scatter_dimension=0, tiled=True
     )
 
     grad_gate, grad_up = seq.run(15.5, down_back, grad_result, act_gate, act_up, w_down)
+
+    def input_grads(a, b, first, second):
+        return back_matmul(a, b, first, second, rows)
+
+    two_keep, two_send = seq.run(20.5, input_grads, grad_gate, grad_up, w_gate, w_up)
+    t_two = task(cube.reduce(two_keep, two_send))
+    seq.idle(t_two.next())
     up_own = lax.psum_scatter(
         seq.run(12.5, lambda a, b: outer_terms(a, b, n_dp), second, grad_up), "dp", scatter_dimension=0, tiled=True
     )
-
-    def input_grads(a, b, first, second):
-        return back_matmul(a, b, first, second, rows)
-
-    two_keep, two_send = seq.run(20.5, input_grads, grad_gate, grad_up, w_gate, w_up)
-    t_two = task(cube.reduce(two_keep, two_send))
-    gate_terms = seq.run(12.5, lambda a, b: outer_terms(a, b, n_dp), second, grad_gate)
     down_keep, down_send = seq.run(11.5, lambda h, w: even_odd(dot(h, w)), hidden, w_down)
     grad_hidden_in, branch_own, gain_two_own = seq.run(
         5.8, lambda *a: norm_back(*a, True), hidden_in, *t_two.finish(), grad_own, gain_two
     )
     t_branch_grad = task(cube.gather(branch_own))
+    gate_terms = seq.run(12.5, lambda a, b: outer_terms(a, b, n_dp), second, grad_gate)
     branch_grad = cube.joined(t_branch_grad.finish()).reshape(bucket, width)
 
     grad_gated = seq.run(3.8, dot_nt, branch_grad, w_out)
@@ -1311,7 +1328,7 @@
     vg_terms = seq.run(9.3, lambda a, b: outer_terms(a, b, n_dp), normed, grad_vg)
 
     gate_all, qk_all, vg_all, out_all = seq.run(
-        150.0, lambda b, *t: reduce_all(b, t, n_dp, n_u), out_parts, gate_terms, qk_terms, vg_terms
+        150.0, lambda b, *t: reduce_all(b, t, n_dp, n_u), out_parts, gate_terms, qk_terms, vg_terms, take=False
     )
     t_up_all = task(cube.gather(seq.tie(up_own)[0]))
     tokens_grad, gain_one_own = seq.run(

time: 789 us -> 768 us (0.973)
  Pallas kernels: 647 us -> 628 us
  waiting for transfers between devices: 55.1 us -> 44.7 us
    pallas_call x1 -> x0, Pallas kernels: 19 us -> none  [gate_up(): pl.pallas_call(kernel, grid=(n // tile,), in_specs=[steady((m, width)), w...]
    ppermute x17, waiting for transfers between devices: 55.1 us -> 44.6 us  [fly(): got = lax.ppermute(value, axis, pairs)]
    concatenate x1, other arithmetic: 0.79 us -> 9.32 us  [joined(): jnp.concatenate([b[at][sub:sub + 1] for _, at, sub in order])]
  transfers between devices with their start and end apart: 19 -> 19, of which waited for: 8 -> 9; matrix products, arithmetic and copies ran while one was open for 2% -> 4% of each run, Pallas kernels for 45% -> 46%
where the time goes in v3:
time: 768 us; the launch traced here: 759 us
  Pallas kernels  628 us (82%)
  waiting for transfers between devices  44.7 us (6%)
  matrix products  25.1 us (3%)
  other arithmetic  17.2 us (2%)
  starting transfers between devices  15.8 us (2%)
  between operations  15.4 us (2%)
  local copies, waits for them, and re-layouts  12.7 us (2%)
    pallas_call x1, Pallas kernels, forward(): pl.pallas_call(functools.partial(forward_kernel, n_dp, n_u, heads, kv_hea...  274 us
    pallas_call x1, Pallas kernels, reduce_all(): pl.pallas_call(functools.partial(reduce_kernel, n_dp, n_u, count), in_spe...  185 us
    ppermute x17, waiting for transfers between devices, fly(): got = lax.ppermute(value, axis, pairs)  44.6 us
    pallas_call x4, Pallas kernels, outer_terms(): pl.pallas_call(kernel, grid=(count,), in_specs=[pl.BlockSpec((m, depth),...  42.7 us
    pallas_call x2, Pallas kernels, back_matmul(): pl.pallas_call(kernel, grid=(m // rows // 2,), in_specs=[step, step, stea...  31.9 us
    pallas_call x4, Pallas kernels, put_call(): pl.pallas_call(body, grid=(grid,), in_specs=[pl.BlockSpec(memory_space=pl...  23.5 us
    pallas_call x1, Pallas kernels, attend_back(): pl.pallas_call(functools.partial(attend_back_kernel, min(256, bucket), co...  19.7 us
    ppermute x17, starting transfers between devices, fly(): got = lax.ppermute(value, axis, pairs)  15.8 us
  transfers between devices with their start and end apart: 19, of which 9 were waited for; matrix products, arithmetic and copies ran while one was open for 4% of the time, Pallas kernels for 46%

profile of v3, /device:TPU:0, one launch (start us, length us, event | category | flops | bytes accessed | tf_op | source)
XLA Modules:
  0.0 758.9 jit_solution(16511371814912889387)
XLA Ops:
  8.7 4.8 take_strips.1
  20.0 273.7 %forward.1 = (bf16[2048,768]{1,0:T(8,128)(2,1)}, bf16[2048,768]{1,0:T(8,128)(2,1)}, bf16[2048,1536]{1,0:T(8,128)(2,1)}, bf16[2048,1536]{1,0:T(8,128)(2,1)}, bf16...) custom-call(s32[1]{0:T(128)} %copy.23.length_ref, ...), custom_call_target="tpu_custom_call" | custom-call | flops 1 | bytes 1 | tf_op jit(solution)/shard_map/forward/pallas_call | solution.py:854
  293.7 11.6 %convolution_convert_fusion = bf16[1536,2048]{1,0:T(8,128)(2,1)} fusion(bf16[1024,1536]{1,0:T(8,128)(2,1)} %bitcast.81, bf16[1024,2048]{1,0:T(8,128)(2,1)} %bitcast.51), kind=kOutput, calls=%fused_computation | convolution fusion | flops 6445596672 | bytes 13631488 | tf_op jit(solution)/shard_map/km,kn->mn/dot_general | solution.py:1189
  305.3 15.3 %down_back.1 = (bf16[1024,1536]{1,0:T(8,128)(2,1)}, bf16[1024,1536]{1,0:T(8,128)(2,1)}) custom-call(bf16[1024,2048]{1,0:T(8,128)(2,1)} %bitcast.52, f32[1024,1536]{1,0:T(8,128)} %bitcast.44, f32[1024,1536]{1,0:T(8,128)} %bitcast.45, bf16[1536,2048]{1,0:T(8,128)(2,1)} %get-tuple-element.381.weight_ref), custom_call_target="tpu_custom_call" | custom-call | flops 1 | bytes 1 | tf_op jit(solution)/shard_map/down_back/pallas_call | solution.py:237
  320.6 20.3 %back_matmul.2 = (bf16[2,256,2048]{2,1,0:T(8,128)(2,1)}, bf16[2,256,2048]{2,1,0:T(8,128)(2,1)}) custom-call(bf16[1024,1536]{1,0:T(8,128)(2,1)} %get-tuple-element.398.a_ref.y_ref, bf16[1024,1536]{1,0:T(8,128)(2,1)} %get-tuple-element.378.b_ref.y_ref, bf16[2048,1536]{1,0:T(8,128)(2,1)} %get-tuple-element.362.first_ref, ...), custom_call_target="tpu_custom_call" | custom-call | flops 1 | bytes 1 | tf_op jit(solution)/shard_map/back_matmul/pallas_call | solution.py:191
  350.9 12.2 %outer_terms.4 = bf16[2048,1536]{1,0:T(8,128)(2,1)} custom-call(bf16[1024,2048]{1,0:T(8,128)(2,1)} %bitcast.40, bf16[1024,1536]{1,0:T(8,128)(2,1)} %get-tuple-element.378.b_ref.y_ref), custom_call_target="tpu_custom_call" | custom-call | flops 1 | bytes 1 | tf_op jit(solution)/shard_map/outer_terms/pallas_call | solution.py:211
  365.4 9.8 %convolution_convert_fusion.1 = bf16[1024,2048]{1,0:T(8,128)(2,1)S(1)} fusion(bf16[1024,1536]{1,0:T(8,128)(2,1)} %bitcast.82, bf16[1536,2048]{1,0:T(8,128)(2,1)} %get-tuple-element.381.weight_ref), kind=kOutput, calls=%fused_computation.2 | convolution fusion | flops 6444548096 | bytes 13631488 | tf_op jit(solution)/shard_map/mk,kn->mn/dot_general | solution.py:1181
  377.8 11.8 %collective-permute-done.1 = bf16[1,256,2048]{2,1,0:T(8,128)(2,1)S(1)} collective-permute-done((bf16[1,256,2048]{2,1,0:T(8,128)(2,1)S(1)}, bf16[1,256,2048]{2,1,0:T(8,128)(2,1)S(1)}, u32[]{:S(2)}, u32[]{:S(2)}) %collective-permute-start.1) | collective-permute-done | bytes 1048608 | tf_op jit(solution)/shard_map/ppermute | solution.py:1034
  390.5 5.9 norm_back.2
  397.5 12.1 %outer_terms.5.refs_0_ = bf16[2048,1536]{1,0:T(8,128)(2,1)} custom-call(bf16[1024,2048]{1,0:T(8,128)(2,1)} %bitcast.41, bf16[1024,1536]{1,0:T(8,128)(2,1)} %get-tuple-element.398.a_ref.y_ref), custom_call_target="tpu_custom_call" | custom-call | flops 1 | bytes 1 | tf_op jit(solution)/shard_map/outer_terms/pallas_call | solution.py:211
  409.6 11.2 %collective-permute-done.2 = bf16[1,256,2048]{2,1,0:T(8,128)(2,1)S(1)} collective-permute-done((bf16[1,256,2048]{2,1,0:T(8,128)(2,1)}, bf16[1,256,2048]{2,1,0:T(8,128)(2,1)S(1)}, u32[]{:S(2)}, u32[]{:S(2)}) %collective-permute-start.2) | collective-permute-done | bytes 1048608 | tf_op jit(solution)/shard_map/ppermute | solution.py:1034
  425.4 9.3 %pad_maximum_fusion = bf16[4,256,2048]{2,1,0:T(8,128)(2,1)S(1)} fusion(bf16[1,256,2048]{2,1,0:T(8,128)(2,1)S(1)} %get-tuple-element.565, bf16[1,256,2048]{2,1,0:T(8,128)(2,1)S(1)} %collective-permute-done.2, bf16[1,256,2048]{2,1,0:T(8,128)(2,1)S(1)} %get-tuple-element.564, bf16[1,256,2048]{2,1,0:T(8,128)(2,1)S(1)} %bitcast.57), kind=kLoop, calls=%fused_computation.1 | loop fusion | flops 6291456 | bytes 8388608 | tf_op jit(solution)/shard_map/concatenate | solution.py:1122
  439.6 19.7 %attention_back.1 = (bf16[4,256,768]{2,1,0:T(8,128)(2,1)}, bf16[4,256,768]{2,1,0:T(8,128)(2,1)}, f32[1,128]{1,0:T(1,128)}, f32[1,128]{1,0:T(1,128)}) custom-call(s32[2]{0:T(128)} %pad_add_fusion.place_ref, f32[4,256,768]{2,1,0:T(8,128)} %get-tuple-element.416.q_raw.k_raw, f32[4,256,768]{2,1,0:T(8,128)} %get-tuple-element.416.q_raw.k_raw, ...), custom_call_target="tpu_custom_call" | custom-call | flops 1 | bytes 1 | tf_op jit(solution)/shard_map/attention_back/pallas_call | solution.py:136
  459.5 4.5 halve.4
  464.0 11.6 %back_matmul.3 = (bf16[2,256,2048]{2,1,0:T(8,128)(2,1)}, bf16[2,256,2048]{2,1,0:T(8,128)(2,1)}) custom-call(bf16[1024,768]{1,0:T(8,128)(2,1)} %bitcast.48, bf16[1024,768]{1,0:T(8,128)(2,1)} %bitcast.46, bf16[2048,768]{1,0:T(8,128)(2,1)} %get-tuple-element.450.first_ref, bf16[2048,768]{1,0:T(8,128)(2,1)} %get-tuple-element.451.second_ref), custom_call_target="tpu_custom_call" | custom-call | flops 1 | bytes 1 | tf_op jit(solution)/shard_map/back_matmul/pallas_call | solution.py:191
  477.2 4.9 collective-permute-done.7.refs_2_
  482.2 7.0 out_terms.1.blocks_ref
  489.2 9.2 %outer_terms.6.refs_1_ = bf16[2048,768]{1,0:T(8,128)(2,1)} custom-call(bf16[1024,2048]{1,0:T(8,128)(2,1)} %bitcast.38, bf16[1024,768]{1,0:T(8,128)(2,1)} %bitcast.49), custom_call_target="tpu_custom_call" | custom-call | flops 1 | bytes 1 | tf_op jit(solution)/shard_map/outer_terms/pallas_call | solution.py:211
  508.3 9.2 %outer_terms.7.refs_2_ = bf16[2048,768]{1,0:T(8,128)(2,1)} custom-call(bf16[1024,2048]{1,0:T(8,128)(2,1)} %bitcast.39, bf16[1024,768]{1,0:T(8,128)(2,1)} %bitcast.47), custom_call_target="tpu_custom_call" | custom-call | flops 1 | bytes 1 | tf_op jit(solution)/shard_map/outer_terms/pallas_call | solution.py:211
  517.5 185.2 %reduce_all.1 = (bf16[4,256,1536]{2,1,0:T(8,128)(2,1)}, bf16[4,256,768]{2,1,0:T(8,128)(2,1)}, bf16[4,256,768]{2,1,0:T(8,128)(2,1)}, bf16[4,256,512]{2,1,0:T(8,128)(2,1)}) custom-call(bf16[4,512,512]{2,1,0:T(8,128)(2,1)} %out_terms.1.blocks_ref, bf16[2048,1536]{1,0:T(8,128)(2,1)} %outer_terms.5.refs_0_, bf16[2048,768]{1,0:T(8,128)(2,1)} %outer_terms.6.refs_1_, ...), custom_call_target="tpu_custom_call" | custom-call | flops 1 | bytes 1 | tf_op jit(solution)/shard_map/reduce_all/pallas_call | solution.py:982
  702.8 5.2 norm_back.3
  709.3 5.1 put_columns.2
  730.8 5.3 put_rows.1
  737.9 9.5 %put_strips.1 = f32[256,12288]{1,0:T(8,128)} custom-call(s32[2]{0:T(128)} %pad_add_fusion.place_ref, bf16[4,256,1536]{2,1,0:T(8,128)(2,1)} %get-tuple-element.545.refs_0_, bf16[1,256,1536]{2,1,0:T(8,128)(2,1)} %bitcast.59, bf16[1,256,1536]{2,1,0:T(8,128)(2,1)} %copy-done.6, bf16[2,256,1536]{2,1,0:T(8,128)(2,1)} %collective-permute-done.16.refs_3_), custom_call_target="tpu_custom_call" | custom-call | flops 1 | bytes 1 | tf_op jit(solution)/shard_map/put_strips/pallas_call | solution.py:293
  (105 shorter events, 69.2 us)
Async XLA Ops:
  7.2 431.4 %reduce-scatter.3.cloned.1.call-start = ((), (), s32[]{:S(2)}) async-start(), calls=%async_computation.2 | async-start | bytes 7077888 | tf_op jit(solution)/shard_map/reduce_scatter | solution.py:1291
  305.3 397.4 %reduce-scatter.5.cloned.1.call-start = ((), (), s32[]{:S(2)}) async-start(), calls=%async_computation.3 | async-start | bytes 7077888 | tf_op jit(solution)/shard_map/reduce_scatter | solution.py:1303
  340.9 4.4 collective-permute-start
  364.3 25.2 %collective-permute-start.1 = (bf16[1,256,2048]{2,1,0:T(8,128)(2,1)S(1)}, bf16[1,256,2048]{2,1,0:T(8,128)(2,1)S(1)}, u32[]{:S(2)}, u32[]{:S(2)}) collective-permute-start(bf16[1,256,2048]{2,1,0:T(8,128)(2,1)S(1)} %copy-done.20), channel_id=1, source_target_pairs={{0,2},{1,3},{2,0},{3,1},{4,6},{5,7},{6,4},{7,5},{8,10},{9,11},{10,... | collective-permute-start | bytes 3145736 | tf_op jit(solution)/shard_map/ppermute | solution.py:1034
  396.4 24.4 %copy-start.4 = (bf16[256,2048]{1,0:T(8,128)(2,1)S(1)}, bf16[256,2048]{1,0:T(8,128)(2,1)}, u32[]{:S(2)}) copy-start(bf16[256,2048]{1,0:T(8,128)(2,1)} %get-tuple-element.393) | copy-start | bytes 3145732
  396.4 24.4 %collective-permute-start.2 = (bf16[1,256,2048]{2,1,0:T(8,128)(2,1)}, bf16[1,256,2048]{2,1,0:T(8,128)(2,1)S(1)}, u32[]{:S(2)}, u32[]{:S(2)}) collective-permute-start(bf16[1,256,2048]{2,1,0:T(8,128)(2,1)} %bitcast.55), channel_id=1, source_target_pairs={{0,2},{1,3},{2,0},{3,1},{4,6},{5,7},{6,4},{7,5},{8,10},{9,11},{10,... | collective-permute-start | bytes 3145736 | tf_op jit(solution)/shard_map/ppermute | solution.py:1034
  421.0 4.2 collective-permute-start.3
  438.5 20.8 %collective-permute-start.4 = (bf16[2,256,2048]{2,1,0:T(8,128)(2,1)}, bf16[2,256,2048]{2,1,0:T(8,128)(2,1)}, u32[]{:S(2)}, u32[]{:S(2)}) collective-permute-start(bf16[2,256,2048]{2,1,0:T(8,128)(2,1)} %get-tuple-element.412), channel_id=1, source_target_pairs={{0,1},{1,0},{2,3},{3,2},{4,5},{5,4},{6,7},{7,6},{8,9},{9,8},{10,11... | collective-permute-start | bytes 6291464 | tf_op jit(solution)/shard_map/ppermute | solution.py:1034
  438.6 20.7 %collective-permute-start.5 = (bf16[1,192,2048]{2,1,0:T(8,128)(2,1)}, bf16[1,192,2048]{2,1,0:T(8,128)(2,1)S(1)}, u32[]{:S(2)}, u32[]{:S(2)}) collective-permute-start(bf16[1,192,2048]{2,1,0:T(8,128)(2,1)} %bitcast.61), channel_id=1, source_target_pairs={{0,2},{1,3},{2,0},{3,1},{4,6},{5,7},{6,4},{7,5},{8,10},{9,11},{10,... | collective-permute-start | bytes 2359304 | tf_op jit(solution)/shard_map/ppermute | solution.py:1034
  439.6 19.7 %copy-start.7 = (bf16[192,2048]{1,0:T(8,128)(2,1)S(1)}, bf16[192,2048]{1,0:T(8,128)(2,1)}, u32[]{:S(2)}) copy-start(bf16[192,2048]{1,0:T(8,128)(2,1)} %reduce-scatter.3.cloned.1.call-done) | copy-start | bytes 2359300
  475.6 25.8 %collective-permute-start.8 = (bf16[2,256,2048]{2,1,0:T(8,128)(2,1)}, bf16[2,256,2048]{2,1,0:T(8,128)(2,1)S(1)}, u32[]{:S(2)}, u32[]{:S(2)}) collective-permute-start(bf16[2,256,2048]{2,1,0:T(8,128)(2,1)} %get-tuple-element.456), channel_id=1, source_target_pairs={{0,1},{1,0},{2,3},{3,2},{4,5},{5,4},{6,7},{7,6},{8,9},{9,8},{10,11... | collective-permute-start | bytes 6291464 | tf_op jit(solution)/shard_map/ppermute | solution.py:1034
  475.8 6.3 collective-permute-start.7
  476.1 25.3 %collective-permute-start.6 = (bf16[1,256,2048]{2,1,0:T(8,128)(2,1)S(1)}, bf16[1,256,2048]{2,1,0:T(8,128)(2,1)S(1)}, u32[]{:S(2)}, u32[]{:S(2)}) collective-permute-start(bf16[1,256,2048]{2,1,0:T(8,128)(2,1)S(1)} %copy-done.19), channel_id=1, source_target_pairs={{0,2},{1,3},{2,0},{3,1},{4,6},{5,7},{6,4},{7,5},{8,10},{9,11},{10,... | collective-permute-start | bytes 3145736 | tf_op jit(solution)/shard_map/ppermute | solution.py:1034
  501.4 201.3 %copy-start.12 = (bf16[1,256,2048]{2,1,0:T(8,128)(2,1)}, bf16[1,256,2048]{2,1,0:T(8,128)(2,1)S(1)}, u32[]{:S(2)}) copy-start(bf16[1,256,2048]{2,1,0:T(8,128)(2,1)S(1)} %collective-permute-done.6) | copy-start | bytes 3145732
  507.2 195.6 %collective-permute-start.9 = (bf16[1,256,2048]{2,1,0:T(8,128)(2,1)}, bf16[1,256,2048]{2,1,0:T(8,128)(2,1)}, u32[]{:S(2)}, u32[]{:S(2)}) collective-permute-start(bf16[1,256,2048]{2,1,0:T(8,128)(2,1)} %get-tuple-element.473), channel_id=1, source_target_pairs={{0,2},{1,3},{2,0},{3,1},{4,6},{5,7},{6,4},{7,5},{8,10},{9,11},{10,... | collective-permute-start | bytes 3145736 | tf_op jit(solution)/shard_map/ppermute | solution.py:1034
  702.7 20.3 %collective-permute-start.12 = (bf16[1,256,1536]{2,1,0:T(8,128)(2,1)}, bf16[1,256,1536]{2,1,0:T(8,128)(2,1)S(1)}, u32[]{:S(2)}, u32[]{:S(2)}) collective-permute-start(bf16[1,256,1536]{2,1,0:T(8,128)(2,1)} %bitcast.58), channel_id=1, source_target_pairs={{0,2},{1,3},{2,0},{3,1},{4,6},{5,7},{6,4},{7,5},{8,10},{9,11},{10,... | collective-permute-start | bytes 2359304 | tf_op jit(solution)/shard_map/ppermute | solution.py:1034
  708.9 5.6 collective-permute-start.10
  714.4 8.8 %collective-permute-start.11 = (f32[4352]{0:T(1024)S(1)}, f32[4352]{0:T(1024)S(1)}, u32[]{:S(2)}, u32[]{:S(2)}) collective-permute-start(f32[4352]{0:T(1024)S(1)} %add.71), channel_id=1, source_target_pairs={{0,2},{1,3},{2,0},{3,1},{4,6},{5,7},{6,4},{7,5},{8,10},{9,11},{10,... | collective-permute-start | bytes 52232 | tf_op jit(solution)/shard_map/ppermute | solution.py:1034
  723.0 13.0 %copy-start.6 = (bf16[1,256,1536]{2,1,0:T(8,128)(2,1)}, bf16[1,256,1536]{2,1,0:T(8,128)(2,1)S(1)}, u32[]{:S(2)}) copy-start(bf16[1,256,1536]{2,1,0:T(8,128)(2,1)S(1)} %collective-permute-done.12.refs_2_) | copy-start | bytes 2359300
  723.4 14.5 %collective-permute-start.16 = (bf16[2,256,1536]{2,1,0:T(8,128)(2,1)S(1)}, bf16[2,256,1536]{2,1,0:T(8,128)(2,1)}, u32[]{:S(2)}, u32[]{:S(2)}) collective-permute-start(bf16[2,256,1536]{2,1,0:T(8,128)(2,1)S(1)} %pad_maximum_fusion.3), channel_id=1, source_target_pairs={{0,1},{1,0},{2,3},{3,2},{4,5},{5,4},{6,7},{7,6},{8,9},{9,8},{10,11... | collective-permute-start | bytes 4718600 | tf_op jit(solution)/shard_map/ppermute | solution.py:1034
  723.5 5.8 collective-permute-start.13
  729.3 6.8 collective-permute-start.14
  736.1 12.4 %copy-start.3 = (f32[256,2048]{1,0:T(8,128)S(1)}, f32[256,2048]{1,0:T(8,128)}, u32[]{:S(2)}) copy-start(f32[256,2048]{1,0:T(8,128)} %get-tuple-element.554.source_ref) | copy-start | bytes 6291460
  736.1 11.3 %collective-permute-start.15 = (f32[4352]{0:T(1024)S(1)}, f32[4352]{0:T(1024)S(1)}, u32[]{:S(2)}, u32[]{:S(2)}) collective-permute-start(f32[4352]{0:T(1024)S(1)} %add.74), channel_id=1, source_target_pairs={{0,16},{4,20},{8,24},{12,28},{16,0},{20,4},{24,8},{28,12},{1,17},{... | collective-permute-start | bytes 52232 | tf_op jit(solution)/shard_map/ppermute | solution.py:1034
  (16 other events, 91.4 us)
Sparse Core Ops, SparseCore 0:
  305.4 117.6 reduce-scatter.2
  427.3 129.7 reduce-scatter.4

commit v4 on v3

--- a/solution.py
+++ b/solution.py
@@ -174,24 +174,25 @@
 def back_matmul(a, b, first, second, rows):
     m, n = a.shape
     width = first.shape[0]
-    part = 256
+    part = 512
+    pairs = m // rows // 2
 
     def kernel(a_ref, b_ref, first_ref, second_ref, keep_ref, send_ref):
-        for at in range(0, width, part):
-            where = slice(at, at + part)
-            out = lax.dot_general(a_ref[...], first_ref[where], NT, preferred_element_type=jnp.float32)
-            out += lax.dot_general(b_ref[...], second_ref[where], NT, preferred_element_type=jnp.float32)
+        for pair in range(pairs):
+            at = slice(2 * pair * rows, (2 * pair + 2) * rows)
+            out = lax.dot_general(a_ref[at], first_ref[...], NT, preferred_element_type=jnp.float32)
+            out += lax.dot_general(b_ref[at], second_ref[...], NT, preferred_element_type=jnp.float32)
             out = out.astype(jnp.bfloat16)
-            keep_ref[0, :, where] = out[:rows]
-            send_ref[0, :, where] = out[rows:]
-
-    step = pl.BlockSpec((2 * rows, n), lambda i: (i, 0))
-    out = pl.BlockSpec((1, rows, width), lambda i: (i, 0, 0))
-    shape = jax.ShapeDtypeStruct((m // rows // 2, rows, width), jnp.bfloat16)
+            keep_ref[pair] = out[:rows]
+            send_ref[pair] = out[rows:]
+
+    weight = pl.BlockSpec((part, n), lambda i: (i, 0))
+    out = pl.BlockSpec((pairs, rows, part), lambda i: (0, 0, i))
+    shape = jax.ShapeDtypeStruct((pairs, rows, width), jnp.bfloat16)
     return pl.pallas_call(
         kernel,
-        grid=(m // rows // 2,),
-        in_specs=[step, step, steady(first.shape), steady(second.shape)],
+        grid=(width // part,),
+        in_specs=[steady((m, n)), steady((m, n)), weight, weight],
         out_specs=[out, out],
         out_shape=[shape, shape],
         compiler_params=params(),
@@ -203,6 +204,7 @@
 def outer_terms(x, y, count):
     m, width = x.shape
     n = y.shape[1]
+    count = count // 2
     depth = width // count
 
     def kernel(x_ref, y_ref, out_ref):
@@ -223,25 +225,28 @@
 def down_back(upstream, a, b, weight):
     m, width = upstream.shape
     n = a.shape[1]
-    rows = min(256, m)
+    tile = tile_of(n)
+    rows = min(512, m)
 
     def kernel(up_ref, a_ref, b_ref, weight_ref, gate_out, up_out):
-        grad = lax.dot_general(up_ref[...], weight_ref[...], NT, preferred_element_type=jnp.float32)
-        a, b = a_ref[...], b_ref[...]
-        sig = jax.nn.sigmoid(a)
-        gate_out[...] = (grad * b * sig * (1.0 + a * (1.0 - sig))).astype(jnp.bfloat16)
-        up_out[...] = (grad * a * sig).astype(jnp.bfloat16)
-
-    step = pl.BlockSpec((rows, n), lambda i: (i, 0))
+        for at in range(0, m, rows):
+            where = slice(at, at + rows)
+            grad = lax.dot_general(up_ref[where], weight_ref[...], NT, preferred_element_type=jnp.float32)
+            a, b = a_ref[where], b_ref[where]
+            sig = jax.nn.sigmoid(a)
+            gate_out[where] = (grad * b * sig * (1.0 + a * (1.0 - sig))).astype(jnp.bfloat16)
+            up_out[where] = (grad * a * sig).astype(jnp.bfloat16)
+
+    step = pl.BlockSpec((m, tile), lambda i: (0, i))
     shape = jax.ShapeDtypeStruct((m, n), jnp.bfloat16)
     return pl.pallas_call(
         kernel,
-        grid=(m // rows,),
-        in_specs=[pl.BlockSpec((rows, width), lambda i: (i, 0)), step, step, steady((n, width))],
+        grid=(n // tile,),
+        in_specs=[steady((m, width)), step, step, pl.BlockSpec((tile, width), lambda i: (i, 0))],
         out_specs=[step, step],
         out_shape=[shape, shape],
         compiler_params=params(),
-        cost_estimate=cost(2 * m * n * width, 2 * m * width + 12 * m * n + 2 * n * width),
+        cost_estimate=cost(),
         name="down_back",
     )(upstream, a, b, weight)
 
@@ -880,11 +885,13 @@
 
 
 def reduce_kernel(n_dp, n_u, count, blocks_ref, *refs):
-    terms, outs = list(refs[: count - 1]), refs[count - 1 : 2 * count - 1]
+    given, outs = list(refs[: count - 1]), refs[count - 1 : 2 * count - 1]
     refs = refs[2 * count - 1 :]
-    slots, sums = refs[:count], refs[count : 2 * count]
-    out_terms_ref, ring_send, ring_recv, cube_send, cube_recv, turn_send, turn_recv, local = refs[2 * count :]
-    terms.append(out_terms_ref)
+    slots, sums, terms = refs[:count], refs[count : 2 * count], refs[2 * count : 3 * count]
+    ring_send, ring_recv, cube_send, cube_recv, turn_send, turn_recv, local = refs[3 * count :]
+    out_terms_ref = terms[-1]
+    given.append(out_terms_ref)
+    loads = {c: pltpu.make_async_copy(given[c], terms[c], local.at[count + 1 + c]) for c in range(count - 1)}
     group = Group(n_dp, n_u)
     group.greet()
     copies = {}
@@ -916,8 +923,10 @@
         offset = (reach - step) if way == 0 else (step - reach)
         if step == 0:
             r = sums[c].shape[0]
-            source = terms[c].at[pl.ds(pl.multiple_of(group.owner(offset) * r, r), r)]
+            source = given[c].at[pl.ds(pl.multiple_of(group.owner(offset) * r, r), r)]
         else:
+            if c in loads:
+                loads.pop(c).wait()
             source = slot(c, way, step - 1)
             add(c, source, offset, [source])
         sems = (c, way, step)
@@ -930,6 +939,8 @@
 
     phases = [(0, 1), (2, 3)]
     start(phases[0])
+    for copy in loads.values():
+        copy.start()
     turns = []
     for k in range(1, n_u):
         turns.append(group.to_cube(k, blocks_ref.at[k], here, turn_send.at[k - 1], turn_recv.at[k - 1]))
@@ -981,15 +992,19 @@
     dma = pltpu.SemaphoreType.DMA
     return pl.pallas_call(
         functools.partial(reduce_kernel, n_dp, n_u, count),
-        in_specs=[local] * count,
+        in_specs=[anywhere] * count,
         out_specs=[anywhere] * count,
         out_shape=[jax.ShapeDtypeStruct((n_u,) + b, jnp.bfloat16) for b in sizes],
         scratch_shapes=[pltpu.VMEM((2, longest) + b, jnp.bfloat16) for b in sizes]
         + [pltpu.VMEM(b, jnp.bfloat16) for b in sizes]
         + [
+            pltpu.VMEM(t.shape, jnp.bfloat16)
+            for t in terms
+        ]
+        + [
             pltpu.VMEM(whole, jnp.bfloat16),
             dma((count, 2, longest)), dma((count, 2, longest)), dma((count, n_u - 1)), dma((count, n_u - 1)),
-            dma((n_u - 1,)), dma((n_u - 1,)), dma((count + 1,)),
+            dma((n_u - 1,)), dma((n_u - 1,)), dma((2 * count,)),
         ],
         compiler_params=pltpu.CompilerParams(vmem_limit_bytes=VMEM_LIMIT, collective_id=1, has_side_effects=True),
         cost_estimate=cost(),
@@ -998,7 +1013,7 @@
 
 
 START = 0.9
-LATENCY = 2.0
+LATENCY = 6.0
 RATES = {"ring": 50.0, "x": 50.0, "core": 250.0}
 
 

time: 768 us -> 767 us (level)
  other arithmetic: 17.2 us -> 8.44 us
    concatenate x1, other arithmetic: 9.32 us -> 0.57 us  [joined(): jnp.concatenate([b[at][sub:sub + 1] for _, at, sub in order])]
    pallas_call x1, Pallas kernels: 19.7 us -> 28.2 us  [attend_back(): pl.pallas_call(functools.partial(attend_back_kernel, min(256, bucket), co...]
  transfers between devices with their start and end apart: 19 -> 19, of which waited for: 9 -> 9; matrix products, arithmetic and copies ran while one was open for 4% -> 3% of each run, Pallas kernels for 46% -> 46%
where the time goes in v4:
time: 767 us; the launch traced here: 758 us
  Pallas kernels  630 us (82%)
  waiting for transfers between devices  49.8 us (6%)
  matrix products  25 us (3%)
  between operations  15.3 us (2%)
  local copies, waits for them, and re-layouts  14.7 us (2%)
  starting transfers between devices  14.3 us (2%)
  other arithmetic  8.44 us (1%)
    pallas_call x1, Pallas kernels, forward(): pl.pallas_call(functools.partial(forward_kernel, n_dp, n_u, heads, kv_hea...  274 us
    pallas_call x1, Pallas kernels, reduce_all(): pl.pallas_call(functools.partial(reduce_kernel, n_dp, n_u, count), in_spe...  188 us
    ppermute x17, waiting for transfers between devices, fly(): got = lax.ppermute(value, axis, pairs)  49.7 us
    pallas_call x4, Pallas kernels, outer_terms(): pl.pallas_call(kernel, grid=(count,), in_specs=[pl.BlockSpec((m, depth),...  36.2 us
    pallas_call x2, Pallas kernels, back_matmul(): pl.pallas_call(kernel, grid=(width // part,), in_specs=[steady((m, n)), s...  29.6 us
    pallas_call x1, Pallas kernels, attend_back(): pl.pallas_call(functools.partial(attend_back_kernel, min(256, bucket), co...  28.2 us
    pallas_call x4, Pallas kernels, put_call(): pl.pallas_call(body, grid=(grid,), in_specs=[pl.BlockSpec(memory_space=pl...  23.5 us
    pallas_call x1, Pallas kernels, down_back(): pl.pallas_call(kernel, grid=(n // tile,), in_specs=[steady((m, width)), s...  15.9 us
  transfers between devices with their start and end apart: 19, of which 9 were waited for; matrix products, arithmetic and copies ran while one was open for 3% of the time, Pallas kernels for 46%

profile of v4, /device:TPU:0, one launch (start us, length us, event | category | flops | bytes accessed | tf_op | source)
XLA Modules:
  0.0 758.0 jit_solution(1369754519978308528)
XLA Ops:
  8.7 4.8 take_strips.1
  20.0 273.7 %forward.1 = (bf16[2048,768]{1,0:T(8,128)(2,1)}, bf16[2048,768]{1,0:T(8,128)(2,1)}, bf16[2048,1536]{1,0:T(8,128)(2,1)}, bf16[2048,1536]{1,0:T(8,128)(2,1)}, bf16...) custom-call(s32[1]{0:T(128)} %copy.23.length_ref, ...), custom_call_target="tpu_custom_call" | custom-call | flops 1 | bytes 1 | tf_op jit(solution)/shard_map/forward/pallas_call | solution.py:859
  293.7 11.6 %convolution_convert_fusion = bf16[1536,2048]{1,0:T(8,128)(2,1)} fusion(bf16[1024,1536]{1,0:T(8,128)(2,1)} %bitcast.82, bf16[1024,2048]{1,0:T(8,128)(2,1)} %bitcast.51), kind=kOutput, calls=%fused_computation | convolution fusion | flops 6445596672 | bytes 13631488 | tf_op jit(solution)/shard_map/km,kn->mn/dot_general | solution.py:1204
  305.3 15.9 %down_back.1 = (bf16[1024,1536]{1,0:T(8,128)(2,1)}, bf16[1024,1536]{1,0:T(8,128)(2,1)}) custom-call(bf16[1024,2048]{1,0:T(8,128)(2,1)} %bitcast.52, f32[1024,1536]{1,0:T(8,128)} %bitcast.44, f32[1024,1536]{1,0:T(8,128)} %bitcast.45, bf16[1536,2048]{1,0:T(8,128)(2,1)} %get-tuple-element.381.weight_ref), custom_call_target="tpu_custom_call" | custom-call | flops 1 | bytes 1 | tf_op jit(solution)/shard_map/down_back/pallas_call | solution.py:242
  321.3 18.6 %back_matmul.2 = (bf16[2,256,2048]{2,1,0:T(8,128)(2,1)}, bf16[2,256,2048]{2,1,0:T(8,128)(2,1)}) custom-call(bf16[1024,1536]{1,0:T(8,128)(2,1)} %get-tuple-element.398.a_ref.y_ref, bf16[1024,1536]{1,0:T(8,128)(2,1)} %get-tuple-element.378.b_ref.y_ref, bf16[2048,1536]{1,0:T(8,128)(2,1)} %get-tuple-element.362.first_ref, ...), custom_call_target="tpu_custom_call" | custom-call | flops 1 | bytes 1 | tf_op jit(solution)/shard_map/back_matmul/pallas_call | solution.py:192
  349.9 10.7 %outer_terms.4 = bf16[2048,1536]{1,0:T(8,128)(2,1)} custom-call(bf16[1024,2048]{1,0:T(8,128)(2,1)} %bitcast.40, bf16[1024,1536]{1,0:T(8,128)(2,1)} %get-tuple-element.378.b_ref.y_ref), custom_call_target="tpu_custom_call" | custom-call | flops 1 | bytes 1 | tf_op jit(solution)/shard_map/outer_terms/pallas_call | solution.py:213
  362.7 9.8 %convolution_convert_fusion.1 = bf16[1024,2048]{1,0:T(8,128)(2,1)S(1)} fusion(bf16[1024,1536]{1,0:T(8,128)(2,1)} %bitcast.83, bf16[1536,2048]{1,0:T(8,128)(2,1)} %get-tuple-element.381.weight_ref), kind=kOutput, calls=%fused_computation.2 | convolution fusion | flops 6444548096 | bytes 13631488 | tf_op jit(solution)/shard_map/mk,kn->mn/dot_general | solution.py:1196
  375.0 12.1 %collective-permute-done.1 = bf16[1,256,2048]{2,1,0:T(8,128)(2,1)S(1)} collective-permute-done((bf16[1,256,2048]{2,1,0:T(8,128)(2,1)S(1)}, bf16[1,256,2048]{2,1,0:T(8,128)(2,1)S(1)}, u32[]{:S(2)}, u32[]{:S(2)}) %collective-permute-start.1) | collective-permute-done | bytes 1048608 | tf_op jit(solution)/shard_map/ppermute | solution.py:1049
  388.1 5.6 norm_back.2
  394.5 10.7 %outer_terms.5.refs_0_ = bf16[2048,1536]{1,0:T(8,128)(2,1)} custom-call(bf16[1024,2048]{1,0:T(8,128)(2,1)} %bitcast.41, bf16[1024,1536]{1,0:T(8,128)(2,1)} %get-tuple-element.398.a_ref.y_ref), custom_call_target="tpu_custom_call" | custom-call | flops 1 | bytes 1 | tf_op jit(solution)/shard_map/outer_terms/pallas_call | solution.py:213
  405.2 13.1 %collective-permute-done.2 = bf16[1,256,2048]{2,1,0:T(8,128)(2,1)S(1)} collective-permute-done((bf16[1,256,2048]{2,1,0:T(8,128)(2,1)}, bf16[1,256,2048]{2,1,0:T(8,128)(2,1)S(1)}, u32[]{:S(2)}, u32[]{:S(2)}) %collective-permute-start.2) | collective-permute-done | bytes 1048608 | tf_op jit(solution)/shard_map/ppermute | solution.py:1049
  429.3 28.2 %attention_back.1 = (bf16[4,256,768]{2,1,0:T(8,128)(2,1)}, bf16[4,256,768]{2,1,0:T(8,128)(2,1)}, f32[1,128]{1,0:T(1,128)}, f32[1,128]{1,0:T(1,128)}) custom-call(s32[2]{0:T(128)} %pad_add_fusion.place_ref, f32[4,256,768]{2,1,0:T(8,128)} %get-tuple-element.416.q_raw.k_raw, f32[4,256,768]{2,1,0:T(8,128)} %get-tuple-element.416.q_raw.k_raw, ...), custom_call_target="tpu_custom_call" | custom-call | flops 1 | bytes 1 | tf_op jit(solution)/shard_map/attention_back/pallas_call | solution.py:136
  457.5 4.5 halve.4
  462.1 11.0 %back_matmul.3 = (bf16[2,256,2048]{2,1,0:T(8,128)(2,1)}, bf16[2,256,2048]{2,1,0:T(8,128)(2,1)}) custom-call(bf16[1024,768]{1,0:T(8,128)(2,1)} %bitcast.48, bf16[1024,768]{1,0:T(8,128)(2,1)} %bitcast.46, bf16[2048,768]{1,0:T(8,128)(2,1)} %get-tuple-element.450.first_ref, bf16[2048,768]{1,0:T(8,128)(2,1)} %get-tuple-element.451.second_ref), custom_call_target="tpu_custom_call" | custom-call | flops 1 | bytes 1 | tf_op jit(solution)/shard_map/back_matmul/pallas_call | solution.py:192
  474.8 4.9 collective-permute-done.7.refs_2_
  479.7 6.8 out_terms.1.blocks_ref
  486.5 7.3 outer_terms.6.refs_1_
  493.8 5.0 collective-permute-done.5
  505.7 7.4 outer_terms.7.refs_2_
  513.1 187.6 %reduce_all.1 = (bf16[4,256,1536]{2,1,0:T(8,128)(2,1)}, bf16[4,256,768]{2,1,0:T(8,128)(2,1)}, bf16[4,256,768]{2,1,0:T(8,128)(2,1)}, bf16[4,256,512]{2,1,0:T(8,128)(2,1)}) custom-call(bf16[4,512,512]{2,1,0:T(8,128)(2,1)} %out_terms.1.blocks_ref, bf16[2048,1536]{1,0:T(8,128)(2,1)} %outer_terms.5.refs_0_, bf16[2048,768]{1,0:T(8,128)(2,1)} %outer_terms.6.refs_1_, ...), custom_call_target="tpu_custom_call" | custom-call | flops 1 | bytes 1 | tf_op jit(solution)/shard_map/reduce_all/pallas_call | solution.py:993
  703.9 5.5 norm_back.3
  710.3 5.1 put_columns.2
  719.1 5.3 put_rows.1
  735.6 9.5 %put_strips.1 = f32[256,12288]{1,0:T(8,128)} custom-call(s32[2]{0:T(128)} %pad_add_fusion.place_ref, bf16[4,256,1536]{2,1,0:T(8,128)(2,1)} %get-tuple-element.540.refs_0_, bf16[1,256,1536]{2,1,0:T(8,128)(2,1)} %bitcast.59, bf16[1,256,1536]{2,1,0:T(8,128)(2,1)} %copy-done.6, bf16[2,256,1536]{2,1,0:T(8,128)(2,1)} %collective-permute-done.15.refs_3_), custom_call_target="tpu_custom_call" | custom-call | flops 1 | bytes 1 | tf_op jit(solution)/shard_map/put_strips/pallas_call | solution.py:298
  (107 shorter events, 68.3 us)
Async XLA Ops:
  7.2 421.2 %reduce-scatter.3.cloned.1.call-start = ((), (), s32[]{:S(2)}) async-start(), calls=%async_computation.2 | async-start | bytes 7077888 | tf_op jit(solution)/shard_map/reduce_scatter | solution.py:1306
  305.3 395.5 %reduce-scatter.5.cloned.1.call-start = ((), (), s32[]{:S(2)}) async-start(), calls=%async_computation.3 | async-start | bytes 7077888 | tf_op jit(solution)/shard_map/reduce_scatter | solution.py:1318
  339.8 4.4 collective-permute-start
  361.9 25.2 %collective-permute-start.1 = (bf16[1,256,2048]{2,1,0:T(8,128)(2,1)S(1)}, bf16[1,256,2048]{2,1,0:T(8,128)(2,1)S(1)}, u32[]{:S(2)}, u32[]{:S(2)}) collective-permute-start(bf16[1,256,2048]{2,1,0:T(8,128)(2,1)S(1)} %copy-done.21), channel_id=1, source_target_pairs={{0,2},{1,3},{2,0},{3,1},{4,6},{5,7},{6,4},{7,5},{8,10},{9,11},{10,... | collective-permute-start | bytes 3145736 | tf_op jit(solution)/shard_map/ppermute | solution.py:1049
  393.6 24.7 %copy-start.4 = (bf16[256,2048]{1,0:T(8,128)(2,1)S(1)}, bf16[256,2048]{1,0:T(8,128)(2,1)}, u32[]{:S(2)}) copy-start(bf16[256,2048]{1,0:T(8,128)(2,1)} %get-tuple-element.393) | copy-start | bytes 3145732
  393.6 24.7 %collective-permute-start.2 = (bf16[1,256,2048]{2,1,0:T(8,128)(2,1)}, bf16[1,256,2048]{2,1,0:T(8,128)(2,1)S(1)}, u32[]{:S(2)}, u32[]{:S(2)}) collective-permute-start(bf16[1,256,2048]{2,1,0:T(8,128)(2,1)} %bitcast.55), channel_id=1, source_target_pairs={{0,2},{1,3},{2,0},{3,1},{4,6},{5,7},{6,4},{7,5},{8,10},{9,11},{10,... | collective-permute-start | bytes 3145736 | tf_op jit(solution)/shard_map/ppermute | solution.py:1049
  418.5 4.2 collective-permute-start.3
  428.2 29.2 %collective-permute-start.4 = (bf16[2,256,2048]{2,1,0:T(8,128)(2,1)}, bf16[2,256,2048]{2,1,0:T(8,128)(2,1)}, u32[]{:S(2)}, u32[]{:S(2)}) collective-permute-start(bf16[2,256,2048]{2,1,0:T(8,128)(2,1)} %get-tuple-element.412), channel_id=1, source_target_pairs={{0,1},{1,0},{2,3},{3,2},{4,5},{5,4},{6,7},{7,6},{8,9},{9,8},{10,11... | collective-permute-start | bytes 6291464 | tf_op jit(solution)/shard_map/ppermute | solution.py:1049
  428.4 33.5 %collective-permute-start.6 = (bf16[1,192,2048]{2,1,0:T(8,128)(2,1)}, bf16[1,192,2048]{2,1,0:T(8,128)(2,1)S(1)}, u32[]{:S(2)}, u32[]{:S(2)}) collective-permute-start(bf16[1,192,2048]{2,1,0:T(8,128)(2,1)} %bitcast.61), channel_id=1, source_target_pairs={{0,2},{1,3},{2,0},{3,1},{4,6},{5,7},{6,4},{7,5},{8,10},{9,11},{10,... | collective-permute-start | bytes 2359304 | tf_op jit(solution)/shard_map/ppermute | solution.py:1049
  462.1 11.6 %copy-start.20 = (bf16[1,256,2048]{2,1,0:T(8,128)(2,1)S(1)}, bf16[1,256,2048]{2,1,0:T(8,128)(2,1)}, u32[]{:S(2)}) copy-start(bf16[1,256,2048]{2,1,0:T(8,128)(2,1)} %get-tuple-element.443) | copy-start | bytes 3145732
  473.1 25.7 %collective-permute-start.8 = (bf16[2,256,2048]{2,1,0:T(8,128)(2,1)}, bf16[2,256,2048]{2,1,0:T(8,128)(2,1)S(1)}, u32[]{:S(2)}, u32[]{:S(2)}) collective-permute-start(bf16[2,256,2048]{2,1,0:T(8,128)(2,1)} %get-tuple-element.456), channel_id=1, source_target_pairs={{0,1},{1,0},{2,3},{3,2},{4,5},{5,4},{6,7},{7,6},{8,9},{9,8},{10,11... | collective-permute-start | bytes 6291464 | tf_op jit(solution)/shard_map/ppermute | solution.py:1049
  473.2 6.5 collective-permute-start.7
  473.6 25.1 %collective-permute-start.5 = (bf16[1,256,2048]{2,1,0:T(8,128)(2,1)S(1)}, bf16[1,256,2048]{2,1,0:T(8,128)(2,1)S(1)}, u32[]{:S(2)}, u32[]{:S(2)}) collective-permute-start(bf16[1,256,2048]{2,1,0:T(8,128)(2,1)S(1)} %copy-done.20), channel_id=1, source_target_pairs={{0,2},{1,3},{2,0},{3,1},{4,6},{5,7},{6,4},{7,5},{8,10},{9,11},{10,... | collective-permute-start | bytes 3145736 | tf_op jit(solution)/shard_map/ppermute | solution.py:1049
  498.8 202.0 %copy-start.12 = (bf16[1,256,2048]{2,1,0:T(8,128)(2,1)}, bf16[1,256,2048]{2,1,0:T(8,128)(2,1)S(1)}, u32[]{:S(2)}) copy-start(bf16[1,256,2048]{2,1,0:T(8,128)(2,1)S(1)} %collective-permute-done.5) | copy-start | bytes 3145732
  504.6 198.4 %collective-permute-start.9 = (bf16[1,256,2048]{2,1,0:T(8,128)(2,1)}, bf16[1,256,2048]{2,1,0:T(8,128)(2,1)S(1)}, u32[]{:S(2)}, u32[]{:S(2)}) collective-permute-start(bf16[1,256,2048]{2,1,0:T(8,128)(2,1)} %get-tuple-element.473), channel_id=1, source_target_pairs={{0,2},{1,3},{2,0},{3,1},{4,6},{5,7},{6,4},{7,5},{8,10},{9,11},{10,... | collective-permute-start | bytes 3145736 | tf_op jit(solution)/shard_map/ppermute | solution.py:1049
  700.8 23.6 %collective-permute-start.12 = (bf16[1,256,1536]{2,1,0:T(8,128)(2,1)}, bf16[1,256,1536]{2,1,0:T(8,128)(2,1)S(1)}, u32[]{:S(2)}, u32[]{:S(2)}) collective-permute-start(bf16[1,256,1536]{2,1,0:T(8,128)(2,1)} %bitcast.58), channel_id=1, source_target_pairs={{0,2},{1,3},{2,0},{3,1},{4,6},{5,7},{6,4},{7,5},{8,10},{9,11},{10,... | collective-permute-start | bytes 2359304 | tf_op jit(solution)/shard_map/ppermute | solution.py:1049
  710.2 8.9 %collective-permute-start.10 = (f32[4352]{0:T(1024)S(1)}, f32[4352]{0:T(1024)S(1)}, u32[]{:S(2)}, u32[]{:S(2)}) collective-permute-start(f32[4352]{0:T(1024)S(1)} %maximum_reduce_fusion), channel_id=1, source_target_pairs={{0,1},{1,0},{2,3},{3,2},{4,5},{5,4},{6,7},{7,6},{8,9},{9,8},{10,11... | collective-permute-start | bytes 52232 | tf_op jit(solution)/shard_map/ppermute | solution.py:1049
  724.6 11.0 %collective-permute-start.15 = (bf16[2,256,1536]{2,1,0:T(8,128)(2,1)S(1)}, bf16[2,256,1536]{2,1,0:T(8,128)(2,1)}, u32[]{:S(2)}, u32[]{:S(2)}) collective-permute-start(bf16[2,256,1536]{2,1,0:T(8,128)(2,1)S(1)} %pad_maximum_fusion.3), channel_id=1, source_target_pairs={{0,1},{1,0},{2,3},{3,2},{4,5},{5,4},{6,7},{7,6},{8,9},{9,8},{10,11... | collective-permute-start | bytes 4718600 | tf_op jit(solution)/shard_map/ppermute | solution.py:1049
  725.1 3.8 collective-permute-start.11
  728.9 5.4 collective-permute-start.13
  734.3 11.6 %copy-start.3 = (f32[256,2048]{1,0:T(8,128)S(1)}, f32[256,2048]{1,0:T(8,128)}, u32[]{:S(2)}) copy-start(f32[256,2048]{1,0:T(8,128)} %get-tuple-element.550.source_ref) | copy-start | bytes 6291460
  734.3 11.6 %copy-start.9 = (f32[1,256,2048]{2,1,0:T(8,128)S(1)}, f32[1,256,2048]{2,1,0:T(8,128)}, u32[]{:S(2)}) copy-start(f32[1,256,2048]{2,1,0:T(8,128)} %get-tuple-element.441) | copy-start | bytes 6291460
  734.3 10.8 %collective-permute-start.14 = (f32[4352]{0:T(1024)S(1)}, f32[4352]{0:T(1024)S(1)}, u32[]{:S(2)}, u32[]{:S(2)}) collective-permute-start(f32[4352]{0:T(1024)S(1)} %add.73), channel_id=1, source_target_pairs={{0,8},{4,12},{8,0},{12,4},{16,24},{20,28},{24,16},{28,20},{1,9},{5... | collective-permute-start | bytes 52232 | tf_op jit(solution)/shard_map/ppermute | solution.py:1049
  745.1 4.7 collective-permute-start.16
  (17 other events, 82.3 us)
Sparse Core Ops, SparseCore 0:
  305.4 117.6 reduce-scatter.2
  427.2 139.4 reduce-scatter.4

commit v5 on v4

--- a/solution.py
+++ b/solution.py
@@ -1304,7 +1304,7 @@
 
     act_gate, act_up, hidden = (v.reshape(bucket, ff_local) for v in (act_gate, act_up, hidden))
     down_own = lax.psum_scatter(
-        seq.run(10.7, lambda h, g: low(dot_tn(h, g)), hidden, grad_result), "dp", scatter_dimension=0, tiled=True
+        seq.run(10.7, lambda h, g: outer_terms(h, g, 6), hidden, grad_result), "dp", scatter_dimension=0, tiled=True
     )
 
     grad_gate, grad_up = seq.run(15.5, down_back, grad_result, act_gate, act_up, w_down)
@@ -1338,8 +1338,8 @@
     grad_qk, grad_vg = grad_qk.reshape(bucket, -1), grad_vg.reshape(bucket, -1)
     one_keep, one_send = seq.run(12.0, input_grads, grad_qk, grad_vg, w_qk, w_vg)
     t_one = task(cube.reduce(one_keep, one_send))
-    out_parts = seq.run(7.0, lambda p, a, b: out_terms(p, a, b, n_u), place, gated, branch_grad)
-    qk_terms = seq.run(9.3, lambda a, b: outer_terms(a, b, n_dp), normed, grad_qk)
+    out_parts = seq.run(7.0, lambda p, a, b: out_terms(p, a, b, n_u), place, gated, branch_grad, take=False)
+    qk_terms = seq.run(9.3, lambda a, b: outer_terms(a, b, n_dp), normed, grad_qk, take=False)
     vg_terms = seq.run(9.3, lambda a, b: outer_terms(a, b, n_dp), normed, grad_vg)
 
     gate_all, qk_all, vg_all, out_all = seq.run(

time: 767 us -> 759 us (0.990)
  matrix products: 25 us -> 12.5 us
    dot_general x1 -> x0, matrix products: 11.6 us -> none  [dot_tn(): return jnp.einsum('km,kn->mn', a, b, preferred_element_type=jnp.float32)]
    pallas_call x4 -> x5, Pallas kernels: 36.2 us -> 47.2 us  [outer_terms(): pl.pallas_call(kernel, grid=(count,), in_specs=[pl.BlockSpec((m, depth),...]
    pallas_call x1, Pallas kernels: 28.2 us -> 19.8 us  [attend_back(): pl.pallas_call(functools.partial(attend_back_kernel, min(256, bucket), co...]
  transfers between devices with their start and end apart: 19 -> 19, of which waited for: 9 -> 8; matrix products, arithmetic and copies ran while one was open for 3% -> 3% of each run, Pallas kernels for 46% -> 46%
where the time goes in v5:
time: 759 us; the launch traced here: 749 us
  Pallas kernels  634 us (84%)
  waiting for transfers between devices  48.4 us (6%)
  starting transfers between devices  15.7 us (2%)
  between operations  15.6 us (2%)
  local copies, waits for them, and re-layouts  14.8 us (2%)
  matrix products  12.5 us (2%)
  other arithmetic  8.44 us (1%)
    pallas_call x1, Pallas kernels, forward(): pl.pallas_call(functools.partial(forward_kernel, n_dp, n_u, heads, kv_hea...  274 us
    pallas_call x1, Pallas kernels, reduce_all(): pl.pallas_call(functools.partial(reduce_kernel, n_dp, n_u, count), in_spe...  188 us
    ppermute x17, waiting for transfers between devices, fly(): got = lax.ppermute(value, axis, pairs)  48.3 us
    pallas_call x5, Pallas kernels, outer_terms(): pl.pallas_call(kernel, grid=(count,), in_specs=[pl.BlockSpec((m, depth),...  47.2 us
    pallas_call x2, Pallas kernels, back_matmul(): pl.pallas_call(kernel, grid=(width // part,), in_specs=[steady((m, n)), s...  29.4 us
    pallas_call x4, Pallas kernels, put_call(): pl.pallas_call(body, grid=(grid,), in_specs=[pl.BlockSpec(memory_space=pl...  23.5 us
    pallas_call x1, Pallas kernels, attend_back(): pl.pallas_call(functools.partial(attend_back_kernel, min(256, bucket), co...  19.8 us
    pallas_call x1, Pallas kernels, down_back(): pl.pallas_call(kernel, grid=(n // tile,), in_specs=[steady((m, width)), s...  16.1 us
  transfers between devices with their start and end apart: 19, of which 8 were waited for; matrix products, arithmetic and copies ran while one was open for 3% of the time, Pallas kernels for 46%

profile of v5, /device:TPU:0, one launch (start us, length us, event | category | flops | bytes accessed | tf_op | source)
XLA Modules:
  0.0 749.4 jit_solution(3362757414049565356)
XLA Ops:
  8.7 4.8 take_strips.1
  20.0 273.7 %forward.1 = (bf16[2048,768]{1,0:T(8,128)(2,1)}, bf16[2048,768]{1,0:T(8,128)(2,1)}, bf16[2048,1536]{1,0:T(8,128)(2,1)}, bf16[2048,1536]{1,0:T(8,128)(2,1)}, bf16...) custom-call(s32[1]{0:T(128)} %copy.23.length_ref, ...), custom_call_target="tpu_custom_call" | custom-call | flops 1 | bytes 1 | tf_op jit(solution)/shard_map/forward/pallas_call | solution.py:859
  293.7 11.0 %outer_terms.5 = bf16[1536,2048]{1,0:T(8,128)(2,1)} custom-call(bf16[1024,1536]{1,0:T(8,128)(2,1)} %bitcast.62, bf16[1024,2048]{1,0:T(8,128)(2,1)} %bitcast.42), custom_call_target="tpu_custom_call" | custom-call | flops 1 | bytes 1 | tf_op jit(solution)/shard_map/outer_terms/pallas_call | solution.py:213
  304.9 16.1 %down_back.1 = (bf16[1024,1536]{1,0:T(8,128)(2,1)}, bf16[1024,1536]{1,0:T(8,128)(2,1)}) custom-call(bf16[1024,2048]{1,0:T(8,128)(2,1)} %bitcast.43, f32[1024,1536]{1,0:T(8,128)} %bitcast.44, f32[1024,1536]{1,0:T(8,128)} %bitcast.45, bf16[1536,2048]{1,0:T(8,128)(2,1)} %get-tuple-element.381.weight_ref), custom_call_target="tpu_custom_call" | custom-call | flops 1 | bytes 1 | tf_op jit(solution)/shard_map/down_back/pallas_call | solution.py:242
  321.0 18.6 %back_matmul.2 = (bf16[2,256,2048]{2,1,0:T(8,128)(2,1)}, bf16[2,256,2048]{2,1,0:T(8,128)(2,1)}) custom-call(bf16[1024,1536]{1,0:T(8,128)(2,1)} %get-tuple-element.398.a_ref.y_ref, bf16[1024,1536]{1,0:T(8,128)(2,1)} %get-tuple-element.378.b_ref.y_ref, bf16[2048,1536]{1,0:T(8,128)(2,1)} %get-tuple-element.362.first_ref, ...), custom_call_target="tpu_custom_call" | custom-call | flops 1 | bytes 1 | tf_op jit(solution)/shard_map/back_matmul/pallas_call | solution.py:192
  349.7 10.7 %outer_terms.6 = bf16[2048,1536]{1,0:T(8,128)(2,1)} custom-call(bf16[1024,2048]{1,0:T(8,128)(2,1)} %bitcast.38, bf16[1024,1536]{1,0:T(8,128)(2,1)} %get-tuple-element.378.b_ref.y_ref), custom_call_target="tpu_custom_call" | custom-call | flops 1 | bytes 1 | tf_op jit(solution)/shard_map/outer_terms/pallas_call | solution.py:213
  362.3 8.8 %convolution_convert_fusion = bf16[1024,2048]{1,0:T(8,128)(2,1)S(1)} fusion(bf16[1024,1536]{1,0:T(8,128)(2,1)S(1)} %bitcast.63, bf16[1536,2048]{1,0:T(8,128)(2,1)} %get-tuple-element.381.weight_ref), kind=kOutput, calls=%fused_computation.1 | convolution fusion | flops 6444548096 | bytes 13631488 | tf_op jit(solution)/shard_map/mk,kn->mn/dot_general | solution.py:1196
  373.6 12.3 %collective-permute-done.1 = bf16[1,256,2048]{2,1,0:T(8,128)(2,1)S(1)} collective-permute-done((bf16[1,256,2048]{2,1,0:T(8,128)(2,1)}, bf16[1,256,2048]{2,1,0:T(8,128)(2,1)S(1)}, u32[]{:S(2)}, u32[]{:S(2)}) %collective-permute-start.1) | collective-permute-done | bytes 1048608 | tf_op jit(solution)/shard_map/ppermute | solution.py:1049
  386.9 5.6 norm_back.2
  393.1 10.8 %outer_terms.7.refs_0_ = bf16[2048,1536]{1,0:T(8,128)(2,1)} custom-call(bf16[1024,2048]{1,0:T(8,128)(2,1)} %bitcast.39, bf16[1024,1536]{1,0:T(8,128)(2,1)} %get-tuple-element.398.a_ref.y_ref), custom_call_target="tpu_custom_call" | custom-call | flops 1 | bytes 1 | tf_op jit(solution)/shard_map/outer_terms/pallas_call | solution.py:213
  403.9 13.2 %collective-permute-done.2 = bf16[1,256,2048]{2,1,0:T(8,128)(2,1)S(1)} collective-permute-done((bf16[1,256,2048]{2,1,0:T(8,128)(2,1)}, bf16[1,256,2048]{2,1,0:T(8,128)(2,1)S(1)}, u32[]{:S(2)}, u32[]{:S(2)}) %collective-permute-start.2) | collective-permute-done | bytes 1048608 | tf_op jit(solution)/shard_map/ppermute | solution.py:1049
  427.9 19.8 %attention_back.1 = (bf16[4,256,768]{2,1,0:T(8,128)(2,1)}, bf16[4,256,768]{2,1,0:T(8,128)(2,1)}, f32[1,128]{1,0:T(1,128)}, f32[1,128]{1,0:T(1,128)}) custom-call(s32[2]{0:T(128)} %pad_add_fusion.place_ref, f32[4,256,768]{2,1,0:T(8,128)} %get-tuple-element.416.q_raw.k_raw, f32[4,256,768]{2,1,0:T(8,128)} %get-tuple-element.416.q_raw.k_raw, ...), custom_call_target="tpu_custom_call" | custom-call | flops 1 | bytes 1 | tf_op jit(solution)/shard_map/attention_back/pallas_call | solution.py:136
  447.7 4.5 halve.4
  452.4 10.8 %back_matmul.3 = (bf16[2,256,2048]{2,1,0:T(8,128)(2,1)}, bf16[2,256,2048]{2,1,0:T(8,128)(2,1)}) custom-call(bf16[1024,768]{1,0:T(8,128)(2,1)} %bitcast.48, bf16[1024,768]{1,0:T(8,128)(2,1)} %bitcast.46, bf16[2048,768]{1,0:T(8,128)(2,1)} %get-tuple-element.450.first_ref, bf16[2048,768]{1,0:T(8,128)(2,1)} %get-tuple-element.451.second_ref), custom_call_target="tpu_custom_call" | custom-call | flops 1 | bytes 1 | tf_op jit(solution)/shard_map/back_matmul/pallas_call | solution.py:192
  465.1 6.8 out_terms.1.blocks_ref
  471.9 7.3 outer_terms.8.refs_1_
  479.2 9.9 %collective-permute-done.5 = bf16[1,256,2048]{2,1,0:T(8,128)(2,1)S(1)} collective-permute-done((bf16[1,256,2048]{2,1,0:T(8,128)(2,1)}, bf16[1,256,2048]{2,1,0:T(8,128)(2,1)S(1)}, u32[]{:S(2)}, u32[]{:S(2)}) %collective-permute-start.5) | collective-permute-done | bytes 1048608 | tf_op jit(solution)/shard_map/ppermute | solution.py:1049
  490.4 5.0 halve.5
  496.8 7.4 outer_terms.9.refs_2_
  504.2 188.0 %reduce_all.1 = (bf16[4,256,1536]{2,1,0:T(8,128)(2,1)}, bf16[4,256,768]{2,1,0:T(8,128)(2,1)}, bf16[4,256,768]{2,1,0:T(8,128)(2,1)}, bf16[4,256,512]{2,1,0:T(8,128)(2,1)}) custom-call(bf16[4,512,512]{2,1,0:T(8,128)(2,1)} %out_terms.1.blocks_ref, bf16[2048,1536]{1,0:T(8,128)(2,1)} %outer_terms.7.refs_0_, bf16[2048,768]{1,0:T(8,128)(2,1)} %outer_terms.8.refs_1_, ...), custom_call_target="tpu_custom_call" | custom-call | flops 1 | bytes 1 | tf_op jit(solution)/shard_map/reduce_all/pallas_call | solution.py:993
  693.3 5.5 norm_back.3
  700.0 5.1 put_columns.2
  708.8 5.3 put_rows.1
  726.6 9.5 %put_strips.1 = f32[256,12288]{1,0:T(8,128)} custom-call(s32[2]{0:T(128)} %pad_add_fusion.place_ref, bf16[4,256,1536]{2,1,0:T(8,128)(2,1)} %get-tuple-element.540.refs_0_, bf16[1,256,1536]{2,1,0:T(8,128)(2,1)} %bitcast.57, bf16[1,256,1536]{2,1,0:T(8,128)(2,1)} %copy-done.6, bf16[2,256,1536]{2,1,0:T(8,128)(2,1)} %collective-permute-done.15.refs_3_), custom_call_target="tpu_custom_call" | custom-call | flops 1 | bytes 1 | tf_op jit(solution)/shard_map/put_strips/pallas_call | solution.py:298
  (107 shorter events, 63.6 us)
Async XLA Ops:
  7.2 420.0 %reduce-scatter.3.cloned.1.call-start = ((), (), s32[]{:S(2)}) async-start(), calls=%async_computation.2 | async-start | bytes 7077888 | tf_op jit(solution)/shard_map/reduce_scatter | solution.py:1306
  304.7 387.5 %reduce-scatter.5.cloned.1.call-start = ((), (), s32[]{:S(2)}) async-start(), calls=%async_computation.3 | async-start | bytes 7077888 | tf_op jit(solution)/shard_map/reduce_scatter | solution.py:1318
  339.6 4.4 collective-permute-start
  360.4 25.5 %collective-permute-start.1 = (bf16[1,256,2048]{2,1,0:T(8,128)(2,1)}, bf16[1,256,2048]{2,1,0:T(8,128)(2,1)S(1)}, u32[]{:S(2)}, u32[]{:S(2)}) collective-permute-start(bf16[1,256,2048]{2,1,0:T(8,128)(2,1)} %get-tuple-element.376), channel_id=1, source_target_pairs={{0,2},{1,3},{2,0},{3,1},{4,6},{5,7},{6,4},{7,5},{8,10},{9,11},{10,... | collective-permute-start | bytes 3145736 | tf_op jit(solution)/shard_map/ppermute | solution.py:1049
  392.4 24.7 %copy-start.4 = (bf16[256,2048]{1,0:T(8,128)(2,1)S(1)}, bf16[256,2048]{1,0:T(8,128)(2,1)}, u32[]{:S(2)}) copy-start(bf16[256,2048]{1,0:T(8,128)(2,1)} %get-tuple-element.393) | copy-start | bytes 3145732
  392.4 24.7 %collective-permute-start.2 = (bf16[1,256,2048]{2,1,0:T(8,128)(2,1)}, bf16[1,256,2048]{2,1,0:T(8,128)(2,1)S(1)}, u32[]{:S(2)}, u32[]{:S(2)}) collective-permute-start(bf16[1,256,2048]{2,1,0:T(8,128)(2,1)} %bitcast.53), channel_id=1, source_target_pairs={{0,2},{1,3},{2,0},{3,1},{4,6},{5,7},{6,4},{7,5},{8,10},{9,11},{10,... | collective-permute-start | bytes 3145736 | tf_op jit(solution)/shard_map/ppermute | solution.py:1049
  417.3 4.2 collective-permute-start.3
  427.2 20.6 %collective-permute-start.4 = (bf16[2,256,2048]{2,1,0:T(8,128)(2,1)}, bf16[2,256,2048]{2,1,0:T(8,128)(2,1)}, u32[]{:S(2)}, u32[]{:S(2)}) collective-permute-start(bf16[2,256,2048]{2,1,0:T(8,128)(2,1)} %get-tuple-element.412), channel_id=1, source_target_pairs={{0,1},{1,0},{2,3},{3,2},{4,5},{5,4},{6,7},{7,6},{8,9},{9,8},{10,11... | collective-permute-start | bytes 6291464 | tf_op jit(solution)/shard_map/ppermute | solution.py:1049
  427.2 25.0 %collective-permute-start.6 = (bf16[1,192,2048]{2,1,0:T(8,128)(2,1)}, bf16[1,192,2048]{2,1,0:T(8,128)(2,1)S(1)}, u32[]{:S(2)}, u32[]{:S(2)}) collective-permute-start(bf16[1,192,2048]{2,1,0:T(8,128)(2,1)} %bitcast.59), channel_id=1, source_target_pairs={{0,2},{1,3},{2,0},{3,1},{4,6},{5,7},{6,4},{7,5},{8,10},{9,11},{10,... | collective-permute-start | bytes 2359304 | tf_op jit(solution)/shard_map/ppermute | solution.py:1049
  463.2 25.9 %collective-permute-start.7 = (bf16[2,256,2048]{2,1,0:T(8,128)(2,1)}, bf16[2,256,2048]{2,1,0:T(8,128)(2,1)S(1)}, u32[]{:S(2)}, u32[]{:S(2)}) collective-permute-start(bf16[2,256,2048]{2,1,0:T(8,128)(2,1)} %get-tuple-element.456), channel_id=1, source_target_pairs={{0,1},{1,0},{2,3},{3,2},{4,5},{5,4},{6,7},{7,6},{8,9},{9,8},{10,11... | collective-permute-start | bytes 6291464 | tf_op jit(solution)/shard_map/ppermute | solution.py:1049
  463.2 25.9 %collective-permute-start.8 = (bf16[2,192,2048]{2,1,0:T(8,128)(2,1)S(1)}, bf16[2,192,2048]{2,1,0:T(8,128)(2,1)S(1)}, u32[]{:S(2)}, u32[]{:S(2)}) collective-permute-start(bf16[2,192,2048]{2,1,0:T(8,128)(2,1)S(1)} %pad_maximum_fusion.2), channel_id=1, source_target_pairs={{0,1},{1,0},{2,3},{3,2},{4,5},{5,4},{6,7},{7,6},{8,9},{9,8},{10,11... | collective-permute-start | bytes 4718600 | tf_op jit(solution)/shard_map/ppermute | solution.py:1049
  463.7 25.4 %collective-permute-start.5 = (bf16[1,256,2048]{2,1,0:T(8,128)(2,1)}, bf16[1,256,2048]{2,1,0:T(8,128)(2,1)S(1)}, u32[]{:S(2)}, u32[]{:S(2)}) collective-permute-start(bf16[1,256,2048]{2,1,0:T(8,128)(2,1)} %get-tuple-element.443), channel_id=1, source_target_pairs={{0,2},{1,3},{2,0},{3,1},{4,6},{5,7},{6,4},{7,5},{8,10},{9,11},{10,... | collective-permute-start | bytes 3145736 | tf_op jit(solution)/shard_map/ppermute | solution.py:1049
  489.1 15.1 %copy-start.14 = (bf16[1,256,2048]{2,1,0:T(8,128)(2,1)}, bf16[1,256,2048]{2,1,0:T(8,128)(2,1)S(1)}, u32[]{:S(2)}) copy-start(bf16[1,256,2048]{2,1,0:T(8,128)(2,1)S(1)} %collective-permute-done.5) | copy-start | bytes 3145732
  495.4 197.0 %collective-permute-start.9 = (bf16[1,256,2048]{2,1,0:T(8,128)(2,1)}, bf16[1,256,2048]{2,1,0:T(8,128)(2,1)S(1)}, u32[]{:S(2)}, u32[]{:S(2)}) collective-permute-start(bf16[1,256,2048]{2,1,0:T(8,128)(2,1)} %get-tuple-element.473), channel_id=1, source_target_pairs={{0,2},{1,3},{2,0},{3,1},{4,6},{5,7},{6,4},{7,5},{8,10},{9,11},{10,... | collective-permute-start | bytes 3145736 | tf_op jit(solution)/shard_map/ppermute | solution.py:1049
  692.2 21.9 %collective-permute-start.12 = (bf16[1,256,1536]{2,1,0:T(8,128)(2,1)}, bf16[1,256,1536]{2,1,0:T(8,128)(2,1)S(1)}, u32[]{:S(2)}, u32[]{:S(2)}) collective-permute-start(bf16[1,256,1536]{2,1,0:T(8,128)(2,1)} %bitcast.56), channel_id=1, source_target_pairs={{0,2},{1,3},{2,0},{3,1},{4,6},{5,7},{6,4},{7,5},{8,10},{9,11},{10,... | collective-permute-start | bytes 2359304 | tf_op jit(solution)/shard_map/ppermute | solution.py:1049
  699.6 9.2 %collective-permute-start.10 = (f32[4352]{0:T(1024)S(1)}, f32[4352]{0:T(1024)S(1)}, u32[]{:S(2)}, u32[]{:S(2)}) collective-permute-start(f32[4352]{0:T(1024)S(1)} %maximum_reduce_fusion), channel_id=1, source_target_pairs={{0,1},{1,0},{2,3},{3,2},{4,5},{5,4},{6,7},{7,6},{8,9},{9,8},{10,11... | collective-permute-start | bytes 52232 | tf_op jit(solution)/shard_map/ppermute | solution.py:1049
  714.1 12.5 %copy-start.6 = (bf16[1,256,1536]{2,1,0:T(8,128)(2,1)}, bf16[1,256,1536]{2,1,0:T(8,128)(2,1)S(1)}, u32[]{:S(2)}) copy-start(bf16[1,256,1536]{2,1,0:T(8,128)(2,1)S(1)} %collective-permute-done.12.refs_2_) | copy-start | bytes 2359300
  714.3 12.3 %collective-permute-start.15 = (bf16[2,256,1536]{2,1,0:T(8,128)(2,1)S(1)}, bf16[2,256,1536]{2,1,0:T(8,128)(2,1)}, u32[]{:S(2)}, u32[]{:S(2)}) collective-permute-start(bf16[2,256,1536]{2,1,0:T(8,128)(2,1)S(1)} %pad_maximum_fusion.3), channel_id=1, source_target_pairs={{0,1},{1,0},{2,3},{3,2},{4,5},{5,4},{6,7},{7,6},{8,9},{9,8},{10,11... | collective-permute-start | bytes 4718600 | tf_op jit(solution)/shard_map/ppermute | solution.py:1049
  714.5 3.8 collective-permute-start.11
  718.3 5.9 collective-permute-start.13
  724.2 12.6 %copy-start.3 = (f32[256,2048]{1,0:T(8,128)S(1)}, f32[256,2048]{1,0:T(8,128)}, u32[]{:S(2)}) copy-start(f32[256,2048]{1,0:T(8,128)} %get-tuple-element.550.source_ref) | copy-start | bytes 6291460
  724.2 12.6 %copy-start.10 = (f32[1,256,2048]{2,1,0:T(8,128)S(1)}, f32[1,256,2048]{2,1,0:T(8,128)}, u32[]{:S(2)}) copy-start(f32[1,256,2048]{2,1,0:T(8,128)} %get-tuple-element.441) | copy-start | bytes 6291460
  724.2 11.9 %collective-permute-start.14 = (f32[4352]{0:T(1024)S(1)}, f32[4352]{0:T(1024)S(1)}, u32[]{:S(2)}, u32[]{:S(2)}) collective-permute-start(f32[4352]{0:T(1024)S(1)} %add.73), channel_id=1, source_target_pairs={{0,8},{4,12},{8,0},{12,4},{16,24},{20,28},{24,16},{28,20},{1,9},{5... | collective-permute-start | bytes 52232 | tf_op jit(solution)/shard_map/ppermute | solution.py:1049
  736.1 4.8 collective-permute-start.16
  (17 other events, 76.1 us)
Sparse Core Ops, SparseCore 0:
  304.8 117.6 reduce-scatter.2
  426.6 139.5 reduce-scatter.4

commit v6 on v5

--- a/solution.py
+++ b/solution.py
@@ -1340,7 +1340,8 @@
     t_one = task(cube.reduce(one_keep, one_send))
     out_parts = seq.run(7.0, lambda p, a, b: out_terms(p, a, b, n_u), place, gated, branch_grad, take=False)
     qk_terms = seq.run(9.3, lambda a, b: outer_terms(a, b, n_dp), normed, grad_qk, take=False)
-    vg_terms = seq.run(9.3, lambda a, b: outer_terms(a, b, n_dp), normed, grad_vg)
+    t_one.poll(seq.now + 100.0)
+    vg_terms = seq.run(9.3, lambda a, b: outer_terms(a, b, n_dp), normed, grad_vg, take=False)
 
     gate_all, qk_all, vg_all, out_all = seq.run(
         150.0, lambda b, *t: reduce_all(b, t, n_dp, n_u), out_parts, gate_terms, qk_terms, vg_terms, take=False

time: 759 us -> 758 us (level)
  no operation moved by 1% of the time
where the time goes in v6:
time: 758 us; the launch traced here: 748 us
  Pallas kernels  634 us (84%)
  waiting for transfers between devices  48.3 us (6%)
  starting transfers between devices  16 us (2%)
  between operations  15.6 us (2%)
  local copies, waits for them, and re-layouts  13.5 us (2%)
  matrix products  12.5 us (2%)
  other arithmetic  8.44 us (1%)
    pallas_call x1, Pallas kernels, forward(): pl.pallas_call(functools.partial(forward_kernel, n_dp, n_u, heads, kv_hea...  274 us
    pallas_call x1, Pallas kernels, reduce_all(): pl.pallas_call(functools.partial(reduce_kernel, n_dp, n_u, count), in_spe...  188 us
    ppermute x17, waiting for transfers between devices, fly(): got = lax.ppermute(value, axis, pairs)  48.2 us
    pallas_call x5, Pallas kernels, outer_terms(): pl.pallas_call(kernel, grid=(count,), in_specs=[pl.BlockSpec((m, depth),...  47.2 us
    pallas_call x2, Pallas kernels, back_matmul(): pl.pallas_call(kernel, grid=(width // part,), in_specs=[steady((m, n)), s...  29.4 us
    pallas_call x4, Pallas kernels, put_call(): pl.pallas_call(body, grid=(grid,), in_specs=[pl.BlockSpec(memory_space=pl...  23.5 us
    pallas_call x1, Pallas kernels, attend_back(): pl.pallas_call(functools.partial(attend_back_kernel, min(256, bucket), co...  19.8 us
    pallas_call x1, Pallas kernels, down_back(): pl.pallas_call(kernel, grid=(n // tile,), in_specs=[steady((m, width)), s...  16.1 us
  transfers between devices with their start and end apart: 19, of which 8 were waited for; matrix products, arithmetic and copies ran while one was open for 3% of the time, Pallas kernels for 46%

profile of v6, /device:TPU:0, one launch (start us, length us, event | category | flops | bytes accessed | tf_op | source)
XLA Modules:
  0.0 748.4 jit_solution(2213056032629107387)
XLA Ops:
  8.7 4.8 take_strips.1
  20.0 273.7 %forward.1 = (bf16[2048,768]{1,0:T(8,128)(2,1)}, bf16[2048,768]{1,0:T(8,128)(2,1)}, bf16[2048,1536]{1,0:T(8,128)(2,1)}, bf16[2048,1536]{1,0:T(8,128)(2,1)}, bf16...) custom-call(s32[1]{0:T(128)} %copy.23.length_ref, ...), custom_call_target="tpu_custom_call" | custom-call | flops 1 | bytes 1 | tf_op jit(solution)/shard_map/forward/pallas_call | solution.py:859
  293.7 11.0 %outer_terms.5 = bf16[1536,2048]{1,0:T(8,128)(2,1)} custom-call(bf16[1024,1536]{1,0:T(8,128)(2,1)} %bitcast.62, bf16[1024,2048]{1,0:T(8,128)(2,1)} %bitcast.42), custom_call_target="tpu_custom_call" | custom-call | flops 1 | bytes 1 | tf_op jit(solution)/shard_map/outer_terms/pallas_call | solution.py:213
  304.9 16.1 %down_back.1 = (bf16[1024,1536]{1,0:T(8,128)(2,1)}, bf16[1024,1536]{1,0:T(8,128)(2,1)}) custom-call(bf16[1024,2048]{1,0:T(8,128)(2,1)} %bitcast.43, f32[1024,1536]{1,0:T(8,128)} %bitcast.44, f32[1024,1536]{1,0:T(8,128)} %bitcast.45, bf16[1536,2048]{1,0:T(8,128)(2,1)} %get-tuple-element.381.weight_ref), custom_call_target="tpu_custom_call" | custom-call | flops 1 | bytes 1 | tf_op jit(solution)/shard_map/down_back/pallas_call | solution.py:242
  321.0 18.6 %back_matmul.2 = (bf16[2,256,2048]{2,1,0:T(8,128)(2,1)}, bf16[2,256,2048]{2,1,0:T(8,128)(2,1)}) custom-call(bf16[1024,1536]{1,0:T(8,128)(2,1)} %get-tuple-element.398.a_ref.y_ref, bf16[1024,1536]{1,0:T(8,128)(2,1)} %get-tuple-element.378.b_ref.y_ref, bf16[2048,1536]{1,0:T(8,128)(2,1)} %get-tuple-element.362.first_ref, ...), custom_call_target="tpu_custom_call" | custom-call | flops 1 | bytes 1 | tf_op jit(solution)/shard_map/back_matmul/pallas_call | solution.py:192
  349.7 10.7 %outer_terms.6 = bf16[2048,1536]{1,0:T(8,128)(2,1)} custom-call(bf16[1024,2048]{1,0:T(8,128)(2,1)} %bitcast.38, bf16[1024,1536]{1,0:T(8,128)(2,1)} %get-tuple-element.378.b_ref.y_ref), custom_call_target="tpu_custom_call" | custom-call | flops 1 | bytes 1 | tf_op jit(solution)/shard_map/outer_terms/pallas_call | solution.py:213
  362.3 8.8 %convolution_convert_fusion = bf16[1024,2048]{1,0:T(8,128)(2,1)S(1)} fusion(bf16[1024,1536]{1,0:T(8,128)(2,1)S(1)} %bitcast.63, bf16[1536,2048]{1,0:T(8,128)(2,1)} %get-tuple-element.381.weight_ref), kind=kOutput, calls=%fused_computation.1 | convolution fusion | flops 6444548096 | bytes 13631488 | tf_op jit(solution)/shard_map/mk,kn->mn/dot_general | solution.py:1196
  373.6 12.3 %collective-permute-done.1 = bf16[1,256,2048]{2,1,0:T(8,128)(2,1)S(1)} collective-permute-done((bf16[1,256,2048]{2,1,0:T(8,128)(2,1)}, bf16[1,256,2048]{2,1,0:T(8,128)(2,1)S(1)}, u32[]{:S(2)}, u32[]{:S(2)}) %collective-permute-start.1) | collective-permute-done | bytes 1048608 | tf_op jit(solution)/shard_map/ppermute | solution.py:1049
  386.9 5.6 norm_back.2
  393.1 10.8 %outer_terms.7.refs_0_ = bf16[2048,1536]{1,0:T(8,128)(2,1)} custom-call(bf16[1024,2048]{1,0:T(8,128)(2,1)} %bitcast.39, bf16[1024,1536]{1,0:T(8,128)(2,1)} %get-tuple-element.398.a_ref.y_ref), custom_call_target="tpu_custom_call" | custom-call | flops 1 | bytes 1 | tf_op jit(solution)/shard_map/outer_terms/pallas_call | solution.py:213
  403.9 13.2 %collective-permute-done.2 = bf16[1,256,2048]{2,1,0:T(8,128)(2,1)S(1)} collective-permute-done((bf16[1,256,2048]{2,1,0:T(8,128)(2,1)}, bf16[1,256,2048]{2,1,0:T(8,128)(2,1)S(1)}, u32[]{:S(2)}, u32[]{:S(2)}) %collective-permute-start.2) | collective-permute-done | bytes 1048608 | tf_op jit(solution)/shard_map/ppermute | solution.py:1049
  427.9 19.8 %attention_back.1 = (bf16[4,256,768]{2,1,0:T(8,128)(2,1)}, bf16[4,256,768]{2,1,0:T(8,128)(2,1)}, f32[1,128]{1,0:T(1,128)}, f32[1,128]{1,0:T(1,128)}) custom-call(s32[2]{0:T(128)} %pad_add_fusion.place_ref, f32[4,256,768]{2,1,0:T(8,128)} %get-tuple-element.416.q_raw.k_raw, f32[4,256,768]{2,1,0:T(8,128)} %get-tuple-element.416.q_raw.k_raw, ...), custom_call_target="tpu_custom_call" | custom-call | flops 1 | bytes 1 | tf_op jit(solution)/shard_map/attention_back/pallas_call | solution.py:136
  447.7 4.5 halve.4
  452.4 10.8 %back_matmul.3 = (bf16[2,256,2048]{2,1,0:T(8,128)(2,1)}, bf16[2,256,2048]{2,1,0:T(8,128)(2,1)}) custom-call(bf16[1024,768]{1,0:T(8,128)(2,1)} %bitcast.48, bf16[1024,768]{1,0:T(8,128)(2,1)} %bitcast.46, bf16[2048,768]{1,0:T(8,128)(2,1)} %get-tuple-element.450.first_ref, bf16[2048,768]{1,0:T(8,128)(2,1)} %get-tuple-element.451.second_ref), custom_call_target="tpu_custom_call" | custom-call | flops 1 | bytes 1 | tf_op jit(solution)/shard_map/back_matmul/pallas_call | solution.py:192
  465.1 6.8 out_terms.1.blocks_ref
  471.9 7.3 outer_terms.8.refs_1_
  479.2 9.9 %collective-permute-done.5 = bf16[1,256,2048]{2,1,0:T(8,128)(2,1)S(1)} collective-permute-done((bf16[1,256,2048]{2,1,0:T(8,128)(2,1)}, bf16[1,256,2048]{2,1,0:T(8,128)(2,1)S(1)}, u32[]{:S(2)}, u32[]{:S(2)}) %collective-permute-start.5) | collective-permute-done | bytes 1048608 | tf_op jit(solution)/shard_map/ppermute | solution.py:1049
  489.1 5.2 halve.5
  495.8 7.4 outer_terms.9.refs_2_
  503.2 187.9 %reduce_all.1 = (bf16[4,256,1536]{2,1,0:T(8,128)(2,1)}, bf16[4,256,768]{2,1,0:T(8,128)(2,1)}, bf16[4,256,768]{2,1,0:T(8,128)(2,1)}, bf16[4,256,512]{2,1,0:T(8,128)(2,1)}) custom-call(bf16[4,512,512]{2,1,0:T(8,128)(2,1)} %out_terms.1.blocks_ref, bf16[2048,1536]{1,0:T(8,128)(2,1)} %outer_terms.7.refs_0_, bf16[2048,768]{1,0:T(8,128)(2,1)} %outer_terms.8.refs_1_, ...), custom_call_target="tpu_custom_call" | custom-call | flops 1 | bytes 1 | tf_op jit(solution)/shard_map/reduce_all/pallas_call | solution.py:993
  692.2 5.5 norm_back.3
  698.9 5.1 put_columns.2
  707.7 5.3 put_rows.1
  725.6 9.5 %put_strips.1 = f32[256,12288]{1,0:T(8,128)} custom-call(s32[2]{0:T(128)} %pad_add_fusion.place_ref, bf16[4,256,1536]{2,1,0:T(8,128)(2,1)} %get-tuple-element.540.refs_0_, bf16[1,256,1536]{2,1,0:T(8,128)(2,1)} %bitcast.57, bf16[1,256,1536]{2,1,0:T(8,128)(2,1)} %copy-done.6, bf16[2,256,1536]{2,1,0:T(8,128)(2,1)} %collective-permute-done.15.refs_3_), custom_call_target="tpu_custom_call" | custom-call | flops 1 | bytes 1 | tf_op jit(solution)/shard_map/put_strips/pallas_call | solution.py:298
  (107 shorter events, 62.5 us)
Async XLA Ops:
  7.2 420.0 %reduce-scatter.3.cloned.1.call-start = ((), (), s32[]{:S(2)}) async-start(), calls=%async_computation.2 | async-start | bytes 7077888 | tf_op jit(solution)/shard_map/reduce_scatter | solution.py:1306
  304.7 386.4 %reduce-scatter.5.cloned.1.call-start = ((), (), s32[]{:S(2)}) async-start(), calls=%async_computation.3 | async-start | bytes 7077888 | tf_op jit(solution)/shard_map/reduce_scatter | solution.py:1318
  339.6 4.4 collective-permute-start
  360.4 25.5 %collective-permute-start.1 = (bf16[1,256,2048]{2,1,0:T(8,128)(2,1)}, bf16[1,256,2048]{2,1,0:T(8,128)(2,1)S(1)}, u32[]{:S(2)}, u32[]{:S(2)}) collective-permute-start(bf16[1,256,2048]{2,1,0:T(8,128)(2,1)} %get-tuple-element.376), channel_id=1, source_target_pairs={{0,2},{1,3},{2,0},{3,1},{4,6},{5,7},{6,4},{7,5},{8,10},{9,11},{10,... | collective-permute-start | bytes 3145736 | tf_op jit(solution)/shard_map/ppermute | solution.py:1049
  392.4 24.7 %copy-start.4 = (bf16[256,2048]{1,0:T(8,128)(2,1)S(1)}, bf16[256,2048]{1,0:T(8,128)(2,1)}, u32[]{:S(2)}) copy-start(bf16[256,2048]{1,0:T(8,128)(2,1)} %get-tuple-element.393) | copy-start | bytes 3145732
  392.4 24.7 %collective-permute-start.2 = (bf16[1,256,2048]{2,1,0:T(8,128)(2,1)}, bf16[1,256,2048]{2,1,0:T(8,128)(2,1)S(1)}, u32[]{:S(2)}, u32[]{:S(2)}) collective-permute-start(bf16[1,256,2048]{2,1,0:T(8,128)(2,1)} %bitcast.53), channel_id=1, source_target_pairs={{0,2},{1,3},{2,0},{3,1},{4,6},{5,7},{6,4},{7,5},{8,10},{9,11},{10,... | collective-permute-start | bytes 3145736 | tf_op jit(solution)/shard_map/ppermute | solution.py:1049
  417.3 4.2 collective-permute-start.3
  427.2 20.6 %collective-permute-start.4 = (bf16[2,256,2048]{2,1,0:T(8,128)(2,1)}, bf16[2,256,2048]{2,1,0:T(8,128)(2,1)}, u32[]{:S(2)}, u32[]{:S(2)}) collective-permute-start(bf16[2,256,2048]{2,1,0:T(8,128)(2,1)} %get-tuple-element.412), channel_id=1, source_target_pairs={{0,1},{1,0},{2,3},{3,2},{4,5},{5,4},{6,7},{7,6},{8,9},{9,8},{10,11... | collective-permute-start | bytes 6291464 | tf_op jit(solution)/shard_map/ppermute | solution.py:1049
  427.2 25.0 %collective-permute-start.6 = (bf16[1,192,2048]{2,1,0:T(8,128)(2,1)}, bf16[1,192,2048]{2,1,0:T(8,128)(2,1)S(1)}, u32[]{:S(2)}, u32[]{:S(2)}) collective-permute-start(bf16[1,192,2048]{2,1,0:T(8,128)(2,1)} %bitcast.59), channel_id=1, source_target_pairs={{0,2},{1,3},{2,0},{3,1},{4,6},{5,7},{6,4},{7,5},{8,10},{9,11},{10,... | collective-permute-start | bytes 2359304 | tf_op jit(solution)/shard_map/ppermute | solution.py:1049
  452.2 11.0 %copy-start.8 = (bf16[1,192,2048]{2,1,0:T(8,128)(2,1)}, bf16[1,192,2048]{2,1,0:T(8,128)(2,1)S(1)}, u32[]{:S(2)}) copy-start(bf16[1,192,2048]{2,1,0:T(8,128)(2,1)S(1)} %collective-permute-done.6.refs_1_) | copy-start | bytes 2359300
  463.2 16.0 %collective-permute-start.7 = (bf16[2,256,2048]{2,1,0:T(8,128)(2,1)}, bf16[2,256,2048]{2,1,0:T(8,128)(2,1)S(1)}, u32[]{:S(2)}, u32[]{:S(2)}) collective-permute-start(bf16[2,256,2048]{2,1,0:T(8,128)(2,1)} %get-tuple-element.456), channel_id=1, source_target_pairs={{0,1},{1,0},{2,3},{3,2},{4,5},{5,4},{6,7},{7,6},{8,9},{9,8},{10,11... | collective-permute-start | bytes 6291464 | tf_op jit(solution)/shard_map/ppermute | solution.py:1049
  463.2 25.9 %collective-permute-start.8 = (bf16[2,192,2048]{2,1,0:T(8,128)(2,1)S(1)}, bf16[2,192,2048]{2,1,0:T(8,128)(2,1)S(1)}, u32[]{:S(2)}, u32[]{:S(2)}) collective-permute-start(bf16[2,192,2048]{2,1,0:T(8,128)(2,1)S(1)} %pad_maximum_fusion.2), channel_id=1, source_target_pairs={{0,1},{1,0},{2,3},{3,2},{4,5},{5,4},{6,7},{7,6},{8,9},{9,8},{10,11... | collective-permute-start | bytes 4718600 | tf_op jit(solution)/shard_map/ppermute | solution.py:1049
  463.7 25.4 %collective-permute-start.5 = (bf16[1,256,2048]{2,1,0:T(8,128)(2,1)}, bf16[1,256,2048]{2,1,0:T(8,128)(2,1)S(1)}, u32[]{:S(2)}, u32[]{:S(2)}) collective-permute-start(bf16[1,256,2048]{2,1,0:T(8,128)(2,1)} %get-tuple-element.443), channel_id=1, source_target_pairs={{0,2},{1,3},{2,0},{3,1},{4,6},{5,7},{6,4},{7,5},{8,10},{9,11},{10,... | collective-permute-start | bytes 3145736 | tf_op jit(solution)/shard_map/ppermute | solution.py:1049
  494.3 196.9 %collective-permute-start.9 = (bf16[1,256,2048]{2,1,0:T(8,128)(2,1)}, bf16[1,256,2048]{2,1,0:T(8,128)(2,1)S(1)}, u32[]{:S(2)}, u32[]{:S(2)}) collective-permute-start(bf16[1,256,2048]{2,1,0:T(8,128)(2,1)} %get-tuple-element.473), channel_id=1, source_target_pairs={{0,2},{1,3},{2,0},{3,1},{4,6},{5,7},{6,4},{7,5},{8,10},{9,11},{10,... | collective-permute-start | bytes 3145736 | tf_op jit(solution)/shard_map/ppermute | solution.py:1049
  691.1 21.9 %collective-permute-start.12 = (bf16[1,256,1536]{2,1,0:T(8,128)(2,1)}, bf16[1,256,1536]{2,1,0:T(8,128)(2,1)S(1)}, u32[]{:S(2)}, u32[]{:S(2)}) collective-permute-start(bf16[1,256,1536]{2,1,0:T(8,128)(2,1)} %bitcast.56), channel_id=1, source_target_pairs={{0,2},{1,3},{2,0},{3,1},{4,6},{5,7},{6,4},{7,5},{8,10},{9,11},{10,... | collective-permute-start | bytes 2359304 | tf_op jit(solution)/shard_map/ppermute | solution.py:1049
  698.4 9.2 %collective-permute-start.10 = (f32[4352]{0:T(1024)S(1)}, f32[4352]{0:T(1024)S(1)}, u32[]{:S(2)}, u32[]{:S(2)}) collective-permute-start(f32[4352]{0:T(1024)S(1)} %maximum_reduce_fusion), channel_id=1, source_target_pairs={{0,1},{1,0},{2,3},{3,2},{4,5},{5,4},{6,7},{7,6},{8,9},{9,8},{10,11... | collective-permute-start | bytes 52232 | tf_op jit(solution)/shard_map/ppermute | solution.py:1049
  713.0 12.6 %copy-start.6 = (bf16[1,256,1536]{2,1,0:T(8,128)(2,1)}, bf16[1,256,1536]{2,1,0:T(8,128)(2,1)S(1)}, u32[]{:S(2)}) copy-start(bf16[1,256,1536]{2,1,0:T(8,128)(2,1)S(1)} %collective-permute-done.12.refs_2_) | copy-start | bytes 2359300
  713.2 12.5 %collective-permute-start.15 = (bf16[2,256,1536]{2,1,0:T(8,128)(2,1)S(1)}, bf16[2,256,1536]{2,1,0:T(8,128)(2,1)}, u32[]{:S(2)}, u32[]{:S(2)}) collective-permute-start(bf16[2,256,1536]{2,1,0:T(8,128)(2,1)S(1)} %pad_maximum_fusion.3), channel_id=1, source_target_pairs={{0,1},{1,0},{2,3},{3,2},{4,5},{5,4},{6,7},{7,6},{8,9},{9,8},{10,11... | collective-permute-start | bytes 4718600 | tf_op jit(solution)/shard_map/ppermute | solution.py:1049
  713.4 3.8 collective-permute-start.11
  717.2 6.1 collective-permute-start.13
  723.2 12.6 %copy-start.3 = (f32[256,2048]{1,0:T(8,128)S(1)}, f32[256,2048]{1,0:T(8,128)}, u32[]{:S(2)}) copy-start(f32[256,2048]{1,0:T(8,128)} %get-tuple-element.550.source_ref) | copy-start | bytes 6291460
  723.2 12.6 %copy-start.10 = (f32[1,256,2048]{2,1,0:T(8,128)S(1)}, f32[1,256,2048]{2,1,0:T(8,128)}, u32[]{:S(2)}) copy-start(f32[1,256,2048]{2,1,0:T(8,128)} %get-tuple-element.441) | copy-start | bytes 6291460
  723.2 11.9 %collective-permute-start.14 = (f32[4352]{0:T(1024)S(1)}, f32[4352]{0:T(1024)S(1)}, u32[]{:S(2)}, u32[]{:S(2)}) collective-permute-start(f32[4352]{0:T(1024)S(1)} %add.73), channel_id=1, source_target_pairs={{0,8},{4,12},{8,0},{12,4},{16,24},{20,28},{24,16},{28,20},{1,9},{5... | collective-permute-start | bytes 52232 | tf_op jit(solution)/shard_map/ppermute | solution.py:1049
  735.1 4.8 collective-permute-start.16
  (17 other events, 78.9 us)
Sparse Core Ops, SparseCore 0:
  304.8 117.6 reduce-scatter.2
  426.6 139.5 reduce-scatter.4
